TPU v7x, 128 devices: a whole 4x4x4 slice. The times are simulated.
128 devices in a mesh: dp: 2 (over core), seq: 16 (over z, y), tensor: 4 (over x).
Axes of the slice: x: 4, y: 4, z: 4, core: 2. Of those that a mesh axis runs over, the one named last changes fastest.
Arguments:
- tokens: bfloat16 [16384, 3072], P(('dp', 'seq'), 'tensor'), parts along dimension 0, may hold values from -6 to 6
- w_qkv: bfloat16 [3072, 3, 4096], P(None, None, 'tensor'), may hold values from -0.109375 to 0.109375
- log_decay: float32 [32, 16384], P('tensor', ('dp', 'seq')), parts along dimension 1, as said below
- w_out: bfloat16 [4096, 3072], P('tensor'), may hold values from -0.125 to 0.125
Outputs:
- mixed: bfloat16 [16384, 3072], P(('dp', 'seq'), 'tensor'), parts along dimension 0
There are 2 independent parts, one for each index of `dp`. A program takes and returns all parts, laid end to end along the dimension named above; an argument that names none is the same for every part. Nothing has to cross between parts.
Inputs may be any that keep to these rules, and one draw needn't show every extreme that they name: `log_decay`: every entry is at most 0.
All inputs are finite; a program needn't handle non-finite values.
Results may differ from a plain program's by a relative error of at most 0.017.
Values may be sent and summed in bfloat16 or wider, within the bound.
No kernel may reach another device: no remote copies, remote signals or barrier semaphores. Data moves between devices by JAX's collectives and lax.ppermute only.
A program may use at most 128 MiB of HBM per device.

v0:
```python
import jax
import jax.numpy as jnp
from jax import lax
from jax.sharding import PartitionSpec as P

exact_mode = lax.Precision.HIGHEST


def block_terms(parts):
    query_part, key_part, value_part, decay_part = parts
    block_rows = query_part.shape[1]
    causal = jnp.arange(block_rows)[:, None] >= jnp.arange(block_rows)[None, :]
    running = jnp.cumsum(decay_part, axis=1)
    spread = jnp.where(causal, running[:, :, None] - running[:, None, :], 0.0)
    weight = jnp.where(causal, jnp.exp(spread), 0.0)
    scores = jnp.einsum("htd,hsd->hts", query_part, key_part, preferred_element_type=jnp.float32)
    weighted = (scores * weight).astype(jnp.bfloat16)
    inner = jnp.einsum("hts,hsd->htd", weighted, value_part, preferred_element_type=jnp.float32)
    final_log = running[:, -1]
    query_scaled = (query_part * jnp.exp(running)[:, :, None]).astype(jnp.bfloat16)
    key_scaled = (key_part * jnp.exp(final_log[:, None] - running)[:, :, None]).astype(jnp.bfloat16)
    block_kv = jnp.einsum(
        "htd,hte->hde", key_scaled, value_part, preferred_element_type=jnp.float32
    )
    return (inner, query_scaled, block_kv, final_log)


def chain_step(carry, item):
    memory, before = carry
    block_kv, final_log = item
    updated = (jnp.exp(final_log)[:, None, None] * memory + block_kv, before + final_log)
    return (updated, (memory, before))


def body(tokens, w_qkv, log_decay, w_out):
    row_count = tokens.shape[0]
    head_count = log_decay.shape[0]
    head_dim = w_out.shape[0] // head_count
    weights = w_qkv.reshape(w_qkv.shape[0], -1)
    projected = jnp.dot(
        lax.all_gather(tokens, "tensor", axis=1, tiled=True),
        weights,
        preferred_element_type=jnp.float32,
    )
    activated = (
        jax.nn.silu(projected).astype(jnp.bfloat16).reshape(row_count, 3, head_count, head_dim)
    )
    queries = activated[:, 0].transpose(1, 0, 2)
    keys = activated[:, 1].transpose(1, 0, 2)
    value_rows = activated[:, 2].transpose(1, 0, 2)
    block_rows = min(512, row_count)
    number_of_tiles = row_count // block_rows

    def blocked(array):
        return array.reshape(head_count, number_of_tiles, block_rows, head_dim).transpose(
            1, 0, 2, 3
        )

    attenuation_tiles = log_decay.reshape(head_count, number_of_tiles, block_rows).transpose(
        1, 0, 2
    )
    inners, query_scaled, block_kvs, final_logs = lax.map(
        block_terms, (blocked(queries), blocked(keys), blocked(value_rows), attenuation_tiles)
    )
    start_state = (
        jnp.zeros((head_count, head_dim, head_dim), jnp.float32),
        jnp.zeros((head_count,), jnp.float32),
    )
    (shard_state, shard_log), (prefix_states, prefix_logs) = lax.scan(
        chain_step, start_state, (block_kvs, final_logs)
    )
    states, totals = (
        lax.all_gather(shard_state[None].astype(jnp.bfloat16), "seq", axis=0, tiled=True).astype(
            jnp.float32
        ),
        lax.all_gather(shard_log[None].astype(jnp.bfloat16), "seq", axis=0, tiled=True).astype(
            jnp.float32
        ),
    )
    position = lax.axis_index("seq")
    shards = jnp.arange(states.shape[0])
    earlier_mask = shards[:, None] < position
    before = jnp.sum(jnp.where(earlier_mask, totals, 0.0), axis=0)
    through = jnp.cumsum(totals, axis=0)
    weight = jnp.where(
        earlier_mask, jnp.exp(jnp.where(earlier_mask, before[None, :] - through, 0.0)), 0.0
    )
    incoming = jnp.einsum("nh,nhde->hde", weight, states, precision=exact_mode)
    states_used = (prefix_states + jnp.exp(prefix_logs)[:, :, None, None] * incoming[None]).astype(
        jnp.bfloat16
    )
    carried = jnp.einsum(
        "bhtd,bhde->bhte", query_scaled, states_used, preferred_element_type=jnp.float32
    )
    attended = (inners + carried).transpose(1, 0, 2, 3).reshape(head_count, row_count, head_dim)
    normed = attended / jnp.sqrt(jnp.mean(attended * attended, axis=2, keepdims=True) + 1e-06)
    attn = normed.astype(jnp.bfloat16).transpose(1, 0, 2).reshape(row_count, head_count * head_dim)
    partial_terms = jnp.dot(attn, w_out, preferred_element_type=jnp.float32)
    return lax.psum_scatter(
        partial_terms.astype(jnp.bfloat16), "tensor", scatter_dimension=1, tiled=True
    )


def solution(mesh):
    in_specs = (
        P(("dp", "seq"), "tensor"),
        P(None, None, "tensor"),
        P("tensor", ("dp", "seq")),
        P("tensor", None),
    )
    out_specs = P(("dp", "seq"), "tensor")
    return jax.shard_map(body, mesh=mesh, in_specs=in_specs, out_specs=out_specs, check_vma=False)
```

profile of v0, /device:TPU:0, one launch (start us, length us, event | category | flops | bytes accessed | tf_op | source)
XLA Modules:
  0.0 183.9 jit_solution(17640436226562593191)
XLA Ops:
  6.5 0.7 all-gather.5.cloned.1.call-update
  7.3 2.2 %reduce-window.6 = f32[8,4,128]{2,0,1:T(8,128)S(1)} reduce-window(f32[8,4,128]{2,0,1:T(8,128)} %bitcast.58, f32[]{:T(128)} %constant.42.clone.1), window={size=1x1x128 pad=0_0x0_0x127_0}, to_apply=%region_0.1 | reduce-window | flops 520192 | bytes 32772 | tf_op jit(solution)/shard_map/reduce-window
  9.5 0.2 slice_reduce_fusion
  9.7 24.6 %copy.24 = bf16[3072,3,1024]{0,2,1:T(8,128)(2,1)} copy(bf16[3072,3,1024]{2,0,1:T(8,128)(2,1)} %param.5) | data formatting | bytes 37748736 | tf_op args[1]
  34.4 0.2 slice_reduce_fusion.1
  34.7 16.3 %all-gather.5.cloned.1.call-done = bf16[512,3072]{1,0:T(8,128)(2,1)} async-done(((bf16[512,768]{1,0:T(8,128)(2,1)}), bf16[512,3072]{1,0:T(8,128)(2,1)}) %all-gather.5.cloned.1.call-update) | async-done | bytes 3145744 | tf_op jit(solution)/shard_map/all_gather | solution.py:41
  51.0 15.5 %fusion.4 = bf16[64,8,24,128]{3,1,2,0:T(8,128)(2,1)S(1)} fusion(bf16[512,3072]{1,0:T(8,128)(2,1)} %all-gather.5.cloned.1.call-done, bf16[3072,3072]{0,1:T(8,128)(2,1)} %bitcast.54), kind=kOutput, calls=%fused_computation.7 | convolution fusion | flops 9671540736 | bytes 25165824 | tf_op jit(solution)/shard_map/dot_general | solution.py:40
  66.5 0.9 copy.43
  67.4 1.5 fusion.15
  68.9 0.7 copy.41
  69.6 3.7 %fusion.6 = bf16[8,128,128]{2,1,0:T(8,128)(2,1)} fusion(bf16[512,1,8,128]{0,3,2,1:T(8,128)(2,1)S(1)} %copy.41, f32[8,512]{1,0:T(8,128)S(1)} %subtract_exponential_fusion, bf16[512,1,8,128]{3,2,1,0:T(8,128)(2,1)} %get-tuple-element.39, f32[8]{0:T(128)S(1)} %exponential_multiply_fusion), kind=kOutput, calls=%fused_computation.15 | convolution fusion | flops 136052736 | bytes 2375712 | tf_op jit(solution)/shard_map/while/body/eval_jaxpr/htd,hte->hde/dot_general | solution.py:22
  73.4 0.6 dynamic-slice.8
  74.5 0.2 fusion.12
  74.7 0.2 dynamic-update-slice
  75.0 41.0 %all-reduce = bf16[128]{0:T(256)(128)(2,1)S(1)} all-reduce(bf16[128]{0:T(256)(128)(2,1)S(1)} %dynamic-update-slice), channel_id=2, replica_groups=mesh['dp'=2,'seq'=16,'tensor'=4] {'seq'}, use_global_device_ids=true, to_apply=%add | all-reduce | flops 128 | bytes 512
  116.1 0.1 select_reduce_fusion
  116.3 5.4 %fusion = f32[8,512,128]{1,2,0:T(8,128)S(1)} fusion(f32[8,512]{1,0:T(8,128)S(1)} %get-tuple-element.38, pred[512,512]{1,0:T(8,128)(4,1)S(1)} %iota_compare_fusion, bf16[512,1,8,128]{0,3,2,1:T(8,128)(2,1)} %copy-done, bf16[512,1,8,128]{3,2,1,0:T(8,128)(2,1)S(1)} %get-tuple-element.40, bf16[512,1,8,128]{3,2,1,0:T(8,128)(2,1)} %get-tuple-element.39), kind=kOutput, calls=%fused_computation.4 | convolution fusion | flops 1084227584 | bytes 5521408 | tf_op jit(solution)/shard_map/while/body/eval_jaxpr/hts,hsd->htd/dot_general | solution.py:18
  121.7 3.8 %all-gather.7.cloned.1.call-done = bf16[128,128,128]{2,1,0:T(8,128)(2,1)} async-done(((bf16[8,128,128]{2,1,0:T(8,128)(2,1)}), bf16[128,128,128]{2,1,0:T(8,128)(2,1)}) %all-gather.7.cloned.1.call-update) | async-done | bytes 4194320 | tf_op jit(solution)/shard_map/all_gather | solution.py:73
  125.6 3.1 %multiply_reduce_fusion = bf16[8,128,128]{2,1,0:T(8,128)(2,1)S(1)} fusion(bf16[8,16,128,128]{3,2,0,1:T(8,128)(2,1)} %bitcast.56, f32[8,16]{0,1:T(8,128)S(1)} %select_bitcast_fusion), kind=kLoop, calls=%fused_computation | loop fusion | flops 6160384 | bytes 4456960
  128.6 0.9 copy.38
  129.5 2.1 %multiply_reduce_fusion.1 = (f32[8,512]{1,0:T(8,128)S(1)}, f32[8,512,128]{1,2,0:T(8,128)S(1)}) fusion(f32[8,512,128]{1,2,0:T(8,128)S(1)} %fusion, bf16[8,128,128]{1,2,0:T(8,128)(2,1)} %copy.38, f32[8,512]{1,0:T(8,128)S(1)} %get-tuple-element.37, bf16[512,1,8,128]{3,2,1,0:T(8,128)(2,1)S(1)} %get-tuple-element.40), kind=kOutput, calls=%fused_computation.10 | convolution fusion | flops 137359360 | bytes 5537792 | tf_op jit(solution)/shard_map/bhtd,bhde->bhte/dot_general | solution.py:92
  131.6 0.3 fusion.5
  131.9 7.6 %convolution_convert_fusion = bf16[512,3072]{1,0:T(8,128)(2,1)} fusion(bf16[512,1024]{0,1:T(8,128)(2,1)S(1)} %bitcast.57, bf16[1024,3072]{1,0:T(8,128)(2,1)} %param.7), kind=kOutput, calls=%fused_computation.3 | convolution fusion | flops 3222798336 | bytes 10485760 | tf_op jit(solution)/shard_map/dot_general | solution.py:98
  139.6 37.8 %reduce-scatter.2.cloned.1.call-done = bf16[512,768]{1,0:T(8,128)(2,1)} async-done(((bf16[512,3072]{1,0:T(8,128)(2,1)}), bf16[512,768]{1,0:T(8,128)(2,1)}) %reduce-scatter.2.cloned.1.call-update) | async-done | bytes 786448 | tf_op jit(solution)/shard_map/reduce_scatter | solution.py:99
  (21 shorter events, 0.6 us)
Async XLA Ops:
  6.5 44.5 %all-gather.5.cloned.1.call-start = ((), (), s32[]{:S(2)}) async-start(), calls=%async_computation.1 | async-start | bytes 3932160 | tf_op jit(solution)/shard_map/all_gather | solution.py:41
  7.3 118.3 %all-gather.7.cloned.1.call-start = ((), (), s32[]{:S(2)}) async-start(), calls=%async_computation.3 | async-start | bytes 4456448 | tf_op jit(solution)/shard_map/all_gather | solution.py:73
  68.9 4.4 %copy-start.1 = (u32[128]{0:T(128)S(1)}, u32[128]{0:T(128)}, u32[]{:S(2)}) copy-start(u32[128]{0:T(128)} %constant.62) | copy-start | bytes 1540
  69.6 46.7 %copy-start = (bf16[512,1,8,128]{0,3,2,1:T(8,128)(2,1)}, bf16[512,1,8,128]{0,3,2,1:T(8,128)(2,1)S(1)}, u32[]{:S(2)}) copy-start(bf16[512,1,8,128]{0,3,2,1:T(8,128)(2,1)S(1)} %copy.41) | copy-start | bytes 3145732
  73.3 104.1 %reduce-scatter.2.cloned.1.call-start = ((), (), s32[]{:S(2)}) async-start(), calls=%async_computation.2 | async-start | bytes 3932160 | tf_op jit(solution)/shard_map/reduce_scatter | solution.py:99
Sparse Core Ops, SparseCore 0:
  9.0 41.9 all-gather.4
  73.4 52.1 all-gather.6
  139.7 37.6 reduce-scatter.1
where the time goes:
time: 186 us; the launch traced here: 184 us
  waiting for transfers between devices  58.7 us (32%)
  blocking collectives  41 us (22%)
  matrix products  34.3 us (18%)
  local copies, waits for them, and re-layouts  30 us (16%)
  between operations  13.8 us (7%)
  other arithmetic  6.08 us (3%)
    unnamed x1, blocking collectives  41 us
    reduce_scatter x1, waiting for transfers between devices, body(): lax.psum_scatter(partial_terms.astype(jnp.bfloat16), 'tensor', scatter_di...  37.8 us
    unnamed x10, local copies, waits for them, and re-layouts  27 us
    all_gather x1, waiting for transfers between devices, body(): lax.all_gather(tokens, 'tensor', axis=1, tiled=True)  16.3 us
    dot_general x1, matrix products, body(): jnp.dot(lax.all_gather(tokens, 'tensor', axis=1, tiled=True), weights, pr...  15.5 us
    dot_general x1, matrix products, body(): partial_terms = jnp.dot(attn, w_out, preferred_element_type=jnp.float32)  7.64 us
    dot_general x1, matrix products, block_terms(): jnp.einsum('hts,hsd->htd', weighted, value_part, preferred_element_type=j...  5.38 us
    all_gather x1, waiting for transfers between devices, body(): lax.all_gather(shard_state[None].astype(jnp.bfloat16), 'seq', axis=0, til...  3.83 us
  transfers between devices with their start and end apart: 3, of which 3 were waited for; matrix products, arithmetic and copies ran while one was open for 19% of the time, Pallas kernels for 0%

commit v1 on v0

v1 whole, which is shorter than its diff:
```python
import functools

import jax
import jax.numpy as jnp
from jax import lax
from jax.experimental import pallas as pl
from jax.experimental.pallas import tpu as pltpu
from jax.sharding import PartitionSpec as P

BF16 = jnp.bfloat16
F32 = jnp.float32
HD = 128
CHUNK = 256
MIB = 1024 * 1024


def dot(a, b):
    return jnp.dot(a, b, preferred_element_type=F32)


def silu(x):
    return x / (1.0 + jnp.exp(-x))


def cost(flops, nbytes, trans=0):
    return pl.CostEstimate(flops=int(flops), bytes_accessed=int(nbytes), transcendentals=int(trans))


def project_kernel(n_x, has_acc, slots_ref, *refs):
    xs, ws, rest = refs[:n_x], refs[n_x : 2 * n_x], refs[2 * n_x :]
    total = rest[0][0] if has_acc else None
    for x, w in zip(xs, ws):
        term = dot(x[...], w[0])
        total = term if total is None else total + term
    rest[-1][0] = total


def project(slots, xs, w, acc, tile=512):
    rows, depth = xs[0].shape
    parts, _, width = w.shape
    n = len(xs)
    per = width // tile
    in_specs = [pl.BlockSpec((rows, depth), lambda j, s: (0, 0)) for _ in xs]
    in_specs += [
        pl.BlockSpec((1, depth, tile), lambda j, s, i=i: (j // per, s[i], j % per)) for i in range(n)
    ]
    block = pl.BlockSpec((1, rows, tile), lambda j, s: (j // per, 0, j % per))
    args = list(xs) + [w] * n
    if acc is not None:
        in_specs.append(block)
        args.append(acc)
    return pl.pallas_call(
        functools.partial(project_kernel, n, acc is not None),
        grid_spec=pltpu.PrefetchScalarGridSpec(
            num_scalar_prefetch=1, grid=(parts * per,), in_specs=in_specs, out_specs=block
        ),
        out_shape=jax.ShapeDtypeStruct((parts, rows, width), F32),
        compiler_params=pltpu.CompilerParams(vmem_limit_bytes=20 * MIB),
        cost_estimate=cost(2 * n * rows * depth * parts * width, n * depth * parts * width * 2 + rows * parts * width * 8),
        name="project",
    )(slots, *args)


def key_value_kernel(slots, xt, xb, wk, wv, ak, av, ek, etail, k_out, v_out, s1_out, s_out):
    half = xt.shape[0]
    for r, x in ((0, xt), (half, xb)):
        sl = pl.ds(r, half)
        k_out[sl, :] = silu(ak[0, sl, :] + dot(x[...], wk[0])).astype(BF16)
        v_out[sl, :] = silu(av[0, sl, :] + dot(x[...], wv[0])).astype(BF16)
    heads = k_out.shape[1] // HD
    for h in range(heads):
        cols = pl.ds(h * HD, HD)
        sums = []
        for c in range(k_out.shape[0] // CHUNK):
            sl = pl.ds(c * CHUNK, CHUNK)
            ks = (k_out[sl, cols].astype(F32) * ek[0, sl, h : h + 1]).astype(BF16)
            sums.append(
                lax.dot_general(ks, v_out[sl, cols], (((0,), (0,)), ((), ())), preferred_element_type=F32)
            )
        s1_out[h] = sums[0]
        s_out[h] = (sums[0] * etail[0, 0:1, h : h + 1] + sums[1]).astype(BF16)


def key_value(slots, xt, xb, w, acc, ek, etail, tile=512):
    rows = acc.shape[1]
    half, depth = xt.shape
    width = w.shape[2]
    per = width // tile
    hp = tile // HD
    heads = width // HD
    ek = ek.reshape(per, hp, rows).transpose(0, 2, 1)
    etail = etail.reshape(per, 1, hp)
    x_spec = pl.BlockSpec((half, depth), lambda j, s: (0, 0))
    return pl.pallas_call(
        key_value_kernel,
        grid_spec=pltpu.PrefetchScalarGridSpec(
            num_scalar_prefetch=1,
            grid=(per,),
            in_specs=[
                x_spec,
                x_spec,
                pl.BlockSpec((1, depth, tile), lambda j, s: (1, s[0], j)),
                pl.BlockSpec((1, depth, tile), lambda j, s: (2, s[0], j)),
                pl.BlockSpec((1, rows, tile), lambda j, s: (1, 0, j)),
                pl.BlockSpec((1, rows, tile), lambda j, s: (2, 0, j)),
                pl.BlockSpec((1, rows, hp), lambda j, s: (j, 0, 0)),
                pl.BlockSpec((1, 1, hp), lambda j, s: (j, 0, 0)),
            ],
            out_specs=[
                pl.BlockSpec((rows, tile), lambda j, s: (0, j)),
                pl.BlockSpec((rows, tile), lambda j, s: (0, j)),
                pl.BlockSpec((hp, HD, HD), lambda j, s: (j, 0, 0)),
                pl.BlockSpec((hp, HD, HD), lambda j, s: (j, 0, 0)),
            ],
        ),
        out_shape=[
            jax.ShapeDtypeStruct((rows, width), BF16),
            jax.ShapeDtypeStruct((rows, width), BF16),
            jax.ShapeDtypeStruct((heads, HD, HD), F32),
            jax.ShapeDtypeStruct((heads, HD, HD), BF16),
        ],
        compiler_params=pltpu.CompilerParams(vmem_limit_bytes=28 * MIB),
        cost_estimate=cost(4 * rows * depth * width, 8 * rows * width + 4 * depth * width),
        name="key_value",
    )(slots, xt, xb, w, w, acc, acc, ek, etail)


def inner_kernel(slots, xt, xb, wq, aq, k, v, acol, arow, q_out, o_out):
    half = xt.shape[0]
    for r, x in ((0, xt), (half, xb)):
        sl = pl.ds(r, half)
        q_out[sl, :] = silu(aq[0, sl, :] + dot(x[...], wq[0])).astype(BF16)
    t = lax.broadcasted_iota(jnp.int32, (CHUNK, CHUNK), 0)
    s = lax.broadcasted_iota(jnp.int32, (CHUNK, CHUNK), 1)
    causal = s <= t
    for h in range(q_out.shape[1] // HD):
        cols = pl.ds(h * HD, HD)
        for c in range(q_out.shape[0] // CHUNK):
            sl = pl.ds(c * CHUNK, CHUNK)
            scores = lax.dot_general(
                q_out[sl, cols], k[sl, cols], (((1,), (1,)), ((), ())), preferred_element_type=F32
            )
            spread = acol[0, sl, h : h + 1] - arow[0, h : h + 1, sl]
            weighted = jnp.where(causal, scores * jnp.exp(jnp.minimum(spread, 0.0)), 0.0)
            o_out[sl, cols] = dot(weighted.astype(BF16), v[sl, cols])


def inner(slots, xt, xb, w, acc, k, v, a, tile=256):
    rows = acc.shape[1]
    half, depth = xt.shape
    width = w.shape[2]
    per = width // tile
    hp = tile // HD
    arow = a.reshape(per, hp, rows)
    acol = arow.transpose(0, 2, 1)
    x_spec = pl.BlockSpec((half, depth), lambda j, s: (0, 0))
    tile_spec = pl.BlockSpec((rows, tile), lambda j, s: (0, j))
    return pl.pallas_call(
        inner_kernel,
        grid_spec=pltpu.PrefetchScalarGridSpec(
            num_scalar_prefetch=1,
            grid=(per,),
            in_specs=[
                x_spec,
                x_spec,
                pl.BlockSpec((1, depth, tile), lambda j, s: (0, s[0], j)),
                pl.BlockSpec((1, rows, tile), lambda j, s: (0, 0, j)),
                tile_spec,
                tile_spec,
                pl.BlockSpec((1, rows, hp), lambda j, s: (j, 0, 0)),
                pl.BlockSpec((1, hp, rows), lambda j, s: (j, 0, 0)),
            ],
            out_specs=[tile_spec, tile_spec],
        ),
        out_shape=[
            jax.ShapeDtypeStruct((rows, width), BF16),
            jax.ShapeDtypeStruct((rows, width), F32),
        ],
        compiler_params=pltpu.CompilerParams(vmem_limit_bytes=20 * MIB),
        cost_estimate=cost(2 * rows * depth * width + 4 * rows * CHUNK * width, 14 * rows * width + 2 * depth * width),
        name="inner",
    )(slots, xt, xb, w, acc, k, v, acol, arow)


def attend_kernel(slots, q, o, state, s1, ea, eh, w, attn, top, bot):
    half = top.shape[0]

    @pl.when(pl.program_id(0) == 0)
    def _():
        for h in range(q.shape[1] // HD):
            cols = pl.ds(h * HD, HD)
            first = state[h]
            second = first * eh[0:1, h : h + 1] + s1[h]
            for c, held in ((0, first), (1, second)):
                sl = pl.ds(c * CHUNK, CHUNK)
                qs = (q[sl, cols].astype(F32) * ea[sl, h : h + 1]).astype(BF16)
                out = o[sl, cols] + dot(qs, held.astype(BF16))
                mean = jnp.mean(out * out, axis=1, keepdims=True)
                attn[sl, cols] = (out * lax.rsqrt(mean + 1e-6)).astype(BF16)

    top[...] = dot(attn[pl.ds(0, half), :], w[...]).astype(BF16)
    bot[...] = dot(attn[pl.ds(half, half), :], w[...]).astype(BF16)


def attend(slots, q, o, state, s1, ea, eh, w_out, slice_width, tile=256):
    rows, width = q.shape
    heads = width // HD
    per = slice_width // tile
    half = rows // 2
    whole = lambda *shape: pl.BlockSpec(shape, lambda j, s: (0,) * len(shape))
    return pl.pallas_call(
        attend_kernel,
        grid_spec=pltpu.PrefetchScalarGridSpec(
            num_scalar_prefetch=1,
            grid=(per,),
            in_specs=[
                whole(rows, width),
                whole(rows, width),
                whole(heads, HD, HD),
                whole(heads, HD, HD),
                whole(rows, heads),
                whole(1, heads),
                pl.BlockSpec((width, tile), lambda j, s: (0, s[0] * per + j)),
            ],
            out_specs=[
                whole(rows, width),
                pl.BlockSpec((half, tile), lambda j, s: (0, j)),
                pl.BlockSpec((half, tile), lambda j, s: (0, j)),
            ],
        ),
        out_shape=[
            jax.ShapeDtypeStruct((rows, width), BF16),
            jax.ShapeDtypeStruct((half, slice_width), BF16),
            jax.ShapeDtypeStruct((half, slice_width), BF16),
        ],
        compiler_params=pltpu.CompilerParams(vmem_limit_bytes=28 * MIB),
        cost_estimate=cost(2 * rows * width * (HD + slice_width), rows * width * 8 + width * slice_width * 2),
        name="attend",
    )(slots, q, o, state, s1, ea, eh, w_out)


def output_kernel(slots, attn, wp, wm, wo, p_top, p_bot, m_top, m_bot, own):
    half = p_top.shape[0]
    for w, halves in ((wp, (p_top, p_bot)), (wm, (m_top, m_bot))):
        for i, out in enumerate(halves):
            out[...] = dot(attn[pl.ds(i * half, half), :], w[...]).astype(BF16)
    own[...] = dot(attn[...], wo[...]).astype(BF16)


def output(slots, attn, w_out, slice_width, tile=256):
    rows, width = attn.shape
    per = slice_width // tile
    half = rows // 2
    w_spec = lambda i: pl.BlockSpec((width, tile), lambda j, s: (0, s[i] * per + j))
    half_spec = pl.BlockSpec((half, tile), lambda j, s: (0, j))
    return pl.pallas_call(
        output_kernel,
        grid_spec=pltpu.PrefetchScalarGridSpec(
            num_scalar_prefetch=1,
            grid=(per,),
            in_specs=[pl.BlockSpec((rows, width), lambda j, s: (0, 0)), w_spec(0), w_spec(1), w_spec(2)],
            out_specs=[half_spec] * 4 + [pl.BlockSpec((rows, tile), lambda j, s: (0, j))],
        ),
        out_shape=[jax.ShapeDtypeStruct((half, slice_width), BF16)] * 4
        + [jax.ShapeDtypeStruct((rows, slice_width), BF16)],
        compiler_params=pltpu.CompilerParams(vmem_limit_bytes=20 * MIB),
        cost_estimate=cost(6 * rows * width * slice_width, 6 * width * slice_width + 8 * rows * slice_width),
        name="output",
    )(slots, attn, w_out, w_out, w_out)


def finish_kernel(own, lt, lb, rt, rb, out):
    half = lt.shape[0]
    for i, (a, b) in enumerate(((lt, rt), (lb, rb))):
        sl = pl.ds(i * half, half)
        out[sl, :] = (own[sl, :].astype(F32) + a[...].astype(F32) + b[...].astype(F32)).astype(BF16)


def finish(own, lt, lb, rt, rb):
    return pl.pallas_call(
        finish_kernel,
        out_shape=jax.ShapeDtypeStruct(own.shape, BF16),
        compiler_params=pltpu.CompilerParams(vmem_limit_bytes=16 * MIB),
        cost_estimate=cost(own.size * 2, own.size * 8),
        name="finish",
    )(own, lt, lb, rt, rb)


def body(n_y, tokens, w_qkv, log_decay, w_out):
    rows, slice_width = tokens.shape
    heads = log_decay.shape[0]
    n_t = lax.axis_size("tensor")
    n_seq = lax.axis_size("seq")
    n_z = n_seq // n_y
    me = lax.axis_index("tensor")
    pos = lax.axis_index("seq")
    my_z, my_y = pos // n_y, pos % n_y
    half = rows // 2

    def along_x(x, shift):
        return lax.ppermute(x, "tensor", [(i, (i + shift) % n_t) for i in range(n_t)])

    def along_y(x, shift):
        return lax.ppermute(
            x, "seq", [(z * n_y + y, z * n_y + (y + shift) % n_y) for z in range(n_z) for y in range(n_y)]
        )

    def along_z(x, shift):
        return lax.ppermute(
            x, "seq", [(z * n_y + y, (z + shift) * n_y + y) for z in range(n_z - shift) for y in range(n_y)]
        )

    def slot(*shifts):
        return jnp.stack([(me + s) % n_t for s in shifts]).astype(jnp.int32)

    left = along_x(tokens, 1)
    right = along_x(tokens, -1)

    chunks = rows // CHUNK
    a = jnp.cumsum(log_decay.reshape(heads, chunks, CHUNK), axis=2)
    ends = a[:, :, -1]
    shard_log = jnp.sum(ends, axis=1)
    ek = jnp.exp(ends[:, :, None] - a).reshape(heads, rows)
    a = a.reshape(heads, rows)
    ea = jnp.exp(a).T
    etail = jnp.exp(ends[:, 1])
    ehead = jnp.exp(ends[:, 0]).reshape(1, heads)

    row_logs = [shard_log] + [along_y(shard_log, d) for d in range(1, n_y)]
    ys = [(my_y - d) % n_y for d in range(n_y)]
    after = [
        sum(jnp.where(ys[e] > ys[d], row_logs[e], 0.0) for e in range(n_y)) for d in range(n_y)
    ]
    between = [
        sum(jnp.where((ys[e] > ys[d]) & (ys[e] < my_y), row_logs[e], 0.0) for e in range(n_y))
        for d in range(n_y)
    ]
    before = sum(jnp.where(ys[e] < my_y, row_logs[e], 0.0) for e in range(n_y))
    to_row_end = [jnp.exp(x) for x in after]
    to_here = [jnp.where(ys[d] < my_y, jnp.exp(between[d]), 0.0) for d in range(n_y)]
    row_log = sum(row_logs)
    other_rows = [along_z(row_log, e) for e in range(1, n_z)]
    from_row = []
    gap = before
    for e in range(1, n_z):
        from_row.append(jnp.where(e <= my_z, jnp.exp(gap), 0.0))
        gap = gap + other_rows[e - 1]

    w = w_qkv.transpose(1, 0, 2)
    acc = project(slot(0), [tokens], w, None)

    opp_top = along_x(left[:half], 1)
    opp_bot = along_x(right[half:], -1)
    acc = project(slot(-1, 1), [left, right], w, acc)

    far = slot(2)
    k, v, s1, shard_kv = key_value(far, opp_top, opp_bot, w, acc, ek, etail)

    def scaled(weight, x):
        return weight[:, None, None] * x.astype(F32)

    row_kvs = [shard_kv] + [along_y(shard_kv, d) for d in range(1, n_y)]
    q, o = inner(far, opp_top, opp_bot, w, acc, k, v, a)
    row_kv = sum(scaled(to_row_end[d], row_kvs[d]) for d in range(n_y)).astype(BF16)
    state = sum(scaled(to_here[d], row_kvs[d]) for d in range(1, n_y))
    earlier = [along_z(row_kv, e) for e in range(1, n_z)]
    state = state + sum(scaled(from_row[e - 1], earlier[e - 1]) for e in range(1, n_z))

    attn, far_top, far_bot = attend(far, q, o, state, s1, ea, ehead, w_out, slice_width)
    relay_top = along_x(far_top, 1)
    relay_bot = along_x(far_bot, -1)
    p_top, p_bot, m_top, m_bot, own = output(slot(1, -1, 0), attn, w_out, slice_width)
    left_bot = along_x(p_bot, 1)
    right_top = along_x(m_top, -1)
    left_top = along_x(p_top + relay_top, 1)
    right_bot = along_x(m_bot + relay_bot, -1)
    return finish(own, left_top, left_bot, right_top, right_bot)


def solution(mesh):
    in_specs = (
        P(("dp", "seq"), "tensor"),
        P(None, None, "tensor"),
        P("tensor", ("dp", "seq")),
        P("tensor", None),
    )
    out_specs = P(("dp", "seq"), "tensor")
    n_seq = mesh.shape["seq"]
    n_y = 4 if n_seq % 4 == 0 else 1
    return jax.shard_map(
        functools.partial(body, n_y), mesh=mesh, in_specs=in_specs, out_specs=out_specs, check_vma=False
    )
```

time: 186 us -> 124 us (0.67)
  waiting for transfers between devices: 58.7 us -> 15.3 us
  starting transfers between devices: 0.08 us -> 43.2 us
  blocking collectives: 41 us -> 0 us
  matrix products: 34.3 us -> 0 us
  Pallas kernels: 0 us -> 32.5 us
  between operations: 13.8 us -> 0.4 us
  other arithmetic: 6.08 us -> 2.54 us
    ppermute x0 -> x21, starting transfers between devices: none -> 43.2 us  [the longest x5 19.9 us: along_z(): lax.ppermute(x, 'seq', [(z * n_y + y, (z + shift) * n_y + y) for z in ran...]
    unnamed x1 -> x0, blocking collectives: 41 us -> none
    reduce_scatter x1 -> x0, waiting for transfers between devices: 37.8 us -> none  [body(): lax.psum_scatter(partial_terms.astype(jnp.bfloat16), 'tensor', scatter_di...]
    dot_general x5 -> x0, matrix products: 34.3 us -> none  [the longest x1 15.5 us: body(): jnp.dot(lax.all_gather(tokens, 'tensor', axis=1, tiled=True), weights, pr...]
    pallas_call x0 -> x7, Pallas kernels: none -> 32.5 us  [the longest x2 12.5 us: project(): pl.pallas_call(functools.partial(project_kernel, n, acc is not None), gri...]
    all_gather x2 -> x0, waiting for transfers between devices: 20.2 us -> none  [the longest x1 16.3 us: body(): lax.all_gather(tokens, 'tensor', axis=1, tiled=True)]
    ppermute x0 -> x21, waiting for transfers between devices: none -> 15.3 us  [the longest x10 14.9 us: along_x(): lax.ppermute(x, 'tensor', [(i, (i + shift) % n_t) for i in range(n_t)])]
    unnamed x2 -> x1, other arithmetic: 3.14 us -> 0.01 us
  transfers between devices with their start and end apart: 3 -> 21, of which waited for: 3 -> 7; matrix products, arithmetic and copies ran while one was open for 19% -> 3% of each run, Pallas kernels for 0% -> 21%
where the time goes in v1:
time: 124 us; the launch traced here: 123 us
  starting transfers between devices  43.2 us (35%)
  Pallas kernels  32.5 us (26%)
  local copies, waits for them, and re-layouts  29.2 us (24%)
  waiting for transfers between devices  15.3 us (12%)
  other arithmetic  2.54 us (2%)
    unnamed x20, local copies, waits for them, and re-layouts  25.7 us
    ppermute x5, starting transfers between devices, along_z(): lax.ppermute(x, 'seq', [(z * n_y + y, (z + shift) * n_y + y) for z in ran...  19.9 us
    ppermute x10, waiting for transfers between devices, along_x(): lax.ppermute(x, 'tensor', [(i, (i + shift) % n_t) for i in range(n_t)])  14.9 us
    ppermute x10, starting transfers between devices, along_x(): lax.ppermute(x, 'tensor', [(i, (i + shift) % n_t) for i in range(n_t)])  14 us
    pallas_call x2, Pallas kernels, project(): pl.pallas_call(functools.partial(project_kernel, n, acc is not None), gri...  12.5 us
    ppermute x6, starting transfers between devices, along_y(): lax.ppermute(x, 'seq', [(z * n_y + y, z * n_y + (y + shift) % n_y) for z...  9.17 us
    pallas_call x1, Pallas kernels, attend(): pl.pallas_call(attend_kernel, grid_spec=pltpu.PrefetchScalarGridSpec(num_...  5 us
    pallas_call x1, Pallas kernels, key_value(): pl.pallas_call(key_value_kernel, grid_spec=pltpu.PrefetchScalarGridSpec(n...  4.7 us
  transfers between devices with their start and end apart: 21, of which 7 were waited for; matrix products, arithmetic and copies ran while one was open for 3% of the time, Pallas kernels for 21%

profile of v1, /device:TPU:0, one launch (start us, length us, event | category | flops | bytes accessed | tf_op | source)
XLA Modules:
  0.0 123.1 jit_solution(8478821290755834389)
XLA Ops:
  2.4 3.3 %collective-permute-start.4 = (f32[8]{0:T(128)S(1)}, f32[8]{0:T(128)S(1)}, u32[]{:S(2)}, u32[]{:S(2)}) collective-permute-start(f32[8]{0:T(128)S(1)} %get-tuple-element.33), channel_id=1, source_target_pairs={{0,8},{4,12},{8,0},{12,4},{16,24},{20,28},{24,16},{28,20},{32,40},... | collective-permute-start | bytes 104 | tf_op jit(solution)/shard_map/ppermute | solution.py:304
  9.2 1.7 %collective-permute-start.2 = (bf16[512,768]{1,0:T(8,128)(2,1)}, bf16[512,768]{1,0:T(8,128)(2,1)S(1)}, u32[]{:S(2)}, u32[]{:S(2)}) collective-permute-start(bf16[512,768]{1,0:T(8,128)(2,1)} %refs_0_.1), channel_id=1, source_target_pairs={{0,3},{1,0},{2,1},{3,2},{4,7},{5,4},{6,5},{7,6},{8,11},{9,8},{10,9... | collective-permute-start | bytes 2359304 | tf_op jit(solution)/shard_map/ppermute | solution.py:301
  13.7 6.4 %copy-done = bf16[3072,3,1024]{2,0,1:T(8,128)(2,1)S(1)} copy-done((bf16[3072,3,1024]{2,0,1:T(8,128)(2,1)S(1)}, bf16[3072,3,1024]{2,0,1:T(8,128)(2,1)}, u32[]{:S(2)}) %copy-start) | copy-done | bytes 18874392
  21.2 4.3 %project.2.refs_4_ = f32[3,512,1024]{2,1,0:T(8,128)S(1)} custom-call(s32[1]{0:T(128)} %bitcast.2.slots_ref, bf16[512,768]{1,0:T(8,128)(2,1)S(1)} %copy-done.7, bf16[3,3072,1024]{2,1,0:T(8,128)(2,1)S(1)} %bitcast.25), custom_call_target="tpu_custom_call" | custom-call | flops 2415919104 | bytes 17301504 | tf_op jit(solution)/shard_map/project/pallas_call | solution.py:52
  25.6 2.6 %copy-done.3 = f32[3,512,1024]{2,1,0:T(8,128)} copy-done((f32[3,512,1024]{2,1,0:T(8,128)}, f32[3,512,1024]{2,1,0:T(8,128)S(1)}, u32[]{:S(2)}) %copy-start.3) | copy-done | bytes 6291480
  28.6 3.0 %collective-permute-start.3 = (bf16[256,768]{1,0:T(8,128)(2,1)S(1)}, bf16[256,768]{1,0:T(8,128)(2,1)S(1)}, u32[]{:S(2)}, u32[]{:S(2)}) collective-permute-start(bf16[256,768]{1,0:T(8,128)(2,1)S(1)} %slice.29), channel_id=1, source_target_pairs={{0,3},{1,0},{2,1},{3,2},{4,7},{5,4},{6,5},{7,6},{8,11},{9,8},{10,9... | collective-permute-start | bytes 1179656 | tf_op jit(solution)/shard_map/ppermute | solution.py:301
  31.6 6.4 %copy-done.1 = bf16[3072,3,1024]{2,0,1:T(8,128)(2,1)S(1)} copy-done((bf16[3072,3,1024]{2,0,1:T(8,128)(2,1)S(1)}, bf16[3072,3,1024]{2,0,1:T(8,128)(2,1)}, u32[]{:S(2)}) %copy-start.1) | copy-done | bytes 18874392
  38.0 2.8 %copy-done.4 = f32[3,512,1024]{2,1,0:T(8,128)S(1)} copy-done((f32[3,512,1024]{2,1,0:T(8,128)S(1)}, f32[3,512,1024]{2,1,0:T(8,128)}, u32[]{:S(2)}) %copy-start.4) | copy-done | bytes 6291480
  40.8 8.2 %project.3.ak.av.aq = f32[3,512,1024]{2,1,0:T(8,128)S(1)} custom-call(s32[2]{0:T(128)S(1)} %pad_add_fusion.1.slots_ref, bf16[512,768]{1,0:T(8,128)(2,1)S(1)} %collective-permute-done.refs_0_, bf16[512,768]{1,0:T(8,128)(2,1)S(1)} %collective-permute-done.2.refs_1_, bf16[3,3072,1024]{2,1,0:T(8,128)(2,1)S(1)} %bitcast.26, bf16[3,3072,1024]{2,1,0:T(8,128)(2,1)S(1)} %bitcast.27, ...), custom_call_target="tpu_custom_call" | custom-call | flops 4831838208 | bytes 22020096 | tf_op jit(solution)/shard_map/project/pallas_call | solution.py:52
  49.0 4.7 %key_value.1 = (bf16[512,1024]{1,0:T(8,128)(2,1)S(1)}, bf16[512,1024]{1,0:T(8,128)(2,1)S(1)}, f32[8,128,128]{2,1,0:T(8,128)S(1)}, bf16[8,128,128]{2,1,0:T(8,128)(2,1)S(1)}) custom-call(s32[1]{0:T(128)} %bitcast.3.slots, bf16[256,768]{1,0:T(8,128)(2,1)S(1)} %collective-permute-done.1.xt, bf16[256,768]{1,0:T(8,128)(2,1)S(1)} %collective-permute-done.3.xb, ...), custom_call_target="tpu_custom_call" | custom-call | flops 1610612736 | bytes 7340032 | tf_op jit(solution)/shard_map/key_value/pallas_call | solution.py:94
  54.5 3.1 %collective-permute-start.8 = (bf16[8,128,128]{2,1,0:T(8,128)(2,1)S(1)}, bf16[8,128,128]{2,1,0:T(8,128)(2,1)S(1)}, u32[]{:S(2)}, u32[]{:S(2)}) collective-permute-start(bf16[8,128,128]{2,1,0:T(8,128)(2,1)S(1)} %get-tuple-element.23), channel_id=1, source_target_pairs={{0,8},{4,12},{8,0},{12,4},{16,24},{20,28},{24,16},{28,20},{32,40},... | collective-permute-start | bytes 786440 | tf_op jit(solution)/shard_map/ppermute | solution.py:304
  57.6 3.8 %collective-permute-start.11 = (f32[8]{0:T(128)S(1)}, f32[8]{0:T(128)S(1)}, u32[]{:S(2)}, u32[]{:S(2)}) collective-permute-start(f32[8]{0:T(128)S(1)} %get-tuple-element.42), channel_id=1, source_target_pairs={{0,16},{4,20},{8,24},{12,28},{16,32},{20,36},{24,40},{28,44},{32,4... | collective-permute-start | bytes 104 | tf_op jit(solution)/shard_map/ppermute | solution.py:309
  61.4 5.5 %collective-permute-start.13 = (f32[8]{0:T(128)S(1)}, f32[8]{0:T(128)S(1)}, u32[]{:S(2)}, u32[]{:S(2)}) collective-permute-start(f32[8]{0:T(128)S(1)} %get-tuple-element.42), channel_id=1, source_target_pairs={{0,32},{4,36},{8,40},{12,44},{16,48},{20,52},{24,56},{28,60},{1,33... | collective-permute-start | bytes 104 | tf_op jit(solution)/shard_map/ppermute | solution.py:309
  67.7 3.8 %collective-permute-start.10 = (bf16[8,128,128]{2,1,0:T(8,128)(2,1)S(1)}, bf16[8,128,128]{2,1,0:T(8,128)(2,1)S(1)}, u32[]{:S(2)}, u32[]{:S(2)}) collective-permute-start(bf16[8,128,128]{2,1,0:T(8,128)(2,1)S(1)} %fusion.6), channel_id=1, source_target_pairs={{0,16},{4,20},{8,24},{12,28},{16,32},{20,36},{24,40},{28,44},{32,4... | collective-permute-start | bytes 786440 | tf_op jit(solution)/shard_map/ppermute | solution.py:309
  71.5 5.5 %collective-permute-start.12 = (bf16[8,128,128]{2,1,0:T(8,128)(2,1)S(1)}, bf16[8,128,128]{2,1,0:T(8,128)(2,1)S(1)}, u32[]{:S(2)}, u32[]{:S(2)}) collective-permute-start(bf16[8,128,128]{2,1,0:T(8,128)(2,1)S(1)} %fusion.6), channel_id=1, source_target_pairs={{0,32},{4,36},{8,40},{12,44},{16,48},{20,52},{24,56},{28,60},{1,33... | collective-permute-start | bytes 786440 | tf_op jit(solution)/shard_map/ppermute | solution.py:309
  78.4 6.4 %copy-done.2 = bf16[3072,3,1024]{2,0,1:T(8,128)(2,1)S(1)} copy-done((bf16[3072,3,1024]{2,0,1:T(8,128)(2,1)S(1)}, bf16[3072,3,1024]{2,0,1:T(8,128)(2,1)}, u32[]{:S(2)}) %copy-start.2) | copy-done | bytes 18874392
  84.7 4.6 %inner.1 = (bf16[512,1024]{1,0:T(8,128)(2,1)S(1)}, f32[512,1024]{1,0:T(8,128)S(1)}) custom-call(s32[1]{0:T(128)} %bitcast.3.slots, bf16[256,768]{1,0:T(8,128)(2,1)S(1)} %collective-permute-done.1.xt, bf16[256,768]{1,0:T(8,128)(2,1)S(1)} %collective-permute-done.3.xb, bf16[3,3072,1024]{2,1,0:T(8,128)(2,1)S(1)} %bitcast.28, ...), custom_call_target="tpu_custom_call" | custom-call | flops 1342177280 | bytes 8912896 | tf_op jit(solution)/shard_map/inner/pallas_call | solution.py:158
  89.8 5.0 %attend.1 = (bf16[512,1024]{1,0:T(8,128)(2,1)S(1)}, bf16[256,768]{1,0:T(8,128)(2,1)S(1)}, bf16[256,768]{1,0:T(8,128)(2,1)S(1)}) custom-call(s32[1]{0:T(128)} %bitcast.3.slots, bf16[512,1024]{1,0:T(8,128)(2,1)S(1)} %get-tuple-element.21.q, f32[512,1024]{1,0:T(8,128)S(1)} %get-tuple-element.22.o, f32[8,128,128]{2,1,0:T(8,128)S(1)} %fusion.2.state, ...), custom_call_target="tpu_custom_call" | custom-call | flops 939524096 | bytes 5767168 | tf_op jit(solution)/shard_map/attend/pallas_call | solution.py:211
  95.4 1.7 %collective-permute-start.15 = (bf16[256,768]{1,0:T(8,128)(2,1)S(1)}, bf16[256,768]{1,0:T(8,128)(2,1)S(1)}, u32[]{:S(2)}, u32[]{:S(2)}) collective-permute-start(bf16[256,768]{1,0:T(8,128)(2,1)S(1)} %get-tuple-element.28), channel_id=1, source_target_pairs={{0,1},{1,2},{2,3},{3,0},{4,5},{5,6},{6,7},{7,4},{8,9},{9,10},{10,1... | collective-permute-start | bytes 1179656 | tf_op jit(solution)/shard_map/ppermute | solution.py:301
  97.1 4.5 %output.1 = (bf16[256,768]{1,0:T(8,128)(2,1)S(1)}, bf16[256,768]{1,0:T(8,128)(2,1)S(1)}, bf16[256,768]{1,0:T(8,128)(2,1)S(1)}, bf16[256,768]{1,0:T(8,128)(2,1)S(1)}, bf16[512,768]{1,0:T(8,128)(2,1)S(1)}) custom-call(s32[3]{0:T(128)S(1)} %pad_add_fusion.slots, bf16[512,1024]{1,0:T(8,128)(2,1)S(1)} %get-tuple-element.25.attn, bf16[1024,3072]{1,0:T(8,128)(2,1)S(1)} %bitcast.30, ...), custom_call_target="tpu_custom_call" | custom-call | flops 2415919104 | bytes 7864320 | tf_op jit(solution)/shard_map/output/pallas_call | solution.py:256
  101.7 3.2 %collective-permute-start.18 = (bf16[256,768]{1,0:T(8,128)(2,1)S(1)}, bf16[256,768]{1,0:T(8,128)(2,1)S(1)}, u32[]{:S(2)}, u32[]{:S(2)}) collective-permute-start(bf16[256,768]{1,0:T(8,128)(2,1)S(1)} %get-tuple-element.30), channel_id=1, source_target_pairs={{0,3},{1,0},{2,1},{3,2},{4,7},{5,4},{6,5},{7,6},{8,11},{9,8},{10,9... | collective-permute-start | bytes 1179656 | tf_op jit(solution)/shard_map/ppermute | solution.py:301
  107.5 1.8 %collective-permute-start.16 = (bf16[256,768]{1,0:T(8,128)(2,1)S(1)}, bf16[256,768]{1,0:T(8,128)(2,1)S(1)}, u32[]{:S(2)}, u32[]{:S(2)}) collective-permute-start(bf16[256,768]{1,0:T(8,128)(2,1)S(1)} %add.191), channel_id=1, source_target_pairs={{0,1},{1,2},{2,3},{3,0},{4,5},{5,6},{6,7},{7,4},{8,9},{9,10},{10,1... | collective-permute-start | bytes 1179656 | tf_op jit(solution)/shard_map/ppermute | solution.py:301
  109.3 6.5 %collective-permute-done.17.lb = bf16[256,768]{1,0:T(8,128)(2,1)S(1)} collective-permute-done((bf16[256,768]{1,0:T(8,128)(2,1)S(1)}, bf16[256,768]{1,0:T(8,128)(2,1)S(1)}, u32[]{:S(2)}, u32[]{:S(2)}) %collective-permute-start.17) | collective-permute-done | bytes 393248 | tf_op jit(solution)/shard_map/ppermute | solution.py:301
  115.8 4.8 %collective-permute-done.20.rb = bf16[256,768]{1,0:T(8,128)(2,1)S(1)} collective-permute-done((bf16[256,768]{1,0:T(8,128)(2,1)S(1)}, bf16[256,768]{1,0:T(8,128)(2,1)S(1)}, u32[]{:S(2)}, u32[]{:S(2)}) %collective-permute-start.20) | collective-permute-done | bytes 393248 | tf_op jit(solution)/shard_map/ppermute | solution.py:301
  (79 shorter events, 19.0 us)
Async XLA Ops:
  2.4 55.2 %collective-permute-start.4 = (f32[8]{0:T(128)S(1)}, f32[8]{0:T(128)S(1)}, u32[]{:S(2)}, u32[]{:S(2)}) collective-permute-start(f32[8]{0:T(128)S(1)} %get-tuple-element.33), channel_id=1, source_target_pairs={{0,8},{4,12},{8,0},{12,4},{16,24},{20,28},{24,16},{28,20},{32,40},... | collective-permute-start | bytes 104 | tf_op jit(solution)/shard_map/ppermute | solution.py:304
  5.7 51.9 %collective-permute-start.5 = (f32[8]{0:T(128)S(1)}, f32[8]{0:T(128)S(1)}, u32[]{:S(2)}, u32[]{:S(2)}) collective-permute-start(f32[8]{0:T(128)S(1)} %get-tuple-element.33), channel_id=1, source_target_pairs={{0,12},{4,0},{8,4},{12,8},{16,28},{20,16},{24,20},{28,24},{32,44},... | collective-permute-start | bytes 104 | tf_op jit(solution)/shard_map/ppermute | solution.py:304
  6.8 50.8 %collective-permute-start.7 = (f32[8]{0:T(128)S(1)}, f32[8]{0:T(128)S(1)}, u32[]{:S(2)}, u32[]{:S(2)}) collective-permute-start(f32[8]{0:T(128)S(1)} %get-tuple-element.33), channel_id=1, source_target_pairs={{0,4},{4,8},{8,12},{12,0},{16,20},{20,24},{24,28},{28,16},{32,36},... | collective-permute-start | bytes 104 | tf_op jit(solution)/shard_map/ppermute | solution.py:304
  7.7 20.5 %collective-permute-start = (bf16[512,768]{1,0:T(8,128)(2,1)}, bf16[512,768]{1,0:T(8,128)(2,1)S(1)}, u32[]{:S(2)}, u32[]{:S(2)}) collective-permute-start(bf16[512,768]{1,0:T(8,128)(2,1)} %refs_0_.1), channel_id=1, source_target_pairs={{0,1},{1,2},{2,3},{3,0},{4,5},{5,6},{6,7},{7,4},{8,9},{9,10},{10,1... | collective-permute-start | bytes 2359304 | tf_op jit(solution)/shard_map/ppermute | solution.py:301
  9.2 19.4 %collective-permute-start.2 = (bf16[512,768]{1,0:T(8,128)(2,1)}, bf16[512,768]{1,0:T(8,128)(2,1)S(1)}, u32[]{:S(2)}, u32[]{:S(2)}) collective-permute-start(bf16[512,768]{1,0:T(8,128)(2,1)} %refs_0_.1), channel_id=1, source_target_pairs={{0,3},{1,0},{2,1},{3,2},{4,7},{5,4},{6,5},{7,6},{8,11},{9,8},{10,9... | collective-permute-start | bytes 2359304 | tf_op jit(solution)/shard_map/ppermute | solution.py:301
  28.2 20.8 %collective-permute-start.1 = (bf16[256,768]{1,0:T(8,128)(2,1)S(1)}, bf16[256,768]{1,0:T(8,128)(2,1)S(1)}, u32[]{:S(2)}, u32[]{:S(2)}) collective-permute-start(bf16[256,768]{1,0:T(8,128)(2,1)S(1)} %slice.28), channel_id=1, source_target_pairs={{0,1},{1,2},{2,3},{3,0},{4,5},{5,6},{6,7},{7,4},{8,9},{9,10},{10,1... | collective-permute-start | bytes 1179656 | tf_op jit(solution)/shard_map/ppermute | solution.py:301
  28.6 20.4 %collective-permute-start.3 = (bf16[256,768]{1,0:T(8,128)(2,1)S(1)}, bf16[256,768]{1,0:T(8,128)(2,1)S(1)}, u32[]{:S(2)}, u32[]{:S(2)}) collective-permute-start(bf16[256,768]{1,0:T(8,128)(2,1)S(1)} %slice.29), channel_id=1, source_target_pairs={{0,3},{1,0},{2,1},{3,2},{4,7},{5,4},{6,5},{7,6},{8,11},{9,8},{10,9... | collective-permute-start | bytes 1179656 | tf_op jit(solution)/shard_map/ppermute | solution.py:301
  40.8 8.2 %copy-start.5 = (f32[2,4,512]{1,2,0:T(8,128)S(1)}, f32[2,4,512]{1,2,0:T(8,128)}, u32[]{:S(2)}) copy-start(f32[2,4,512]{1,2,0:T(8,128)} %copy.43) | copy-start | bytes 49156
  40.8 48.9 %slice-start = ((s8[6291456]{0:T(1024)(128)(4,1)}), s8[4194304]{0:T(1024)(128)(4,1)S(1)}, s32[]{:S(2)}) async-start(s8[6291456]{0:T(1024)(128)(4,1)} %bitcast.29), calls=%async_computation | async-start | bytes 8388608
  49.0 40.7 %slice-start.1 = ((s8[6291456]{0:T(1024)(128)(4,1)}), s8[2097152]{0:T(1024)(128)(4,1)S(1)}, s32[]{:S(2)}) async-start(s8[6291456]{0:T(1024)(128)(4,1)} %bitcast.29), calls=%async_computation.1 | async-start | bytes 4194304
  53.8 13.2 %collective-permute-start.6 = (bf16[8,128,128]{2,1,0:T(8,128)(2,1)S(1)}, bf16[8,128,128]{2,1,0:T(8,128)(2,1)S(1)}, u32[]{:S(2)}, u32[]{:S(2)}) collective-permute-start(bf16[8,128,128]{2,1,0:T(8,128)(2,1)S(1)} %get-tuple-element.23), channel_id=1, source_target_pairs={{0,4},{4,8},{8,12},{12,0},{16,20},{20,24},{24,28},{28,16},{32,36},... | collective-permute-start | bytes 786440 | tf_op jit(solution)/shard_map/ppermute | solution.py:304
  54.5 12.7 %collective-permute-start.8 = (bf16[8,128,128]{2,1,0:T(8,128)(2,1)S(1)}, bf16[8,128,128]{2,1,0:T(8,128)(2,1)S(1)}, u32[]{:S(2)}, u32[]{:S(2)}) collective-permute-start(bf16[8,128,128]{2,1,0:T(8,128)(2,1)S(1)} %get-tuple-element.23), channel_id=1, source_target_pairs={{0,8},{4,12},{8,0},{12,4},{16,24},{20,28},{24,16},{28,20},{32,40},... | collective-permute-start | bytes 786440 | tf_op jit(solution)/shard_map/ppermute | solution.py:304
  57.6 9.8 %collective-permute-start.9 = (bf16[8,128,128]{2,1,0:T(8,128)(2,1)S(1)}, bf16[8,128,128]{2,1,0:T(8,128)(2,1)S(1)}, u32[]{:S(2)}, u32[]{:S(2)}) collective-permute-start(bf16[8,128,128]{2,1,0:T(8,128)(2,1)S(1)} %get-tuple-element.23), channel_id=1, source_target_pairs={{0,12},{4,0},{8,4},{12,8},{16,28},{20,16},{24,20},{28,24},{32,44},... | collective-permute-start | bytes 786440 | tf_op jit(solution)/shard_map/ppermute | solution.py:304
  57.6 20.7 %collective-permute-start.11 = (f32[8]{0:T(128)S(1)}, f32[8]{0:T(128)S(1)}, u32[]{:S(2)}, u32[]{:S(2)}) collective-permute-start(f32[8]{0:T(128)S(1)} %get-tuple-element.42), channel_id=1, source_target_pairs={{0,16},{4,20},{8,24},{12,28},{16,32},{20,36},{24,40},{28,44},{32,4... | collective-permute-start | bytes 104 | tf_op jit(solution)/shard_map/ppermute | solution.py:309
  61.4 16.9 %collective-permute-start.13 = (f32[8]{0:T(128)S(1)}, f32[8]{0:T(128)S(1)}, u32[]{:S(2)}, u32[]{:S(2)}) collective-permute-start(f32[8]{0:T(128)S(1)} %get-tuple-element.42), channel_id=1, source_target_pairs={{0,32},{4,36},{8,40},{12,44},{16,48},{20,52},{24,56},{28,60},{1,33... | collective-permute-start | bytes 104 | tf_op jit(solution)/shard_map/ppermute | solution.py:309
  67.7 21.7 %collective-permute-start.10 = (bf16[8,128,128]{2,1,0:T(8,128)(2,1)S(1)}, bf16[8,128,128]{2,1,0:T(8,128)(2,1)S(1)}, u32[]{:S(2)}, u32[]{:S(2)}) collective-permute-start(bf16[8,128,128]{2,1,0:T(8,128)(2,1)S(1)} %fusion.6), channel_id=1, source_target_pairs={{0,16},{4,20},{8,24},{12,28},{16,32},{20,36},{24,40},{28,44},{32,4... | collective-permute-start | bytes 786440 | tf_op jit(solution)/shard_map/ppermute | solution.py:309
  71.5 17.9 %collective-permute-start.12 = (bf16[8,128,128]{2,1,0:T(8,128)(2,1)S(1)}, bf16[8,128,128]{2,1,0:T(8,128)(2,1)S(1)}, u32[]{:S(2)}, u32[]{:S(2)}) collective-permute-start(bf16[8,128,128]{2,1,0:T(8,128)(2,1)S(1)} %fusion.6), channel_id=1, source_target_pairs={{0,32},{4,36},{8,40},{12,44},{16,48},{20,52},{24,56},{28,60},{1,33... | collective-permute-start | bytes 786440 | tf_op jit(solution)/shard_map/ppermute | solution.py:309
  77.0 12.4 %collective-permute-start.14 = (bf16[8,128,128]{2,1,0:T(8,128)(2,1)S(1)}, bf16[8,128,128]{2,1,0:T(8,128)(2,1)S(1)}, u32[]{:S(2)}, u32[]{:S(2)}) collective-permute-start(bf16[8,128,128]{2,1,0:T(8,128)(2,1)S(1)} %fusion.6), channel_id=1, source_target_pairs={{0,48},{4,52},{8,56},{12,60},{1,49},{5,53},{9,57},{13,61},{2,50},{... | collective-permute-start | bytes 786440 | tf_op jit(solution)/shard_map/ppermute | solution.py:309
  94.8 11.2 %collective-permute-start.19 = (bf16[256,768]{1,0:T(8,128)(2,1)S(1)}, bf16[256,768]{1,0:T(8,128)(2,1)S(1)}, u32[]{:S(2)}, u32[]{:S(2)}) collective-permute-start(bf16[256,768]{1,0:T(8,128)(2,1)S(1)} %get-tuple-element.32), channel_id=1, source_target_pairs={{0,3},{1,0},{2,1},{3,2},{4,7},{5,4},{6,5},{7,6},{8,11},{9,8},{10,9... | collective-permute-start | bytes 1179656 | tf_op jit(solution)/shard_map/ppermute | solution.py:301
  95.4 12.0 %collective-permute-start.15 = (bf16[256,768]{1,0:T(8,128)(2,1)S(1)}, bf16[256,768]{1,0:T(8,128)(2,1)S(1)}, u32[]{:S(2)}, u32[]{:S(2)}) collective-permute-start(bf16[256,768]{1,0:T(8,128)(2,1)S(1)} %get-tuple-element.28), channel_id=1, source_target_pairs={{0,1},{1,2},{2,3},{3,0},{4,5},{5,6},{6,7},{7,4},{8,9},{9,10},{10,1... | collective-permute-start | bytes 1179656 | tf_op jit(solution)/shard_map/ppermute | solution.py:301
  101.6 14.2 %collective-permute-start.17 = (bf16[256,768]{1,0:T(8,128)(2,1)S(1)}, bf16[256,768]{1,0:T(8,128)(2,1)S(1)}, u32[]{:S(2)}, u32[]{:S(2)}) collective-permute-start(bf16[256,768]{1,0:T(8,128)(2,1)S(1)} %get-tuple-element.29), channel_id=1, source_target_pairs={{0,1},{1,2},{2,3},{3,0},{4,5},{5,6},{6,7},{7,4},{8,9},{9,10},{10,1... | collective-permute-start | bytes 1179656 | tf_op jit(solution)/shard_map/ppermute | solution.py:301
  101.7 14.1 %collective-permute-start.18 = (bf16[256,768]{1,0:T(8,128)(2,1)S(1)}, bf16[256,768]{1,0:T(8,128)(2,1)S(1)}, u32[]{:S(2)}, u32[]{:S(2)}) collective-permute-start(bf16[256,768]{1,0:T(8,128)(2,1)S(1)} %get-tuple-element.30), channel_id=1, source_target_pairs={{0,3},{1,0},{2,1},{3,2},{4,7},{5,4},{6,5},{7,6},{8,11},{9,8},{10,9... | collective-permute-start | bytes 1179656 | tf_op jit(solution)/shard_map/ppermute | solution.py:301
  106.1 14.6 %collective-permute-start.20 = (bf16[256,768]{1,0:T(8,128)(2,1)S(1)}, bf16[256,768]{1,0:T(8,128)(2,1)S(1)}, u32[]{:S(2)}, u32[]{:S(2)}) collective-permute-start(bf16[256,768]{1,0:T(8,128)(2,1)S(1)} %add.192), channel_id=1, source_target_pairs={{0,3},{1,0},{2,1},{3,2},{4,7},{5,4},{6,5},{7,6},{8,11},{9,8},{10,9... | collective-permute-start | bytes 1179656 | tf_op jit(solution)/shard_map/ppermute | solution.py:301
  107.5 14.4 %collective-permute-start.16 = (bf16[256,768]{1,0:T(8,128)(2,1)S(1)}, bf16[256,768]{1,0:T(8,128)(2,1)S(1)}, u32[]{:S(2)}, u32[]{:S(2)}) collective-permute-start(bf16[256,768]{1,0:T(8,128)(2,1)S(1)} %add.191), channel_id=1, source_target_pairs={{0,1},{1,2},{2,3},{3,0},{4,5},{5,6},{6,7},{7,4},{8,9},{9,10},{10,1... | collective-permute-start | bytes 1179656 | tf_op jit(solution)/shard_map/ppermute | solution.py:301
  (7 other events, 30.7 us)

commit v2 on v0

v2 whole, which is shorter than its diff:
```python
import functools

import jax
import jax.numpy as jnp
from jax import lax
from jax.experimental import pallas as pl
from jax.experimental.pallas import tpu as pltpu
from jax.sharding import PartitionSpec as P

BF16 = jnp.bfloat16
F32 = jnp.float32
HD = 128
TILE = 2 * HD
CHUNK = 256
LOG_ROWS = 16
MIB = 1024 * 1024

ANY = pl.BlockSpec(memory_space=pl.ANY)
HBM = pl.BlockSpec(memory_space=pltpu.HBM)


def dot(a, b):
    return jnp.dot(a, b, preferred_element_type=F32)


def exact_dot(a, b):
    return jnp.dot(a, b, preferred_element_type=F32, precision=lax.Precision.HIGHEST)


def silu(x):
    half = 0.5 * x
    return half + half * jnp.tanh(half)


def whole(x):
    return pl.BlockSpec(x.shape, lambda i: (0,) * len(x.shape))


def like(dtype, *shape):
    return jax.ShapeDtypeStruct(shape, dtype)


def call(kernel, name, args, outs, mib, flops, nbytes, scratch=(), big=(), big_outs=(), aliases=None, loose=()):
    args = [pltpu.with_memory_space_constraint(a, pltpu.HBM) if i in big else a for i, a in enumerate(args)]
    return pl.pallas_call(
        kernel,
        grid=(1,),
        in_specs=[HBM if i in big else ANY if i in loose else whole(a) for i, a in enumerate(args)],
        out_specs=[HBM if i in big_outs else whole(a) for i, a in enumerate(outs)],
        out_shape=[pltpu.HBM(a.shape, a.dtype) if i in big_outs else a for i, a in enumerate(outs)],
        scratch_shapes=list(scratch),
        input_output_aliases=aliases or {},
        compiler_params=pltpu.CompilerParams(vmem_limit_bytes=mib * MIB),
        cost_estimate=pl.CostEstimate(flops=int(flops), bytes_accessed=int(nbytes), transcendentals=0),
        name=name,
    )(*args)


class Copies:
    def __init__(self, sems):
        self.sems, self.used = sems, 0

    def start(self, src, dst):
        copy = pltpu.make_async_copy(src, dst, self.sems.at[self.used])
        self.used += 1
        copy.start()
        return copy


class Stages:
    def __init__(self, copies, groups, ahead=2):
        self.copies, self.groups, self.ahead = copies, groups, ahead
        self.running = []
        for _ in range(min(ahead, len(groups))):
            self.begin()

    def begin(self):
        if len(self.running) < len(self.groups):
            self.running.append([self.copies.start(*pair) for pair in self.groups[len(self.running)]])

    def take(self, i):
        for r in self.running[i]:
            r.wait()
        self.begin()


def tensor_at(shift):
    n = lax.axis_size("tensor")
    return lax.rem(lax.axis_index("tensor") + (shift + n), n)


def decay_kernel(ld, ldt, arow, acol, ek, ea, ends, shard):
    heads, rows = ld.shape
    r = lax.broadcasted_iota(jnp.int32, (CHUNK, CHUNK), 0)
    c = lax.broadcasted_iota(jnp.int32, (CHUNK, CHUNK), 1)
    lower = (c <= r).astype(F32)
    upper = (r <= c).astype(F32)
    total = jnp.zeros((1, heads), F32)
    for i in range(rows // CHUNK):
        sl = pl.ds(i * CHUNK, CHUNK)
        down = exact_dot(lower, ldt[sl, :])
        end = down[CHUNK - 1 : CHUNK, :]
        arow[:, sl] = exact_dot(ld[:, sl], upper)
        acol[sl, :] = down
        ek[sl, :] = jnp.exp(jnp.minimum(end - down, 0.0))
        ea[sl, :] = jnp.exp(jnp.minimum(down, 0.0))
        ends[i : i + 1, :] = jnp.exp(jnp.minimum(end, 0.0))
        total = total + end
    shard[...] = jnp.zeros_like(shard)
    shard[0:1, 0:heads] = jnp.minimum(total, 0.0)


def decays(log_decay):
    heads, rows = log_decay.shape
    outs = [like(F32, heads, rows)] + [like(F32, rows, heads)] * 3
    outs += [like(F32, rows // CHUNK, heads), like(F32, 1, HD)]
    return call(decay_kernel, "decays", (log_decay, log_decay.T), outs, 4, 0, 1e5)


def piece_rows(w, part, place, depth):
    shift, half = place
    row = pl.multiple_of((tensor_at(shift) * 2 + half) * depth, HD)
    return w.at[part, pl.ds(row, depth), :]


def near_kernel(parts, places, *refs):
    n = len(places)
    pieces, (w, total, x, wv, sems) = refs[:n], refs[n:]
    depth = pieces[0].shape[1]
    groups = []
    for p, part in enumerate(parts):
        for i in range(0, n, 2):
            groups.append(
                [
                    (piece_rows(w, part, places[m], depth), wv.at[p, pl.ds(m * depth, depth), :])
                    for m in (i, i + 1)
                ]
            )
    stages = Stages(Copies(sems), groups, 3)
    for m in range(n):
        x[:, m * depth : (m + 1) * depth] = pieces[m][...]
    for p in range(len(parts)):
        for i in range(n // 2):
            stages.take(p * (n // 2) + i)
            rows = pl.ds(2 * i * depth, 2 * depth)
            for j in range(total.shape[1]):
                term = dot(x[:, rows], wv[p, rows, pl.ds(j * TILE, TILE)])
                total[p, j] = total[p, j] + term if i else term


def near(parts, places, pieces, w):
    rows, depth = pieces[0].shape
    width = w.shape[2]
    n, n_parts = len(pieces), len(parts)
    return call(
        functools.partial(near_kernel, parts, places),
        "near",
        [*pieces, w],
        [like(F32, n_parts, width // TILE, rows, TILE)],
        36,
        2 * n * rows * depth * n_parts * width,
        n * depth * n_parts * width * 2 + rows * n_parts * width * 4,
        scratch=[
            pltpu.VMEM((rows, n * depth), BF16),
            pltpu.VMEM((n_parts, n * depth, width), BF16),
            pltpu.SemaphoreType.DMA((n_parts * n,)),
        ],
        big=(n,),
    )[0]


def log_rows(log):
    high = log.astype(BF16).astype(F32)
    middle = (log - high).astype(BF16).astype(F32)
    low = log - high - middle
    row = lax.broadcasted_iota(jnp.int32, (LOG_ROWS, HD), 0)
    rows = jnp.where(row == 0, high, jnp.where(row == 1, middle, low))
    return jnp.where(row < 3, rows, 0.0).astype(BF16)


def log_of(message):
    tail = message[pl.ds(message.shape[0] - LOG_ROWS, LOG_ROWS), :].astype(F32)
    return jnp.minimum(tail[0:1] + tail[1:2] + tail[2:3], 0.0)


def place_along_y(n_y, shift=0):
    return lax.rem(lax.axis_index("seq") + (shift + n_y), n_y)


def key_value_kernel(n_y, f0, f1, w, total, ek, ends, shard, k_out, v_out, s1_out, *refs):
    messages, (x, wv, scaled, sv, sems) = refs[:n_y], refs[n_y:]
    n_tiles, rows, _ = k_out.shape
    depth = f0.shape[1]
    row = pl.multiple_of(tensor_at(2) * 2 * depth, HD)
    groups = []
    for i in range(2):
        for j in range(0, n_tiles, 2):
            cols = pl.ds(j * TILE, 2 * TILE)
            groups.append([(w.at[i + 1, pl.ds(row, 2 * depth), cols], wv.at[i, :, cols])])
    stages = Stages(Copies(sems), groups, 3)
    for i, f in enumerate((f0, f1)):
        x[:, i * depth : (i + 1) * depth] = f[...]
    group = n_tiles * 2 // n_y
    for i, out in enumerate((k_out, v_out)):
        for j in range(n_tiles):
            if j % 2 == 0:
                stages.take((i * n_tiles + j) // 2)
            made = silu(total[i, j] + dot(x[...], wv[i, :, pl.ds(j * TILE, TILE)])).astype(BF16)
            out[j] = made
            if i == 0:
                for b in range(2):
                    key = made[:, b * HD : (b + 1) * HD].astype(F32)
                    scaled[j, :, pl.ds(b * HD, HD)] = (key * ek[:, 2 * j + b : 2 * j + b + 1]).astype(BF16)
                continue
            both = []
            for c in range(rows // CHUNK):
                sl = pl.ds(c * CHUNK, CHUNK)
                both.append(
                    lax.dot_general(
                        scaled[j, sl, :], out[j, sl, :], (((0,), (0,)), ((), ())), preferred_element_type=F32
                    )
                )
            for b in range(2):
                h = 2 * j + b
                one = slice(b * HD, (b + 1) * HD)
                sums = [m[one, one] for m in both]
                s1_out[pl.ds(h * HD, HD), :] = sums[0]
                sv[h // group, pl.ds(h % group * HD, HD), :] = (
                    sums[0] * ends[1:2, h : h + 1] + sums[1]
                ).astype(BF16)
    for p in range(n_y):
        log = shard[...] if p == 0 else pltpu.roll(shard[...], HD - p * group, 1)
        sv[p, pl.ds(group * HD, LOG_ROWS), :] = log_rows(log)
    for d in range(n_y):
        messages[d][...] = sv[place_along_y(n_y, d)]


def key_value(n_y, far, w, total, ek, ends, shard):
    _, n_tiles, rows, _ = total.shape
    width = w.shape[2]
    depth = far[0].shape[1]
    size = (width // n_y + LOG_ROWS, HD)
    tiles = like(BF16, n_tiles, rows, TILE)
    return call(
        functools.partial(key_value_kernel, n_y),
        "key_value",
        (*far, w, total, ek, ends, shard),
        [tiles, tiles, like(F32, width, HD)] + [like(BF16, *size)] * n_y,
        32,
        4 * rows * 2 * depth * width,
        8 * rows * width + 8 * depth * width,
        scratch=[
            pltpu.VMEM((rows, 2 * depth), BF16),
            pltpu.VMEM((2, 2 * depth, width), BF16),
            pltpu.VMEM((n_tiles, rows, TILE), BF16),
            pltpu.VMEM((n_y, *size), BF16),
            pltpu.SemaphoreType.DMA((n_tiles,)),
        ],
        big=(2,),
    )


def query_kernel(places, *refs):
    n = len(places)
    pieces, (w, total, q_out, x, wv, sems) = refs[:n], refs[n:]
    depth = pieces[0].shape[1]
    groups = [
        [(piece_rows(w, 0, places[m], depth), wv.at[pl.ds(m * depth, depth), :]) for m in (i, i + 1)]
        for i in range(0, n, 2)
    ]
    stages = Stages(Copies(sems), groups, n // 2)
    for m in range(n):
        x[:, m * depth : (m + 1) * depth] = pieces[m][...]
    for i in range(n // 2):
        stages.take(i)
    for j in range(q_out.shape[0]):
        q_out[j] = silu(total[0, j] + dot(x[...], wv[:, pl.ds(j * TILE, TILE)])).astype(BF16)


def query(places, pieces, w, total):
    _, n_tiles, rows, _ = total.shape
    width = w.shape[2]
    n = len(pieces)
    depth = pieces[0].shape[1]
    return call(
        functools.partial(query_kernel, places),
        "query",
        (*pieces, w, total),
        [like(BF16, n_tiles, rows, TILE)],
        24,
        2 * rows * n * depth * width,
        6 * rows * width + 2 * n * depth * width,
        scratch=[
            pltpu.VMEM((rows, n * depth), BF16),
            pltpu.VMEM((n * depth, width), BF16),
            pltpu.SemaphoreType.DMA((n,)),
        ],
        big=(n,),
    )[0]


def inner_kernel(q, k, v, acol, arow, ea, qs_out, o_out):
    n_tiles, rows, _ = q.shape
    t = lax.broadcasted_iota(jnp.int32, (CHUNK, CHUNK), 0)
    s = lax.broadcasted_iota(jnp.int32, (CHUNK, CHUNK), 1)
    causal = s <= t
    for j in range(n_tiles):
        for b in range(2):
            h = 2 * j + b
            one = pl.ds(b * HD, HD)
            for c in range(rows // CHUNK):
                sl = pl.ds(c * CHUNK, CHUNK)
                scores = lax.dot_general(
                    q[j, sl, one], k[j, sl, one], (((1,), (1,)), ((), ())), preferred_element_type=F32
                )
                spread = acol[sl, h : h + 1] - arow[h : h + 1, sl]
                weighted = jnp.where(causal, scores * jnp.exp(jnp.minimum(spread, 0.0)), 0.0)
                o_out[j, sl, one] = dot(weighted.astype(BF16), v[j, sl, one])
                qs_out[j, sl, one] = (q[j, sl, one].astype(F32) * ea[sl, h : h + 1]).astype(BF16)


def inner(q, k, v, acol, arow, ea):
    n_tiles, rows, _ = k.shape
    tiles = (n_tiles, rows, TILE)
    return call(
        inner_kernel,
        "inner",
        (q, k, v, acol, arow, ea),
        [like(BF16, *tiles), like(F32, *tiles)],
        24,
        4 * rows * CHUNK * n_tiles * TILE,
        14 * rows * n_tiles * TILE,
    )


def sum_logs(choose, logs):
    total = jnp.zeros_like(logs[0])
    for y, log in enumerate(logs):
        total = total + jnp.where(choose(y), log, 0.0)
    return total


def row_kernel(n_y, *refs):
    messages, out = refs[:n_y], refs[n_y + 1]
    at = [place_along_y(n_y, -d) for d in range(n_y)]
    logs = [log_of(m) for m in messages]
    weights = [jnp.exp(sum_logs(lambda e: at[e] > at[d], logs)) for d in range(n_y)]
    for h in range(out.shape[0] // HD):
        one = pl.ds(h * HD, HD)
        total = None
        for weight, m in zip(weights, messages):
            term = m[one, :].astype(F32) * weight[:, h : h + 1]
            total = term if total is None else total + term
        out[one, :] = total.astype(BF16)
    out[pl.ds(out.shape[0] - LOG_ROWS, LOG_ROWS), :] = log_rows(sum(logs[1:], logs[0]))


def row_sum(messages, after):
    size = messages[0].shape
    n = len(messages)
    return call(
        functools.partial(row_kernel, n),
        "row_sum",
        (*messages, after),
        [like(BF16, *size)],
        4,
        8 * size[0] * HD,
        16 * size[0] * HD,
        big=(n,),
    )[0]


def state_kernel(n_y, n_z, *refs):
    messages, earlier, outs = refs[:n_y], refs[n_y : n_y + n_z - 1], refs[n_y + n_z :]
    my_z = lax.axis_index("seq") // n_y
    at = [place_along_y(n_y, -d) for d in range(n_y)]
    logs = [log_of(m) for m in messages]
    gap = jnp.zeros_like(logs[0])
    from_rows = []
    for e in range(1, n_z):
        from_rows.append(jnp.where(e <= my_z, jnp.exp(gap), 0.0))
        gap = gap + log_of(earlier[e - 1])
    for d in range(n_y):
        there = place_along_y(n_y, d)
        start = jnp.exp(sum_logs(lambda e: at[e] < there, logs))
        weights = [
            jnp.where(at[s] < there, jnp.exp(sum_logs(lambda e: (at[e] > at[s]) & (at[e] < there), logs)), 0.0)
            for s in range(n_y)
        ]
        for h in range(outs[d].shape[0] // HD):
            one = pl.ds(h * HD, HD)
            state = jnp.zeros((HD, HD), F32)
            for weight, m in zip(from_rows, earlier):
                state = state + m[one, :].astype(F32) * (weight[:, h : h + 1] * start[:, h : h + 1])
            for weight, m in zip(weights, messages):
                state = state + m[one, :].astype(F32) * weight[:, h : h + 1]
            outs[d][one, :] = state.astype(BF16)


def states(messages, earlier, after):
    n_y, n_z = len(messages), len(earlier) + 1
    rows = messages[0].shape[0] - LOG_ROWS
    return call(
        functools.partial(state_kernel, n_y, n_z),
        "states",
        (*messages, *earlier, after),
        [like(BF16, rows, HD)] * n_y,
        4,
        64 * rows * HD,
        24 * rows * HD,
        big=(n_y + n_z - 1,),
    )


def out_weights(w, shift, slice_width):
    start = pl.multiple_of(tensor_at(shift) * slice_width, HD)
    return w.at[:, pl.ds(start, slice_width)]


def attend_kernel(n_y, qs, o, w, s1, ends, *refs):
    received, (attn, top, bot, wv, state, sem) = refs[:n_y], refs[n_y:]
    half, slice_width = top.shape
    n_tiles = qs.shape[0]
    fetch = pltpu.make_async_copy(out_weights(w, 2, slice_width), wv, sem)
    fetch.start()
    size = received[0].shape[0]
    for d in range(n_y):
        row = pl.multiple_of(place_along_y(n_y, -d) * size, HD)
        state[pl.ds(row, size), :] = received[d][...]
    for j in range(n_tiles):
        for b in range(2):
            h = 2 * j + b
            cols = pl.ds(h * HD, HD)
            one = pl.ds(b * HD, HD)
            first = state[cols, :]
            second = (first.astype(F32) * ends[0:1, h : h + 1] + s1[cols, :]).astype(BF16)
            for c, held in ((0, first), (1, second)):
                sl = pl.ds(c * CHUNK, CHUNK)
                out = o[j, sl, one] + dot(qs[j, sl, one], held)
                mean = jnp.mean(out * out, axis=1, keepdims=True)
                attn[sl, cols] = (out * lax.rsqrt(mean + 1e-6)).astype(BF16)
    fetch.wait()
    for j in range(slice_width // TILE):
        cols = pl.ds(j * TILE, TILE)
        out = dot(attn[...], wv[:, cols]).astype(BF16)
        top[:, cols] = out[:half]
        bot[:, cols] = out[half:]


def attend(n_y, qs, o, w_out, s1, ends, received, slice_width):
    n_tiles, rows, _ = qs.shape
    width = n_tiles * TILE
    half = rows // 2
    return call(
        functools.partial(attend_kernel, n_y),
        "attend",
        (qs, o, w_out, s1, ends, *received),
        [like(BF16, rows, width), like(BF16, half, slice_width), like(BF16, half, slice_width)],
        24,
        2 * rows * width * (HD + slice_width),
        rows * width * 8 + width * slice_width * 2,
        scratch=[
            pltpu.VMEM((width, slice_width), BF16),
            pltpu.VMEM((width, HD), BF16),
            pltpu.SemaphoreType.DMA,
        ],
        big=(2,),
    )


def output_kernel(attn, w, p_top, p_bot, m_top, m_bot, own, wv, sems):
    half, slice_width = p_top.shape
    copies = Copies(sems)
    fetches = [copies.start(out_weights(w, shift, slice_width), wv.at[i]) for i, shift in enumerate((1, -1, 0))]
    for i, outs in enumerate(((p_top, p_bot), (m_top, m_bot), (own,))):
        fetches[i].wait()
        for j in range(slice_width // TILE):
            cols = pl.ds(j * TILE, TILE)
            out = dot(attn[...], wv[i, :, cols]).astype(BF16)
            if len(outs) == 1:
                own[:, cols] = out
            else:
                outs[0][:, cols] = out[:half]
                outs[1][:, cols] = out[half:]


def output(attn, w_out, slice_width):
    rows, width = attn.shape
    half = rows // 2
    return call(
        output_kernel,
        "output",
        (attn, w_out),
        [like(BF16, half, slice_width)] * 4 + [like(BF16, rows, slice_width)],
        16,
        6 * rows * width * slice_width,
        6 * width * slice_width + 8 * rows * slice_width,
        scratch=[pltpu.VMEM((3, width, slice_width), BF16), pltpu.SemaphoreType.DMA((3,))],
        big=(1,),
    )


def finish_kernel(own, lt, lb, rt, rb, out):
    half = lt.shape[0]
    for i, (a, b) in enumerate(((lt, rt), (lb, rb))):
        sl = pl.ds(i * half, half)
        out[sl, :] = (own[sl, :].astype(F32) + a[...].astype(F32) + b[...].astype(F32)).astype(BF16)


def finish(*parts):
    own = parts[0]
    return call(finish_kernel, "finish", parts, [like(BF16, *own.shape)], 8, own.size * 2, own.size * 8)[0]


def body(n_y, tokens, w_qkv, log_decay, w_out):
    slice_width = tokens.shape[1]
    n_t = lax.axis_size("tensor")
    n_z = lax.axis_size("seq") // n_y

    def along_x(x, shift):
        return lax.ppermute(x, "tensor", [(i, (i + shift) % n_t) for i in range(n_t)])

    def along_y(x, shift):
        return lax.ppermute(
            x, "seq", [(z * n_y + y, z * n_y + (y + shift) % n_y) for z in range(n_z) for y in range(n_y)]
        )

    def along_z(x, shift):
        return lax.ppermute(
            x, "seq", [(z * n_y + y, (z + shift) % n_z * n_y + y) for z in range(n_z) for y in range(n_y)]
        )

    w = w_qkv.transpose(1, 0, 2)
    part = slice_width // 2
    t0, t1 = tokens[:, :part], tokens[:, part:]

    l0 = along_x(t0, 1)
    r1 = along_x(t1, -1)
    l1 = along_x(t1, 1)
    r0 = along_x(t0, -1)
    f0 = along_x(l0, 1)
    f1 = along_x(r1, -1)
    pieces = {(0, 0): t0, (0, 1): t1, (-1, 0): l0, (-1, 1): l1, (1, 0): r0, (1, 1): r1, (2, 0): f0, (2, 1): f1}

    def take(*places):
        return places, [pieces[p] for p in places], w

    arow, acol, ek, ea, ends, shard = decays(log_decay)
    q_total = near((0,), *take((0, 0), (0, 1), (-1, 0), (1, 1)))
    total = near((1, 2), *take((0, 0), (0, 1), (-1, 0), (1, 1), (-1, 1), (1, 0)))
    k, v, s1, *kvs = key_value(n_y, (f0, f1), w, total, ek, ends, shard)

    sums = [kvs[0]] + [along_y(kvs[d], d) for d in range(1, n_y)]
    q = query(*take((-1, 1), (1, 0), (2, 0), (2, 1)), q_total)
    row = row_sum(sums, q)
    earlier = [along_z(row, e) for e in range(1, n_z)]
    qs, o = inner(q, k, v, acol, arow, ea)
    starts = states(sums, earlier, qs)
    received = [starts[0]] + [along_y(starts[d], d) for d in range(1, n_y)]

    attn, far_top, far_bot = attend(n_y, qs, o, w_out, s1, ends, received, slice_width)
    relay_top = along_x(far_top, 1)
    relay_bot = along_x(far_bot, -1)
    p_top, p_bot, m_top, m_bot, own = output(attn, w_out, slice_width)
    left_bot = along_x(p_bot, 1)
    right_top = along_x(m_top, -1)
    left_top = along_x(p_top + relay_top, 1)
    right_bot = along_x(m_bot + relay_bot, -1)
    return finish(own, left_top, left_bot, right_top, right_bot)


def solution(mesh):
    in_specs = (
        P(("dp", "seq"), "tensor"),
        P(None, None, "tensor"),
        P("tensor", ("dp", "seq")),
        P("tensor", None),
    )
    out_specs = P(("dp", "seq"), "tensor")
    n_seq = mesh.shape["seq"]
    n_y = 4 if n_seq % 4 == 0 else 1
    return jax.shard_map(
        functools.partial(body, n_y), mesh=mesh, in_specs=in_specs, out_specs=out_specs, check_vma=False
    )
```

time: 186 us -> 97.1 us (0.52)
  blocking collectives: 41 us -> 0 us
  waiting for transfers between devices: 58.7 us -> 23.9 us
  matrix products: 34.3 us -> 0 us
  starting transfers between devices: 0.08 us -> 33.3 us
  Pallas kernels: 0 us -> 32 us
  local copies, waits for them, and re-layouts: 30 us -> 7.14 us
  between operations: 13.8 us -> 0.15 us
  other arithmetic: 6.08 us -> 0.19 us
    unnamed x1 -> x0, blocking collectives: 41 us -> none
    reduce_scatter x1 -> x0, waiting for transfers between devices: 37.8 us -> none  [body(): lax.psum_scatter(partial_terms.astype(jnp.bfloat16), 'tensor', scatter_di...]
    dot_general x5 -> x0, matrix products: 34.3 us -> none  [the longest x1 15.5 us: body(): jnp.dot(lax.all_gather(tokens, 'tensor', axis=1, tiled=True), weights, pr...]
    ppermute x0 -> x21, starting transfers between devices: none -> 33.3 us  [the longest x12 18.5 us: along_x(): lax.ppermute(x, 'tensor', [(i, (i + shift) % n_t) for i in range(n_t)])]
    pallas_call x0 -> x11, Pallas kernels: none -> 32 us  [call(): pl.pallas_call(kernel, grid=(1,), in_specs=[HBM if i in big else ANY if i...]
    ppermute x0 -> x21, waiting for transfers between devices: none -> 23.9 us  [the longest x12 19 us: along_x(): lax.ppermute(x, 'tensor', [(i, (i + shift) % n_t) for i in range(n_t)])]
    unnamed x10 -> x11, local copies, waits for them, and re-layouts: 27 us -> 5.94 us
    all_gather x2 -> x0, waiting for transfers between devices: 20.2 us -> none  [the longest x1 16.3 us: body(): lax.all_gather(tokens, 'tensor', axis=1, tiled=True)]
  transfers between devices with their start and end apart: 3 -> 21, of which waited for: 3 -> 11; matrix products, arithmetic and copies ran while one was open for 19% -> 1% of each run, Pallas kernels for 0% -> 22%
where the time goes in v2:
time: 97.1 us; the launch traced here: 96.6 us
  starting transfers between devices  33.3 us (34%)
  Pallas kernels  32 us (33%)
  waiting for transfers between devices  23.9 us (25%)
  local copies, waits for them, and re-layouts  7.14 us (7%)
    pallas_call x11, Pallas kernels, call(): pl.pallas_call(kernel, grid=(1,), in_specs=[HBM if i in big else ANY if i...  32 us
    ppermute x12, waiting for transfers between devices, along_x(): lax.ppermute(x, 'tensor', [(i, (i + shift) % n_t) for i in range(n_t)])  19 us
    ppermute x12, starting transfers between devices, along_x(): lax.ppermute(x, 'tensor', [(i, (i + shift) % n_t) for i in range(n_t)])  18.5 us
    ppermute x6, starting transfers between devices, along_y(): lax.ppermute(x, 'seq', [(z * n_y + y, z * n_y + (y + shift) % n_y) for z...  9.43 us
    unnamed x11, local copies, waits for them, and re-layouts  5.94 us
    ppermute x3, starting transfers between devices, along_z(): lax.ppermute(x, 'seq', [(z * n_y + y, (z + shift) % n_z * n_y + y) for z...  5.37 us
    ppermute x6, waiting for transfers between devices, along_y(): lax.ppermute(x, 'seq', [(z * n_y + y, z * n_y + (y + shift) % n_y) for z...  3.59 us
  transfers between devices with their start and end apart: 21, of which 11 were waited for; matrix products, arithmetic and copies ran while one was open for 1% of the time, Pallas kernels for 22%

profile of v2, /device:TPU:0, one launch (start us, length us, event | category | flops | bytes accessed | tf_op | source)
XLA Modules:
  0.0 96.6 jit_solution(12832530778027977807)
XLA Ops:
  1.2 1.6 %collective-permute-start.2 = (bf16[512,384]{1,0:T(8,128)(2,1)S(1)}, bf16[512,384]{1,0:T(8,128)(2,1)S(1)}, u32[]{:S(2)}, u32[]{:S(2)}) collective-permute-start(bf16[512,384]{1,0:T(8,128)(2,1)S(1)} %get-tuple-element.59.refs_0_), channel_id=1, source_target_pairs={{0,1},{1,2},{2,3},{3,0},{4,5},{5,6},{6,7},{7,4},{8,9},{9,10},{10,1... | collective-permute-start | bytes 1179656 | tf_op jit(solution)/shard_map/ppermute | solution.py:521
  2.8 1.7 %collective-permute-start.4 = (bf16[512,384]{1,0:T(8,128)(2,1)S(1)}, bf16[512,384]{1,0:T(8,128)(2,1)S(1)}, u32[]{:S(2)}, u32[]{:S(2)}) collective-permute-start(bf16[512,384]{1,0:T(8,128)(2,1)S(1)} %get-tuple-element.60.refs_1_), channel_id=1, source_target_pairs={{0,3},{1,0},{2,1},{3,2},{4,7},{5,4},{6,5},{7,6},{8,11},{9,8},{10,9... | collective-permute-start | bytes 1179656 | tf_op jit(solution)/shard_map/ppermute | solution.py:521
  4.5 1.6 %collective-permute-start.1 = (bf16[512,384]{1,0:T(8,128)(2,1)S(1)}, bf16[512,384]{1,0:T(8,128)(2,1)S(1)}, u32[]{:S(2)}, u32[]{:S(2)}) collective-permute-start(bf16[512,384]{1,0:T(8,128)(2,1)S(1)} %get-tuple-element.59.refs_0_), channel_id=1, source_target_pairs={{0,3},{1,0},{2,1},{3,2},{4,7},{5,4},{6,5},{7,6},{8,11},{9,8},{10,9... | collective-permute-start | bytes 1179656 | tf_op jit(solution)/shard_map/ppermute | solution.py:521
  8.9 5.6 %collective-permute-done.2.refs_2_ = bf16[512,384]{1,0:T(8,128)(2,1)S(1)} collective-permute-done((bf16[512,384]{1,0:T(8,128)(2,1)S(1)}, bf16[512,384]{1,0:T(8,128)(2,1)S(1)}, u32[]{:S(2)}, u32[]{:S(2)}) %collective-permute-start.2) | collective-permute-done | bytes 393248 | tf_op jit(solution)/shard_map/ppermute | solution.py:521
  14.9 2.9 %collective-permute-start.5 = (bf16[512,384]{1,0:T(8,128)(2,1)S(1)}, bf16[512,384]{1,0:T(8,128)(2,1)S(1)}, u32[]{:S(2)}, u32[]{:S(2)}) collective-permute-start(bf16[512,384]{1,0:T(8,128)(2,1)S(1)} %collective-permute-done.4.refs_3_), channel_id=1, source_target_pairs={{0,3},{1,0},{2,1},{3,2},{4,7},{5,4},{6,5},{7,6},{8,11},{9,8},{10,9... | collective-permute-start | bytes 1179656 | tf_op jit(solution)/shard_map/ppermute | solution.py:521
  17.8 3.3 %near.2.refs_5_ = f32[1,4,512,256]{3,2,1,0:T(8,128)S(1)} custom-call(bf16[512,384]{1,0:T(8,128)(2,1)S(1)} %get-tuple-element.59.refs_0_, bf16[512,384]{1,0:T(8,128)(2,1)S(1)} %get-tuple-element.60.refs_1_, bf16[512,384]{1,0:T(8,128)(2,1)S(1)} %collective-permute-done.2.refs_2_, bf16[512,384]{1,0:T(8,128)(2,1)S(1)} %collective-permute-done.4.refs_3_, ...), custom_call_target="tpu_custom_call" | custom-call | flops 1610612736 | bytes 5242880 | tf_op jit(solution)/shard_map/near/pallas_call | solution.py:45
  21.0 2.3 %collective-permute-done.1.refs_1_.refs_5_ = bf16[512,384]{1,0:T(8,128)(2,1)S(1)} collective-permute-done((bf16[512,384]{1,0:T(8,128)(2,1)S(1)}, bf16[512,384]{1,0:T(8,128)(2,1)S(1)}, u32[]{:S(2)}, u32[]{:S(2)}) %collective-permute-start.1) | collective-permute-done | bytes 393248 | tf_op jit(solution)/shard_map/ppermute | solution.py:521
  23.3 6.9 %near.3.total = f32[2,4,512,256]{3,2,1,0:T(8,128)S(1)} custom-call(bf16[512,384]{1,0:T(8,128)(2,1)S(1)} %get-tuple-element.59.refs_0_, bf16[512,384]{1,0:T(8,128)(2,1)S(1)} %get-tuple-element.60.refs_1_, bf16[512,384]{1,0:T(8,128)(2,1)S(1)} %collective-permute-done.2.refs_2_, bf16[512,384]{1,0:T(8,128)(2,1)S(1)} %collective-permute-done.4.refs_3_, ...), custom_call_target="tpu_custom_call" | custom-call | flops 4831838208 | bytes 13631488 | tf_op jit(solution)/shard_map/near/pallas_call | solution.py:45
  30.3 5.7 %key_value.1 = (bf16[4,512,256]{2,1,0:T(8,128)(2,1)S(1)}, bf16[4,512,256]{2,1,0:T(8,128)(2,1)S(1)}, f32[1024,128]{1,0:T(8,128)S(1)}, bf16[272,128]{1,0:T(8,128)(...) custom-call(bf16[512,384]{1,0:T(8,128)(2,1)S(1)} %collective-permute-done.3.refs_, ...), custom_call_target="tpu_custom_call" | custom-call | flops 1610612736 | bytes 7340032 | tf_op jit(solution)/shard_map/key_value/pallas_call | solution.py:45
  35.9 1.7 %collective-permute-start.6 = (bf16[272,128]{1,0:T(8,128)(2,1)S(1)}, bf16[272,128]{1,0:T(8,128)(2,1)S(1)}, u32[]{:S(2)}, u32[]{:S(2)}) collective-permute-start(bf16[272,128]{1,0:T(8,128)(2,1)S(1)} %get-tuple-element.44), channel_id=1, source_target_pairs={{0,4},{4,8},{8,12},{12,0},{16,20},{20,24},{24,28},{28,16},{32,36},... | collective-permute-start | bytes 208904 | tf_op jit(solution)/shard_map/ppermute | solution.py:524
  37.6 2.9 %collective-permute-start.7 = (bf16[272,128]{1,0:T(8,128)(2,1)S(1)}, bf16[272,128]{1,0:T(8,128)(2,1)S(1)}, u32[]{:S(2)}, u32[]{:S(2)}) collective-permute-start(bf16[272,128]{1,0:T(8,128)(2,1)S(1)} %get-tuple-element.45), channel_id=1, source_target_pairs={{0,8},{4,12},{8,0},{12,4},{16,24},{20,28},{24,16},{28,20},{32,40},... | collective-permute-start | bytes 208904 | tf_op jit(solution)/shard_map/ppermute | solution.py:524
  41.9 3.9 %query.1.q.refs_4_ = bf16[4,512,256]{2,1,0:T(8,128)(2,1)S(1)} custom-call(bf16[512,384]{1,0:T(8,128)(2,1)S(1)} %collective-permute-done.refs_0_.refs_4_, bf16[512,384]{1,0:T(8,128)(2,1)S(1)} %collective-permute-done.1.refs_1_.refs_5_, bf16[512,384]{1,0:T(8,128)(2,1)S(1)} %collective-permute-done.3.refs_2_.f0, ...), custom_call_target="tpu_custom_call" | custom-call | flops 1610612736 | bytes 6291456 | tf_op jit(solution)/shard_map/query/pallas_call | solution.py:45
  46.9 4.1 %collective-permute-start.11 = (bf16[272,128]{1,0:T(8,128)(2,1)S(1)}, bf16[272,128]{1,0:T(8,128)(2,1)S(1)}, u32[]{:S(2)}, u32[]{:S(2)}) collective-permute-start(bf16[272,128]{1,0:T(8,128)(2,1)S(1)} %row_sum.1), channel_id=1, source_target_pairs={{0,48},{4,52},{8,56},{12,60},{16,0},{20,4},{24,8},{28,12},{32,16},... | collective-permute-start | bytes 208904 | tf_op jit(solution)/shard_map/ppermute | solution.py:529
  53.5 1.6 %inner.1 = (bf16[4,512,256]{2,1,0:T(8,128)(2,1)S(1)}, f32[4,512,256]{2,1,0:T(8,128)S(1)}) custom-call(bf16[4,512,256]{2,1,0:T(8,128)(2,1)S(1)} %copy-done.1, bf16[4,512,256]{2,1,0:T(8,128)(2,1)S(1)} %get-tuple-element.35.k, bf16[4,512,256]{2,1,0:T(8,128)(2,1)S(1)} %get-tuple-element.36.v, f32[512,8]{1,0:T(8,128)S(1)} %get-tuple-element.37.acol, ...), custom_call_target="tpu_custom_call" | custom-call | flops 536870912 | bytes 7340032 | tf_op jit(solution)/shard_map/inner/pallas_call | solution.py:45
  58.5 1.4 %collective-permute-start.13 = (bf16[256,128]{1,0:T(8,128)(2,1)S(1)}, bf16[256,128]{1,0:T(8,128)(2,1)S(1)}, u32[]{:S(2)}, u32[]{:S(2)}) collective-permute-start(bf16[256,128]{1,0:T(8,128)(2,1)S(1)} %get-tuple-element.49), channel_id=1, source_target_pairs={{0,8},{4,12},{8,0},{12,4},{16,24},{20,28},{24,16},{28,20},{32,40},... | collective-permute-start | bytes 196616 | tf_op jit(solution)/shard_map/ppermute | solution.py:524
  61.3 2.0 %collective-permute-done.12.refs_1_ = bf16[256,128]{1,0:T(8,128)(2,1)S(1)} collective-permute-done((bf16[256,128]{1,0:T(8,128)(2,1)S(1)}, bf16[256,128]{1,0:T(8,128)(2,1)S(1)}, u32[]{:S(2)}, u32[]{:S(2)}) %collective-permute-start.12) | collective-permute-done | bytes 65568 | tf_op jit(solution)/shard_map/ppermute | solution.py:524
  66.1 3.1 %attend.1 = (bf16[512,1024]{1,0:T(8,128)(2,1)S(1)}, bf16[256,768]{1,0:T(8,128)(2,1)S(1)}, bf16[256,768]{1,0:T(8,128)(2,1)S(1)}) custom-call(bf16[4,512,256]{2,1,0:T(8,128)(2,1)S(1)} %copy-done.3, f32[4,512,256]{2,1,0:T(8,128)S(1)} %get-tuple-element.41.o, bf16[1024,3072]{1,0:T(8,128)(2,1)} %w.3, f32[1024,128]{1,0:T(8,128)S(1)} %get-tuple-element.42.s1, ...), custom_call_target="tpu_custom_call" | custom-call | flops 939524096 | bytes 5767168 | tf_op jit(solution)/shard_map/attend/pallas_call | solution.py:45
  69.2 1.6 %collective-permute-start.15 = (bf16[256,768]{1,0:T(8,128)(2,1)S(1)}, bf16[256,768]{1,0:T(8,128)(2,1)S(1)}, u32[]{:S(2)}, u32[]{:S(2)}) collective-permute-start(bf16[256,768]{1,0:T(8,128)(2,1)S(1)} %get-tuple-element.54), channel_id=1, source_target_pairs={{0,1},{1,2},{2,3},{3,0},{4,5},{5,6},{6,7},{7,4},{8,9},{9,10},{10,1... | collective-permute-start | bytes 1179656 | tf_op jit(solution)/shard_map/ppermute | solution.py:521
  70.8 1.7 %collective-permute-start.19 = (bf16[256,768]{1,0:T(8,128)(2,1)S(1)}, bf16[256,768]{1,0:T(8,128)(2,1)S(1)}, u32[]{:S(2)}, u32[]{:S(2)}) collective-permute-start(bf16[256,768]{1,0:T(8,128)(2,1)S(1)} %get-tuple-element.58), channel_id=1, source_target_pairs={{0,3},{1,0},{2,1},{3,2},{4,7},{5,4},{6,5},{7,6},{8,11},{9,8},{10,9... | collective-permute-start | bytes 1179656 | tf_op jit(solution)/shard_map/ppermute | solution.py:521
  72.5 4.9 %output.1 = (bf16[256,768]{1,0:T(8,128)(2,1)S(1)}, bf16[256,768]{1,0:T(8,128)(2,1)S(1)}, bf16[256,768]{1,0:T(8,128)(2,1)S(1)}, bf16[256,768]{1,0:T(8,128)(2,1)S(1)}, bf16[512,768]{1,0:T(8,128)(2,1)S(1)}) custom-call(bf16[512,1024]{1,0:T(8,128)(2,1)S(1)} %get-tuple-element.51.attn, bf16[1024,3072]{1,0:T(8,128)(2,1)} %w.3), custom_call_target="tpu_custom_call" | custom-call | flops 2415919104 | bytes 7864320 | tf_op jit(solution)/shard_map/output/pallas_call | solution.py:45
  77.8 3.0 %collective-permute-start.18 = (bf16[256,768]{1,0:T(8,128)(2,1)S(1)}, bf16[256,768]{1,0:T(8,128)(2,1)S(1)}, u32[]{:S(2)}, u32[]{:S(2)}) collective-permute-start(bf16[256,768]{1,0:T(8,128)(2,1)S(1)} %get-tuple-element.56), channel_id=1, source_target_pairs={{0,3},{1,0},{2,1},{3,2},{4,7},{5,4},{6,5},{7,6},{8,11},{9,8},{10,9... | collective-permute-start | bytes 1179656 | tf_op jit(solution)/shard_map/ppermute | solution.py:521
  82.4 2.0 %collective-permute-start.20 = (bf16[256,768]{1,0:T(8,128)(2,1)S(1)}, bf16[256,768]{1,0:T(8,128)(2,1)S(1)}, u32[]{:S(2)}, u32[]{:S(2)}) collective-permute-start(bf16[256,768]{1,0:T(8,128)(2,1)S(1)} %add.7), channel_id=1, source_target_pairs={{0,3},{1,0},{2,1},{3,2},{4,7},{5,4},{6,5},{7,6},{8,11},{9,8},{10,9... | collective-permute-start | bytes 1179656 | tf_op jit(solution)/shard_map/ppermute | solution.py:521
  84.3 6.5 %collective-permute-done.17.lb = bf16[256,768]{1,0:T(8,128)(2,1)S(1)} collective-permute-done((bf16[256,768]{1,0:T(8,128)(2,1)S(1)}, bf16[256,768]{1,0:T(8,128)(2,1)S(1)}, u32[]{:S(2)}, u32[]{:S(2)}) %collective-permute-start.17) | collective-permute-done | bytes 393248 | tf_op jit(solution)/shard_map/ppermute | solution.py:521
  90.8 4.3 %collective-permute-done.16.lt = bf16[256,768]{1,0:T(8,128)(2,1)S(1)} collective-permute-done((bf16[256,768]{1,0:T(8,128)(2,1)S(1)}, bf16[256,768]{1,0:T(8,128)(2,1)S(1)}, u32[]{:S(2)}, u32[]{:S(2)}) %collective-permute-start.16) | collective-permute-done | bytes 393248 | tf_op jit(solution)/shard_map/ppermute | solution.py:521
  (43 shorter events, 20.3 us)
Async XLA Ops:
  1.2 13.3 %collective-permute-start.2 = (bf16[512,384]{1,0:T(8,128)(2,1)S(1)}, bf16[512,384]{1,0:T(8,128)(2,1)S(1)}, u32[]{:S(2)}, u32[]{:S(2)}) collective-permute-start(bf16[512,384]{1,0:T(8,128)(2,1)S(1)} %get-tuple-element.59.refs_0_), channel_id=1, source_target_pairs={{0,1},{1,2},{2,3},{3,0},{4,5},{5,6},{6,7},{7,4},{8,9},{9,10},{10,1... | collective-permute-start | bytes 1179656 | tf_op jit(solution)/shard_map/ppermute | solution.py:521
  2.8 12.0 %collective-permute-start.4 = (bf16[512,384]{1,0:T(8,128)(2,1)S(1)}, bf16[512,384]{1,0:T(8,128)(2,1)S(1)}, u32[]{:S(2)}, u32[]{:S(2)}) collective-permute-start(bf16[512,384]{1,0:T(8,128)(2,1)S(1)} %get-tuple-element.60.refs_1_), channel_id=1, source_target_pairs={{0,3},{1,0},{2,1},{3,2},{4,7},{5,4},{6,5},{7,6},{8,11},{9,8},{10,9... | collective-permute-start | bytes 1179656 | tf_op jit(solution)/shard_map/ppermute | solution.py:521
  4.5 18.8 %collective-permute-start.1 = (bf16[512,384]{1,0:T(8,128)(2,1)S(1)}, bf16[512,384]{1,0:T(8,128)(2,1)S(1)}, u32[]{:S(2)}, u32[]{:S(2)}) collective-permute-start(bf16[512,384]{1,0:T(8,128)(2,1)S(1)} %get-tuple-element.59.refs_0_), channel_id=1, source_target_pairs={{0,3},{1,0},{2,1},{3,2},{4,7},{5,4},{6,5},{7,6},{8,11},{9,8},{10,9... | collective-permute-start | bytes 1179656 | tf_op jit(solution)/shard_map/ppermute | solution.py:521
  6.1 17.2 %collective-permute-start = (bf16[512,384]{1,0:T(8,128)(2,1)S(1)}, bf16[512,384]{1,0:T(8,128)(2,1)S(1)}, u32[]{:S(2)}, u32[]{:S(2)}) collective-permute-start(bf16[512,384]{1,0:T(8,128)(2,1)S(1)} %get-tuple-element.60.refs_1_), channel_id=1, source_target_pairs={{0,1},{1,2},{2,3},{3,0},{4,5},{5,6},{6,7},{7,4},{8,9},{9,10},{10,1... | collective-permute-start | bytes 1179656 | tf_op jit(solution)/shard_map/ppermute | solution.py:521
  14.5 15.8 %collective-permute-start.3 = (bf16[512,384]{1,0:T(8,128)(2,1)S(1)}, bf16[512,384]{1,0:T(8,128)(2,1)S(1)}, u32[]{:S(2)}, u32[]{:S(2)}) collective-permute-start(bf16[512,384]{1,0:T(8,128)(2,1)S(1)} %collective-permute-done.2.refs_2_), channel_id=1, source_target_pairs={{0,1},{1,2},{2,3},{3,0},{4,5},{5,6},{6,7},{7,4},{8,9},{9,10},{10,1... | collective-permute-start | bytes 1179656 | tf_op jit(solution)/shard_map/ppermute | solution.py:521
  14.9 15.4 %collective-permute-start.5 = (bf16[512,384]{1,0:T(8,128)(2,1)S(1)}, bf16[512,384]{1,0:T(8,128)(2,1)S(1)}, u32[]{:S(2)}, u32[]{:S(2)}) collective-permute-start(bf16[512,384]{1,0:T(8,128)(2,1)S(1)} %collective-permute-done.4.refs_3_), channel_id=1, source_target_pairs={{0,3},{1,0},{2,1},{3,2},{4,7},{5,4},{6,5},{7,6},{8,11},{9,8},{10,9... | collective-permute-start | bytes 1179656 | tf_op jit(solution)/shard_map/ppermute | solution.py:521
  35.9 10.8 %collective-permute-start.6 = (bf16[272,128]{1,0:T(8,128)(2,1)S(1)}, bf16[272,128]{1,0:T(8,128)(2,1)S(1)}, u32[]{:S(2)}, u32[]{:S(2)}) collective-permute-start(bf16[272,128]{1,0:T(8,128)(2,1)S(1)} %get-tuple-element.44), channel_id=1, source_target_pairs={{0,4},{4,8},{8,12},{12,0},{16,20},{20,24},{24,28},{28,16},{32,36},... | collective-permute-start | bytes 208904 | tf_op jit(solution)/shard_map/ppermute | solution.py:524
  37.6 9.1 %collective-permute-start.7 = (bf16[272,128]{1,0:T(8,128)(2,1)S(1)}, bf16[272,128]{1,0:T(8,128)(2,1)S(1)}, u32[]{:S(2)}, u32[]{:S(2)}) collective-permute-start(bf16[272,128]{1,0:T(8,128)(2,1)S(1)} %get-tuple-element.45), channel_id=1, source_target_pairs={{0,8},{4,12},{8,0},{12,4},{16,24},{20,28},{24,16},{28,20},{32,40},... | collective-permute-start | bytes 208904 | tf_op jit(solution)/shard_map/ppermute | solution.py:524
  40.5 6.2 %collective-permute-start.8 = (bf16[272,128]{1,0:T(8,128)(2,1)S(1)}, bf16[272,128]{1,0:T(8,128)(2,1)S(1)}, u32[]{:S(2)}, u32[]{:S(2)}) collective-permute-start(bf16[272,128]{1,0:T(8,128)(2,1)S(1)} %get-tuple-element.46), channel_id=1, source_target_pairs={{0,12},{4,0},{8,4},{12,8},{16,28},{20,16},{24,20},{28,24},{32,44},... | collective-permute-start | bytes 208904 | tf_op jit(solution)/shard_map/ppermute | solution.py:524
  45.7 1.0 %copy-start = (bf16[4,512,256]{2,1,0:T(8,128)(2,1)}, bf16[4,512,256]{2,1,0:T(8,128)(2,1)S(1)}, u32[]{:S(2)}) copy-start(bf16[4,512,256]{2,1,0:T(8,128)(2,1)S(1)} %query.1.q.refs_4_) | copy-start | bytes 3145732
  46.9 9.2 %collective-permute-start.11 = (bf16[272,128]{1,0:T(8,128)(2,1)S(1)}, bf16[272,128]{1,0:T(8,128)(2,1)S(1)}, u32[]{:S(2)}, u32[]{:S(2)}) collective-permute-start(bf16[272,128]{1,0:T(8,128)(2,1)S(1)} %row_sum.1), channel_id=1, source_target_pairs={{0,48},{4,52},{8,56},{12,60},{16,0},{20,4},{24,8},{28,12},{32,16},... | collective-permute-start | bytes 208904 | tf_op jit(solution)/shard_map/ppermute | solution.py:529
  51.0 5.9 %collective-permute-start.10 = (bf16[272,128]{1,0:T(8,128)(2,1)S(1)}, bf16[272,128]{1,0:T(8,128)(2,1)S(1)}, u32[]{:S(2)}, u32[]{:S(2)}) collective-permute-start(bf16[272,128]{1,0:T(8,128)(2,1)S(1)} %row_sum.1), channel_id=1, source_target_pairs={{0,32},{4,36},{8,40},{12,44},{16,48},{20,52},{24,56},{28,60},{32,0... | collective-permute-start | bytes 208904 | tf_op jit(solution)/shard_map/ppermute | solution.py:529
  51.0 6.3 %collective-permute-start.9 = (bf16[272,128]{1,0:T(8,128)(2,1)S(1)}, bf16[272,128]{1,0:T(8,128)(2,1)S(1)}, u32[]{:S(2)}, u32[]{:S(2)}) collective-permute-start(bf16[272,128]{1,0:T(8,128)(2,1)S(1)} %row_sum.1), channel_id=1, source_target_pairs={{0,16},{4,20},{8,24},{12,28},{16,32},{20,36},{24,40},{28,44},{32,4... | collective-permute-start | bytes 208904 | tf_op jit(solution)/shard_map/ppermute | solution.py:529
  52.3 1.2 %copy-start.1 = (bf16[4,512,256]{2,1,0:T(8,128)(2,1)S(1)}, bf16[4,512,256]{2,1,0:T(8,128)(2,1)}, u32[]{:S(2)}) copy-start(bf16[4,512,256]{2,1,0:T(8,128)(2,1)} %copy-done) | copy-start | bytes 3145732
  57.7 5.5 %collective-permute-start.12 = (bf16[256,128]{1,0:T(8,128)(2,1)S(1)}, bf16[256,128]{1,0:T(8,128)(2,1)S(1)}, u32[]{:S(2)}, u32[]{:S(2)}) collective-permute-start(bf16[256,128]{1,0:T(8,128)(2,1)S(1)} %get-tuple-element.48), channel_id=1, source_target_pairs={{0,4},{4,8},{8,12},{12,0},{16,20},{20,24},{24,28},{28,16},{32,36},... | collective-permute-start | bytes 196616 | tf_op jit(solution)/shard_map/ppermute | solution.py:524
  58.5 5.8 %collective-permute-start.13 = (bf16[256,128]{1,0:T(8,128)(2,1)S(1)}, bf16[256,128]{1,0:T(8,128)(2,1)S(1)}, u32[]{:S(2)}, u32[]{:S(2)}) collective-permute-start(bf16[256,128]{1,0:T(8,128)(2,1)S(1)} %get-tuple-element.49), channel_id=1, source_target_pairs={{0,8},{4,12},{8,0},{12,4},{16,24},{20,28},{24,16},{28,20},{32,40},... | collective-permute-start | bytes 196616 | tf_op jit(solution)/shard_map/ppermute | solution.py:524
  59.9 4.9 %collective-permute-start.14 = (bf16[256,128]{1,0:T(8,128)(2,1)S(1)}, bf16[256,128]{1,0:T(8,128)(2,1)S(1)}, u32[]{:S(2)}, u32[]{:S(2)}) collective-permute-start(bf16[256,128]{1,0:T(8,128)(2,1)S(1)} %get-tuple-element.50), channel_id=1, source_target_pairs={{0,12},{4,0},{8,4},{12,8},{16,28},{20,16},{24,20},{28,24},{32,44},... | collective-permute-start | bytes 196616 | tf_op jit(solution)/shard_map/ppermute | solution.py:524
  64.8 1.2 %copy-start.3 = (bf16[4,512,256]{2,1,0:T(8,128)(2,1)S(1)}, bf16[4,512,256]{2,1,0:T(8,128)(2,1)}, u32[]{:S(2)}) copy-start(bf16[4,512,256]{2,1,0:T(8,128)(2,1)} %copy-done.2) | copy-start | bytes 3145732
  69.2 11.6 %collective-permute-start.15 = (bf16[256,768]{1,0:T(8,128)(2,1)S(1)}, bf16[256,768]{1,0:T(8,128)(2,1)S(1)}, u32[]{:S(2)}, u32[]{:S(2)}) collective-permute-start(bf16[256,768]{1,0:T(8,128)(2,1)S(1)} %get-tuple-element.54), channel_id=1, source_target_pairs={{0,1},{1,2},{2,3},{3,0},{4,5},{5,6},{6,7},{7,4},{8,9},{9,10},{10,1... | collective-permute-start | bytes 1179656 | tf_op jit(solution)/shard_map/ppermute | solution.py:521
  70.8 11.5 %collective-permute-start.19 = (bf16[256,768]{1,0:T(8,128)(2,1)S(1)}, bf16[256,768]{1,0:T(8,128)(2,1)S(1)}, u32[]{:S(2)}, u32[]{:S(2)}) collective-permute-start(bf16[256,768]{1,0:T(8,128)(2,1)S(1)} %get-tuple-element.58), channel_id=1, source_target_pairs={{0,3},{1,0},{2,1},{3,2},{4,7},{5,4},{6,5},{7,6},{8,11},{9,8},{10,9... | collective-permute-start | bytes 1179656 | tf_op jit(solution)/shard_map/ppermute | solution.py:521
  77.4 13.3 %collective-permute-start.17 = (bf16[256,768]{1,0:T(8,128)(2,1)S(1)}, bf16[256,768]{1,0:T(8,128)(2,1)S(1)}, u32[]{:S(2)}, u32[]{:S(2)}) collective-permute-start(bf16[256,768]{1,0:T(8,128)(2,1)S(1)} %get-tuple-element.55), channel_id=1, source_target_pairs={{0,1},{1,2},{2,3},{3,0},{4,5},{5,6},{6,7},{7,4},{8,9},{9,10},{10,1... | collective-permute-start | bytes 1179656 | tf_op jit(solution)/shard_map/ppermute | solution.py:521
  77.8 13.0 %collective-permute-start.18 = (bf16[256,768]{1,0:T(8,128)(2,1)S(1)}, bf16[256,768]{1,0:T(8,128)(2,1)S(1)}, u32[]{:S(2)}, u32[]{:S(2)}) collective-permute-start(bf16[256,768]{1,0:T(8,128)(2,1)S(1)} %get-tuple-element.56), channel_id=1, source_target_pairs={{0,3},{1,0},{2,1},{3,2},{4,7},{5,4},{6,5},{7,6},{8,11},{9,8},{10,9... | collective-permute-start | bytes 1179656 | tf_op jit(solution)/shard_map/ppermute | solution.py:521
  80.9 14.3 %collective-permute-start.16 = (bf16[256,768]{1,0:T(8,128)(2,1)S(1)}, bf16[256,768]{1,0:T(8,128)(2,1)S(1)}, u32[]{:S(2)}, u32[]{:S(2)}) collective-permute-start(bf16[256,768]{1,0:T(8,128)(2,1)S(1)} %add.6), channel_id=1, source_target_pairs={{0,1},{1,2},{2,3},{3,0},{4,5},{5,6},{6,7},{7,4},{8,9},{9,10},{10,1... | collective-permute-start | bytes 1179656 | tf_op jit(solution)/shard_map/ppermute | solution.py:521
  82.4 13.0 %collective-permute-start.20 = (bf16[256,768]{1,0:T(8,128)(2,1)S(1)}, bf16[256,768]{1,0:T(8,128)(2,1)S(1)}, u32[]{:S(2)}, u32[]{:S(2)}) collective-permute-start(bf16[256,768]{1,0:T(8,128)(2,1)S(1)} %add.7), channel_id=1, source_target_pairs={{0,3},{1,0},{2,1},{3,2},{4,7},{5,4},{6,5},{7,6},{8,11},{9,8},{10,9... | collective-permute-start | bytes 1179656 | tf_op jit(solution)/shard_map/ppermute | solution.py:521
  (2 other events, 1.7 us)

commit v3 on v2

--- a/solution.py
+++ b/solution.py
@@ -54,6 +54,9 @@
         cost_estimate=pl.CostEstimate(flops=int(flops), bytes_accessed=int(nbytes), transcendentals=0),
         name=name,
     )(*args)
+
+
+MARK = like(F32, 8, HD)
 
 
 class Copies:
@@ -123,50 +126,58 @@
     return w.at[part, pl.ds(row, depth), :]
 
 
-def near_kernel(parts, places, *refs):
-    n = len(places)
-    pieces, (w, total, x, wv, sems) = refs[:n], refs[n:]
-    depth = pieces[0].shape[1]
-    groups = []
-    for p, part in enumerate(parts):
-        for i in range(0, n, 2):
-            groups.append(
-                [
-                    (piece_rows(w, part, places[m], depth), wv.at[p, pl.ds(m * depth, depth), :])
-                    for m in (i, i + 1)
-                ]
-            )
-    stages = Stages(Copies(sems), groups, 3)
-    for m in range(n):
-        x[:, m * depth : (m + 1) * depth] = pieces[m][...]
-    for p in range(len(parts)):
-        for i in range(n // 2):
-            stages.take(p * (n // 2) + i)
-            rows = pl.ds(2 * i * depth, 2 * depth)
-            for j in range(total.shape[1]):
-                term = dot(x[:, rows], wv[p, rows, pl.ds(j * TILE, TILE)])
-                total[p, j] = total[p, j] + term if i else term
-
-
-def near(parts, places, pieces, w):
-    rows, depth = pieces[0].shape
-    width = w.shape[2]
-    n, n_parts = len(pieces), len(parts)
-    return call(
-        functools.partial(near_kernel, parts, places),
+def near_kernel(places, ahead, has_before, has_weights, a, b, w, *refs):
+    refs = list(refs)
+    before = refs.pop(0) if has_before else None
+    held = refs.pop(0) if has_weights else None
+    total = refs.pop(0)
+    fetched = refs.pop(0) if ahead else None
+    x, *wv, sems = refs
+    depth = a.shape[1]
+    parts = w.shape[0]
+    copies = Copies(sems)
+
+    def rows_of(part, two, to):
+        return [(piece_rows(w, part, place, depth), to.at[part, pl.ds(m * depth, depth), :]) for m, place in enumerate(two)]
+
+    groups = [] if has_weights else [rows_of(p, places, wv[0]) for p in range(parts)]
+    if ahead:
+        groups += [rows_of(p, ahead, fetched) for p in range(parts)]
+    stages = Stages(copies, groups, 3)
+    x[:, :depth] = a[...]
+    x[:, depth:] = b[...]
+    for p in range(parts):
+        if not has_weights:
+            stages.take(p)
+        source = held if has_weights else wv[0]
+        for j in range(total.shape[1]):
+            term = dot(x[...], source[p, :, pl.ds(j * TILE, TILE)])
+            total[p, j] = before[p, j] + term if has_before else term
+    if ahead:
+        for p in range(parts):
+            stages.take(p if has_weights else parts + p)
+
+
+def near(places, two, w, before=None, held=None, ahead=None):
+    rows, depth = two[0].shape
+    parts, _, width = w.shape
+    outs = [like(F32, parts, width // TILE, rows, TILE)]
+    block = (parts, 2 * depth, width)
+    if ahead:
+        outs.append(like(BF16, *block))
+    return call(
+        functools.partial(near_kernel, places, ahead, before is not None, held is not None),
         "near",
-        [*pieces, w],
-        [like(F32, n_parts, width // TILE, rows, TILE)],
-        36,
-        2 * n * rows * depth * n_parts * width,
-        n * depth * n_parts * width * 2 + rows * n_parts * width * 4,
-        scratch=[
-            pltpu.VMEM((rows, n * depth), BF16),
-            pltpu.VMEM((n_parts, n * depth, width), BF16),
-            pltpu.SemaphoreType.DMA((n_parts * n,)),
-        ],
-        big=(n,),
-    )[0]
+        [*two, w] + [m for m in (before, held) if m is not None],
+        outs,
+        16,
+        4 * rows * depth * parts * width,
+        4 * depth * parts * width + rows * parts * width * 4,
+        scratch=[pltpu.VMEM((rows, 2 * depth), BF16)]
+        + ([] if held is not None else [pltpu.VMEM(block, BF16)])
+        + [pltpu.SemaphoreType.DMA((4 * parts,))],
+        big=(2,),
+    )
 
 
 def log_rows(log):
@@ -188,24 +199,15 @@
 
 
 def key_value_kernel(n_y, f0, f1, w, total, ek, ends, shard, k_out, v_out, s1_out, *refs):
-    messages, (x, wv, scaled, sv, sems) = refs[:n_y], refs[n_y:]
+    messages, (x, scaled, sv) = refs[:n_y], refs[n_y:]
     n_tiles, rows, _ = k_out.shape
     depth = f0.shape[1]
-    row = pl.multiple_of(tensor_at(2) * 2 * depth, HD)
-    groups = []
-    for i in range(2):
-        for j in range(0, n_tiles, 2):
-            cols = pl.ds(j * TILE, 2 * TILE)
-            groups.append([(w.at[i + 1, pl.ds(row, 2 * depth), cols], wv.at[i, :, cols])])
-    stages = Stages(Copies(sems), groups, 3)
     for i, f in enumerate((f0, f1)):
         x[:, i * depth : (i + 1) * depth] = f[...]
     group = n_tiles * 2 // n_y
     for i, out in enumerate((k_out, v_out)):
         for j in range(n_tiles):
-            if j % 2 == 0:
-                stages.take((i * n_tiles + j) // 2)
-            made = silu(total[i, j] + dot(x[...], wv[i, :, pl.ds(j * TILE, TILE)])).astype(BF16)
+            made = silu(total[i + 1, j] + dot(x[...], w[i + 1, :, pl.ds(j * TILE, TILE)])).astype(BF16)
             out[j] = made
             if i == 0:
                 for b in range(2):
@@ -246,60 +248,42 @@
         "key_value",
         (*far, w, total, ek, ends, shard),
         [tiles, tiles, like(F32, width, HD)] + [like(BF16, *size)] * n_y,
-        32,
+        16,
         4 * rows * 2 * depth * width,
         8 * rows * width + 8 * depth * width,
         scratch=[
             pltpu.VMEM((rows, 2 * depth), BF16),
-            pltpu.VMEM((2, 2 * depth, width), BF16),
             pltpu.VMEM((n_tiles, rows, TILE), BF16),
             pltpu.VMEM((n_y, *size), BF16),
-            pltpu.SemaphoreType.DMA((n_tiles,)),
         ],
-        big=(2,),
-    )
-
-
-def query_kernel(places, *refs):
-    n = len(places)
-    pieces, (w, total, q_out, x, wv, sems) = refs[:n], refs[n:]
-    depth = pieces[0].shape[1]
-    groups = [
-        [(piece_rows(w, 0, places[m], depth), wv.at[pl.ds(m * depth, depth), :]) for m in (i, i + 1)]
-        for i in range(0, n, 2)
-    ]
-    stages = Stages(Copies(sems), groups, n // 2)
-    for m in range(n):
-        x[:, m * depth : (m + 1) * depth] = pieces[m][...]
-    for i in range(n // 2):
-        stages.take(i)
+    )
+
+
+def query_kernel(f0, f1, w, total, q_out, x):
+    depth = f0.shape[1]
+    for i, f in enumerate((f0, f1)):
+        x[:, i * depth : (i + 1) * depth] = f[...]
     for j in range(q_out.shape[0]):
-        q_out[j] = silu(total[0, j] + dot(x[...], wv[:, pl.ds(j * TILE, TILE)])).astype(BF16)
-
-
-def query(places, pieces, w, total):
+        q_out[j] = silu(total[0, j] + dot(x[...], w[0, :, pl.ds(j * TILE, TILE)])).astype(BF16)
+
+
+def query(far, w, total):
     _, n_tiles, rows, _ = total.shape
-    width = w.shape[2]
-    n = len(pieces)
-    depth = pieces[0].shape[1]
-    return call(
-        functools.partial(query_kernel, places),
+    depth = 2 * far[0].shape[1]
+    return call(
+        query_kernel,
         "query",
-        (*pieces, w, total),
+        (*far, w, total),
         [like(BF16, n_tiles, rows, TILE)],
-        24,
-        2 * rows * n * depth * width,
-        6 * rows * width + 2 * n * depth * width,
-        scratch=[
-            pltpu.VMEM((rows, n * depth), BF16),
-            pltpu.VMEM((n * depth, width), BF16),
-            pltpu.SemaphoreType.DMA((n,)),
-        ],
-        big=(n,),
+        12,
+        2 * rows * depth * n_tiles * TILE,
+        6 * rows * n_tiles * TILE,
+        scratch=[pltpu.VMEM((rows, depth), BF16)],
     )[0]
 
 
-def inner_kernel(q, k, v, acol, arow, ea, qs_out, o_out):
+def inner_kernel(q, k, v, acol, arow, ea, qs_out, o_out, mark):
+    mark[...] = jnp.zeros_like(mark)
     n_tiles, rows, _ = q.shape
     t = lax.broadcasted_iota(jnp.int32, (CHUNK, CHUNK), 0)
     s = lax.broadcasted_iota(jnp.int32, (CHUNK, CHUNK), 1)
@@ -326,8 +310,8 @@
         inner_kernel,
         "inner",
         (q, k, v, acol, arow, ea),
-        [like(BF16, *tiles), like(F32, *tiles)],
-        24,
+        [like(BF16, *tiles), like(F32, *tiles), MARK],
+        16,
         4 * rows * CHUNK * n_tiles * TILE,
         14 * rows * n_tiles * TILE,
     )
@@ -341,7 +325,8 @@
 
 
 def row_kernel(n_y, *refs):
-    messages, out = refs[:n_y], refs[n_y + 1]
+    messages, (mark, out, done) = refs[:n_y], refs[n_y:]
+    done[...] = mark[...]
     at = [place_along_y(n_y, -d) for d in range(n_y)]
     logs = [log_of(m) for m in messages]
     weights = [jnp.exp(sum_logs(lambda e: at[e] > at[d], logs)) for d in range(n_y)]
@@ -362,12 +347,11 @@
         functools.partial(row_kernel, n),
         "row_sum",
         (*messages, after),
-        [like(BF16, *size)],
+        [like(BF16, *size), MARK],
         4,
         8 * size[0] * HD,
         16 * size[0] * HD,
-        big=(n,),
-    )[0]
+    )
 
 
 def state_kernel(n_y, n_z, *refs):
@@ -408,21 +392,40 @@
         4,
         64 * rows * HD,
         24 * rows * HD,
-        big=(n_y + n_z - 1,),
-    )
-
-
-def out_weights(w, shift, slice_width):
-    start = pl.multiple_of(tensor_at(shift) * slice_width, HD)
-    return w.at[:, pl.ds(start, slice_width)]
+    )
+
+
+def fetch_kernel(shifts, w, mark, out, done, sems):
+    copies = Copies(sems)
+    slice_width = out.shape[2]
+    reads = []
+    for i, shift in enumerate(shifts):
+        start = pl.multiple_of(tensor_at(shift) * slice_width, HD)
+        reads.append(copies.start(w.at[:, pl.ds(start, slice_width)], out.at[i]))
+    done[...] = mark[...]
+    for r in reads:
+        r.wait()
+
+
+def fetch_out(shifts, w_out, slice_width, after):
+    n = len(shifts)
+    return call(
+        functools.partial(fetch_kernel, shifts),
+        "fetch_out",
+        (w_out, after),
+        [like(BF16, n, w_out.shape[0], slice_width), MARK],
+        4,
+        0,
+        2 * w_out.size,
+        scratch=[pltpu.SemaphoreType.DMA((n,))],
+        big=(0,),
+    )
 
 
 def attend_kernel(n_y, qs, o, w, s1, ends, *refs):
-    received, (attn, top, bot, wv, state, sem) = refs[:n_y], refs[n_y:]
+    received, (attn, top, bot, state) = refs[:n_y], refs[n_y:]
     half, slice_width = top.shape
     n_tiles = qs.shape[0]
-    fetch = pltpu.make_async_copy(out_weights(w, 2, slice_width), wv, sem)
-    fetch.start()
     size = received[0].shape[0]
     for d in range(n_y):
         row = pl.multiple_of(place_along_y(n_y, -d) * size, HD)
@@ -439,10 +442,9 @@
                 out = o[j, sl, one] + dot(qs[j, sl, one], held)
                 mean = jnp.mean(out * out, axis=1, keepdims=True)
                 attn[sl, cols] = (out * lax.rsqrt(mean + 1e-6)).astype(BF16)
-    fetch.wait()
     for j in range(slice_width // TILE):
         cols = pl.ds(j * TILE, TILE)
-        out = dot(attn[...], wv[:, cols]).astype(BF16)
+        out = dot(attn[...], w[0, :, cols]).astype(BF16)
         top[:, cols] = out[:half]
         bot[:, cols] = out[half:]
 
@@ -456,27 +458,19 @@
         "attend",
         (qs, o, w_out, s1, ends, *received),
         [like(BF16, rows, width), like(BF16, half, slice_width), like(BF16, half, slice_width)],
-        24,
+        16,
         2 * rows * width * (HD + slice_width),
         rows * width * 8 + width * slice_width * 2,
-        scratch=[
-            pltpu.VMEM((width, slice_width), BF16),
-            pltpu.VMEM((width, HD), BF16),
-            pltpu.SemaphoreType.DMA,
-        ],
-        big=(2,),
-    )
-
-
-def output_kernel(attn, w, p_top, p_bot, m_top, m_bot, own, wv, sems):
+        scratch=[pltpu.VMEM((width, HD), BF16)],
+    )
+
+
+def output_kernel(attn, w, p_top, p_bot, m_top, m_bot, own):
     half, slice_width = p_top.shape
-    copies = Copies(sems)
-    fetches = [copies.start(out_weights(w, shift, slice_width), wv.at[i]) for i, shift in enumerate((1, -1, 0))]
     for i, outs in enumerate(((p_top, p_bot), (m_top, m_bot), (own,))):
-        fetches[i].wait()
         for j in range(slice_width // TILE):
             cols = pl.ds(j * TILE, TILE)
-            out = dot(attn[...], wv[i, :, cols]).astype(BF16)
+            out = dot(attn[...], w[i + 1, :, cols]).astype(BF16)
             if len(outs) == 1:
                 own[:, cols] = out
             else:
@@ -495,8 +489,6 @@
         16,
         6 * rows * width * slice_width,
         6 * width * slice_width + 8 * rows * slice_width,
-        scratch=[pltpu.VMEM((3, width, slice_width), BF16), pltpu.SemaphoreType.DMA((3,))],
-        big=(1,),
     )
 
 
@@ -540,28 +532,29 @@
     r0 = along_x(t0, -1)
     f0 = along_x(l0, 1)
     f1 = along_x(r1, -1)
-    pieces = {(0, 0): t0, (0, 1): t1, (-1, 0): l0, (-1, 1): l1, (1, 0): r0, (1, 1): r1, (2, 0): f0, (2, 1): f1}
-
-    def take(*places):
-        return places, [pieces[p] for p in places], w
 
     arow, acol, ek, ea, ends, shard = decays(log_decay)
-    q_total = near((0,), *take((0, 0), (0, 1), (-1, 0), (1, 1)))
-    total = near((1, 2), *take((0, 0), (0, 1), (-1, 0), (1, 1), (-1, 1), (1, 0)))
-    k, v, s1, *kvs = key_value(n_y, (f0, f1), w, total, ek, ends, shard)
+    far_places = ((2, 0), (2, 1))
+    side_places = ((-1, 1), (1, 0))
+    total = near(((0, 0), (0, 1)), (t0, t1), w)[0]
+    total, w_side = near(((-1, 0), (1, 1)), (l0, r1), w, total, ahead=side_places)
+    total, w_far = near(side_places, (l1, r0), w, total, w_side, ahead=far_places)
+    far = (f0, f1)
+    k, v, s1, *kvs = key_value(n_y, far, w_far, total, ek, ends, shard)
 
     sums = [kvs[0]] + [along_y(kvs[d], d) for d in range(1, n_y)]
-    q = query(*take((-1, 1), (1, 0), (2, 0), (2, 1)), q_total)
-    row = row_sum(sums, q)
+    q = query(far, w_far, total)
+    qs, o, mark = inner(q, k, v, acol, arow, ea)
+    row, mark = row_sum(sums, mark)
     earlier = [along_z(row, e) for e in range(1, n_z)]
-    qs, o = inner(q, k, v, acol, arow, ea)
-    starts = states(sums, earlier, qs)
+    w_slices, mark = fetch_out((2, 1, -1, 0), w_out, slice_width, mark)
+    starts = states(sums, earlier, mark)
     received = [starts[0]] + [along_y(starts[d], d) for d in range(1, n_y)]
 
-    attn, far_top, far_bot = attend(n_y, qs, o, w_out, s1, ends, received, slice_width)
+    attn, far_top, far_bot = attend(n_y, qs, o, w_slices, s1, ends, received, slice_width)
     relay_top = along_x(far_top, 1)
     relay_bot = along_x(far_bot, -1)
-    p_top, p_bot, m_top, m_bot, own = output(attn, w_out, slice_width)
+    p_top, p_bot, m_top, m_bot, own = output(attn, w_slices, slice_width)
     left_bot = along_x(p_bot, 1)
     right_top = along_x(m_top, -1)
     left_top = along_x(p_top + relay_top, 1)

time: 97.1 us -> 91.5 us (0.942)
  local copies, waits for them, and re-layouts: 7.14 us -> 2.75 us
  Pallas kernels: 32 us -> 28.4 us
  starting transfers between devices: 33.3 us -> 36.2 us
    unnamed x11 -> x3, local copies, waits for them, and re-layouts: 5.94 us -> 1.55 us
    pallas_call x11 -> x13, Pallas kernels: 32 us -> 28.4 us  [call(): pl.pallas_call(kernel, grid=(1,), in_specs=[HBM if i in big else ANY if i...]
    ppermute x12, starting transfers between devices: 18.5 us -> 20.1 us  [along_x(): lax.ppermute(x, 'tensor', [(i, (i + shift) % n_t) for i in range(n_t)])]
    ppermute x12, waiting for transfers between devices: 19 us -> 18 us  [along_x(): lax.ppermute(x, 'tensor', [(i, (i + shift) % n_t) for i in range(n_t)])]
  transfers between devices with their start and end apart: 21 -> 21, of which waited for: 11 -> 13; matrix products, arithmetic and copies ran while one was open for 1% -> 1% of each run, Pallas kernels for 22% -> 23%
where the time goes in v3:
time: 91.5 us; the launch traced here: 91.2 us
  starting transfers between devices  36.2 us (40%)
  Pallas kernels  28.4 us (31%)
  waiting for transfers between devices  23.6 us (26%)
  local copies, waits for them, and re-layouts  2.75 us (3%)
    pallas_call x13, Pallas kernels, call(): pl.pallas_call(kernel, grid=(1,), in_specs=[HBM if i in big else ANY if i...  28.4 us
    ppermute x12, starting transfers between devices, along_x(): lax.ppermute(x, 'tensor', [(i, (i + shift) % n_t) for i in range(n_t)])  20.1 us
    ppermute x12, waiting for transfers between devices, along_x(): lax.ppermute(x, 'tensor', [(i, (i + shift) % n_t) for i in range(n_t)])  18 us
    ppermute x6, starting transfers between devices, along_y(): lax.ppermute(x, 'seq', [(z * n_y + y, z * n_y + (y + shift) % n_y) for z...  10.1 us
    ppermute x3, starting transfers between devices, along_z(): lax.ppermute(x, 'seq', [(z * n_y + y, (z + shift) % n_z * n_y + y) for z...  5.98 us
    ppermute x6, waiting for transfers between devices, along_y(): lax.ppermute(x, 'seq', [(z * n_y + y, z * n_y + (y + shift) % n_y) for z...  4.27 us
  transfers between devices with their start and end apart: 21, of which 13 were waited for; matrix products, arithmetic and copies ran while one was open for 1% of the time, Pallas kernels for 23%

profile of v3, /device:TPU:0, one launch (start us, length us, event | category | flops | bytes accessed | tf_op | source)
XLA Modules:
  0.0 91.2 jit_solution(15532292877581283676)
XLA Ops:
  1.2 1.6 %collective-permute-start = (bf16[512,384]{1,0:T(8,128)(2,1)S(1)}, bf16[512,384]{1,0:T(8,128)(2,1)S(1)}, u32[]{:S(2)}, u32[]{:S(2)}) collective-permute-start(bf16[512,384]{1,0:T(8,128)(2,1)S(1)} %get-tuple-element.78.a), channel_id=1, source_target_pairs={{0,1},{1,2},{2,3},{3,0},{4,5},{5,6},{6,7},{7,4},{8,9},{9,10},{10,1... | collective-permute-start | bytes 1179656 | tf_op jit(solution)/shard_map/ppermute | solution.py:513
  2.8 1.7 %collective-permute-start.2 = (bf16[512,384]{1,0:T(8,128)(2,1)S(1)}, bf16[512,384]{1,0:T(8,128)(2,1)S(1)}, u32[]{:S(2)}, u32[]{:S(2)}) collective-permute-start(bf16[512,384]{1,0:T(8,128)(2,1)S(1)} %get-tuple-element.77.b), channel_id=1, source_target_pairs={{0,3},{1,0},{2,1},{3,2},{4,7},{5,4},{6,5},{7,6},{8,11},{9,8},{10,9... | collective-permute-start | bytes 1179656 | tf_op jit(solution)/shard_map/ppermute | solution.py:513
  4.9 2.9 %collective-permute-start.5 = (bf16[512,384]{1,0:T(8,128)(2,1)S(1)}, bf16[512,384]{1,0:T(8,128)(2,1)S(1)}, u32[]{:S(2)}, u32[]{:S(2)}) collective-permute-start(bf16[512,384]{1,0:T(8,128)(2,1)S(1)} %get-tuple-element.78.a), channel_id=1, source_target_pairs={{0,3},{1,0},{2,1},{3,2},{4,7},{5,4},{6,5},{7,6},{8,11},{9,8},{10,9... | collective-permute-start | bytes 1179656 | tf_op jit(solution)/shard_map/ppermute | solution.py:513
  10.1 4.5 %near.3.refs_0_ = f32[3,4,512,256]{3,2,1,0:T(8,128)S(1)} custom-call(bf16[512,384]{1,0:T(8,128)(2,1)S(1)} %get-tuple-element.78.a, bf16[512,384]{1,0:T(8,128)(2,1)S(1)} %get-tuple-element.77.b, bf16[3,3072,1024]{2,1,0:T(8,128)(2,1)} %bitcast.3), custom_call_target="tpu_custom_call" | custom-call | flops 2415919104 | bytes 11010048 | tf_op jit(solution)/shard_map/near/pallas_call | solution.py:45
  14.9 3.0 %collective-permute-start.3 = (bf16[512,384]{1,0:T(8,128)(2,1)S(1)}, bf16[512,384]{1,0:T(8,128)(2,1)S(1)}, u32[]{:S(2)}, u32[]{:S(2)}) collective-permute-start(bf16[512,384]{1,0:T(8,128)(2,1)S(1)} %collective-permute-done.2.b), channel_id=1, source_target_pairs={{0,3},{1,0},{2,1},{3,2},{4,7},{5,4},{6,5},{7,6},{8,11},{9,8},{10,9... | collective-permute-start | bytes 1179656 | tf_op jit(solution)/shard_map/ppermute | solution.py:513
  17.9 5.0 %near.4 = (f32[3,4,512,256]{3,2,1,0:T(8,128)S(1)}, bf16[3,768,1024]{2,1,0:T(8,128)(2,1)S(1)}) custom-call(bf16[512,384]{1,0:T(8,128)(2,1)S(1)} %collective-permute-done.a, bf16[512,384]{1,0:T(8,128)(2,1)S(1)} %collective-permute-done.2.b, bf16[3,3072,1024]{2,1,0:T(8,128)(2,1)} %bitcast.4, f32[3,4,512,256]{3,2,1,0:T(8,128)S(1)} %near.3.refs_0_), custom_call_target="tpu_custom_call" | custom-call | flops 2415919104 | bytes 11010048 | tf_op jit(solution)/shard_map/near/pallas_call | solution.py:45
  23.3 2.7 %near.5 = (f32[3,4,512,256]{3,2,1,0:T(8,128)S(1)}, bf16[3,768,1024]{2,1,0:T(8,128)(2,1)S(1)}) custom-call(bf16[512,384]{1,0:T(8,128)(2,1)S(1)} %collective-permute-done.4.a, bf16[512,384]{1,0:T(8,128)(2,1)S(1)} %collective-permute-done.5.b, bf16[3,3072,1024]{2,1,0:T(8,128)(2,1)} %bitcast.5, f32[3,4,512,256]{3,2,1,0:T(8,128)S(1)} %get-tuple-element.41.refs_0_, ...), custom_call_target="tpu_custom_call" | custom-call | flops 2415919104 | bytes 11010048 | tf_op jit(solution)/shard_map/near/pallas_call | solution.py:45
  26.1 4.0 %collective-permute-done.1.f0 = bf16[512,384]{1,0:T(8,128)(2,1)S(1)} collective-permute-done((bf16[512,384]{1,0:T(8,128)(2,1)S(1)}, bf16[512,384]{1,0:T(8,128)(2,1)S(1)}, u32[]{:S(2)}, u32[]{:S(2)}) %collective-permute-start.1) | collective-permute-done | bytes 393248 | tf_op jit(solution)/shard_map/ppermute | solution.py:513
  30.3 3.7 %key_value.1 = (bf16[4,512,256]{2,1,0:T(8,128)(2,1)S(1)}, bf16[4,512,256]{2,1,0:T(8,128)(2,1)S(1)}, f32[1024,128]{1,0:T(8,128)S(1)}, bf16[272,128]{1,0:T(8,128)(...) custom-call(bf16[512,384]{1,0:T(8,128)(2,1)S(1)} %collective-permute-done.1.f0, ...), custom_call_target="tpu_custom_call" | custom-call | flops 1610612736 | bytes 7340032 | tf_op jit(solution)/shard_map/key_value/pallas_call | solution.py:45
  34.0 1.6 %collective-permute-start.6 = (bf16[272,128]{1,0:T(8,128)(2,1)S(1)}, bf16[272,128]{1,0:T(8,128)(2,1)S(1)}, u32[]{:S(2)}, u32[]{:S(2)}) collective-permute-start(bf16[272,128]{1,0:T(8,128)(2,1)S(1)} %get-tuple-element.56), channel_id=1, source_target_pairs={{0,4},{4,8},{8,12},{12,0},{16,20},{20,24},{24,28},{28,16},{32,36},... | collective-permute-start | bytes 208904 | tf_op jit(solution)/shard_map/ppermute | solution.py:516
  35.6 2.9 %collective-permute-start.7 = (bf16[272,128]{1,0:T(8,128)(2,1)S(1)}, bf16[272,128]{1,0:T(8,128)(2,1)S(1)}, u32[]{:S(2)}, u32[]{:S(2)}) collective-permute-start(bf16[272,128]{1,0:T(8,128)(2,1)S(1)} %get-tuple-element.57), channel_id=1, source_target_pairs={{0,8},{4,12},{8,0},{12,4},{16,24},{20,28},{24,16},{28,20},{32,40},... | collective-permute-start | bytes 208904 | tf_op jit(solution)/shard_map/ppermute | solution.py:516
  41.1 1.6 %inner.1 = (bf16[4,512,256]{2,1,0:T(8,128)(2,1)S(1)}, f32[4,512,256]{2,1,0:T(8,128)S(1)}, f32[8,128]{1,0:T(8,128)S(1)}) custom-call(bf16[4,512,256]{2,1,0:T(8,128)(2,1)S(1)} %query.1.q, bf16[4,512,256]{2,1,0:T(8,128)(2,1)S(1)} %get-tuple-element.48.k, bf16[4,512,256]{2,1,0:T(8,128)(2,1)S(1)} %get-tuple-element.49.v, f32[512,8]{1,0:T(8,128)S(1)} %get-tuple-element.50.acol, ...), custom_call_target="tpu_custom_call" | custom-call | flops 536870912 | bytes 7340032 | tf_op jit(solution)/shard_map/inner/pallas_call | solution.py:45
  43.0 4.0 %collective-permute-start.10 = (bf16[272,128]{1,0:T(8,128)(2,1)S(1)}, bf16[272,128]{1,0:T(8,128)(2,1)S(1)}, u32[]{:S(2)}, u32[]{:S(2)}) collective-permute-start(bf16[272,128]{1,0:T(8,128)(2,1)S(1)} %get-tuple-element.63), channel_id=1, source_target_pairs={{0,32},{4,36},{8,40},{12,44},{16,48},{20,52},{24,56},{28,60},{32,0... | collective-permute-start | bytes 208904 | tf_op jit(solution)/shard_map/ppermute | solution.py:521
  49.0 2.9 %fetch_out.1 = (bf16[4,1024,768]{2,1,0:T(8,128)(2,1)S(1)}, f32[8,128]{1,0:T(8,128)S(1)}) custom-call(bf16[1024,3072]{1,0:T(8,128)(2,1)} %w.1, f32[8,128]{1,0:T(8,128)S(1)} %get-tuple-element.60.mark), custom_call_target="tpu_custom_call" | custom-call | bytes 6291456 | tf_op jit(solution)/shard_map/fetch_out/pallas_call | solution.py:45
  54.3 3.5 %collective-permute-start.13 = (bf16[256,128]{1,0:T(8,128)(2,1)S(1)}, bf16[256,128]{1,0:T(8,128)(2,1)S(1)}, u32[]{:S(2)}, u32[]{:S(2)}) collective-permute-start(bf16[256,128]{1,0:T(8,128)(2,1)S(1)} %get-tuple-element.67), channel_id=1, source_target_pairs={{0,8},{4,12},{8,0},{12,4},{16,24},{20,28},{24,16},{28,20},{32,40},... | collective-permute-start | bytes 196616 | tf_op jit(solution)/shard_map/ppermute | solution.py:516
  62.0 1.6 %attend.1 = (bf16[512,1024]{1,0:T(8,128)(2,1)S(1)}, bf16[256,768]{1,0:T(8,128)(2,1)S(1)}, bf16[256,768]{1,0:T(8,128)(2,1)S(1)}) custom-call(bf16[4,512,256]{2,1,0:T(8,128)(2,1)S(1)} %get-tuple-element.53.qs, f32[4,512,256]{2,1,0:T(8,128)S(1)} %get-tuple-element.54.o, bf16[4,1024,768]{2,1,0:T(8,128)(2,1)S(1)} %get-tuple-element.61.w, ...), custom_call_target="tpu_custom_call" | custom-call | flops 939524096 | bytes 5767168 | tf_op jit(solution)/shard_map/attend/pallas_call | solution.py:45
  63.7 3.0 %collective-permute-start.19 = (bf16[256,768]{1,0:T(8,128)(2,1)S(1)}, bf16[256,768]{1,0:T(8,128)(2,1)S(1)}, u32[]{:S(2)}, u32[]{:S(2)}) collective-permute-start(bf16[256,768]{1,0:T(8,128)(2,1)S(1)} %get-tuple-element.76), channel_id=1, source_target_pairs={{0,3},{1,0},{2,1},{3,2},{4,7},{5,4},{6,5},{7,6},{8,11},{9,8},{10,9... | collective-permute-start | bytes 1179656 | tf_op jit(solution)/shard_map/ppermute | solution.py:513
  66.7 2.6 %output.1 = (bf16[256,768]{1,0:T(8,128)(2,1)S(1)}, bf16[256,768]{1,0:T(8,128)(2,1)S(1)}, bf16[256,768]{1,0:T(8,128)(2,1)S(1)}, bf16[256,768]{1,0:T(8,128)(2,1)S(1)}, bf16[512,768]{1,0:T(8,128)(2,1)S(1)}) custom-call(bf16[512,1024]{1,0:T(8,128)(2,1)S(1)} %get-tuple-element.69.attn, bf16[4,1024,768]{2,1,0:T(8,128)(2,1)S(1)} %get-tuple-element.61.w), custom_call_target="tpu_custom_call" | custom-call | flops 2415919104 | bytes 7864320 | tf_op jit(solution)/shard_map/output/pallas_call | solution.py:45
  69.9 2.8 %collective-permute-start.18 = (bf16[256,768]{1,0:T(8,128)(2,1)S(1)}, bf16[256,768]{1,0:T(8,128)(2,1)S(1)}, u32[]{:S(2)}, u32[]{:S(2)}) collective-permute-start(bf16[256,768]{1,0:T(8,128)(2,1)S(1)} %get-tuple-element.74), channel_id=1, source_target_pairs={{0,3},{1,0},{2,1},{3,2},{4,7},{5,4},{6,5},{7,6},{8,11},{9,8},{10,9... | collective-permute-start | bytes 1179656 | tf_op jit(solution)/shard_map/ppermute | solution.py:513
  72.7 3.5 %collective-permute-done.19 = bf16[256,768]{1,0:T(8,128)(2,1)S(1)} collective-permute-done((bf16[256,768]{1,0:T(8,128)(2,1)S(1)}, bf16[256,768]{1,0:T(8,128)(2,1)S(1)}, u32[]{:S(2)}, u32[]{:S(2)}) %collective-permute-start.19) | collective-permute-done | bytes 393248 | tf_op jit(solution)/shard_map/ppermute | solution.py:513
  76.3 3.8 %collective-permute-start.20 = (bf16[256,768]{1,0:T(8,128)(2,1)S(1)}, bf16[256,768]{1,0:T(8,128)(2,1)S(1)}, u32[]{:S(2)}, u32[]{:S(2)}) collective-permute-start(bf16[256,768]{1,0:T(8,128)(2,1)S(1)} %add.7), channel_id=1, source_target_pairs={{0,3},{1,0},{2,1},{3,2},{4,7},{5,4},{6,5},{7,6},{8,11},{9,8},{10,9... | collective-permute-start | bytes 1179656 | tf_op jit(solution)/shard_map/ppermute | solution.py:513
  80.2 5.6 %collective-permute-done.17.lb = bf16[256,768]{1,0:T(8,128)(2,1)S(1)} collective-permute-done((bf16[256,768]{1,0:T(8,128)(2,1)S(1)}, bf16[256,768]{1,0:T(8,128)(2,1)S(1)}, u32[]{:S(2)}, u32[]{:S(2)}) %collective-permute-start.17) | collective-permute-done | bytes 393248 | tf_op jit(solution)/shard_map/ppermute | solution.py:513
  85.8 2.1 %collective-permute-done.20.rb = bf16[256,768]{1,0:T(8,128)(2,1)S(1)} collective-permute-done((bf16[256,768]{1,0:T(8,128)(2,1)S(1)}, bf16[256,768]{1,0:T(8,128)(2,1)S(1)}, u32[]{:S(2)}, u32[]{:S(2)}) %collective-permute-start.20) | collective-permute-done | bytes 393248 | tf_op jit(solution)/shard_map/ppermute | solution.py:513
  87.9 2.2 %collective-permute-done.16.lt = bf16[256,768]{1,0:T(8,128)(2,1)S(1)} collective-permute-done((bf16[256,768]{1,0:T(8,128)(2,1)S(1)}, bf16[256,768]{1,0:T(8,128)(2,1)S(1)}, u32[]{:S(2)}, u32[]{:S(2)}) %collective-permute-start.16) | collective-permute-done | bytes 393248 | tf_op jit(solution)/shard_map/ppermute | solution.py:513
  (37 shorter events, 18.4 us)
Async XLA Ops:
  1.2 13.4 %collective-permute-start = (bf16[512,384]{1,0:T(8,128)(2,1)S(1)}, bf16[512,384]{1,0:T(8,128)(2,1)S(1)}, u32[]{:S(2)}, u32[]{:S(2)}) collective-permute-start(bf16[512,384]{1,0:T(8,128)(2,1)S(1)} %get-tuple-element.78.a), channel_id=1, source_target_pairs={{0,1},{1,2},{2,3},{3,0},{4,5},{5,6},{6,7},{7,4},{8,9},{9,10},{10,1... | collective-permute-start | bytes 1179656 | tf_op jit(solution)/shard_map/ppermute | solution.py:513
  2.8 12.0 %collective-permute-start.2 = (bf16[512,384]{1,0:T(8,128)(2,1)S(1)}, bf16[512,384]{1,0:T(8,128)(2,1)S(1)}, u32[]{:S(2)}, u32[]{:S(2)}) collective-permute-start(bf16[512,384]{1,0:T(8,128)(2,1)S(1)} %get-tuple-element.77.b), channel_id=1, source_target_pairs={{0,3},{1,0},{2,1},{3,2},{4,7},{5,4},{6,5},{7,6},{8,11},{9,8},{10,9... | collective-permute-start | bytes 1179656 | tf_op jit(solution)/shard_map/ppermute | solution.py:513
  4.5 18.4 %collective-permute-start.4 = (bf16[512,384]{1,0:T(8,128)(2,1)S(1)}, bf16[512,384]{1,0:T(8,128)(2,1)S(1)}, u32[]{:S(2)}, u32[]{:S(2)}) collective-permute-start(bf16[512,384]{1,0:T(8,128)(2,1)S(1)} %get-tuple-element.77.b), channel_id=1, source_target_pairs={{0,1},{1,2},{2,3},{3,0},{4,5},{5,6},{6,7},{7,4},{8,9},{9,10},{10,1... | collective-permute-start | bytes 1179656 | tf_op jit(solution)/shard_map/ppermute | solution.py:513
  4.9 18.4 %collective-permute-start.5 = (bf16[512,384]{1,0:T(8,128)(2,1)S(1)}, bf16[512,384]{1,0:T(8,128)(2,1)S(1)}, u32[]{:S(2)}, u32[]{:S(2)}) collective-permute-start(bf16[512,384]{1,0:T(8,128)(2,1)S(1)} %get-tuple-element.78.a), channel_id=1, source_target_pairs={{0,3},{1,0},{2,1},{3,2},{4,7},{5,4},{6,5},{7,6},{8,11},{9,8},{10,9... | collective-permute-start | bytes 1179656 | tf_op jit(solution)/shard_map/ppermute | solution.py:513
  8.6 0.7 copy-start
  14.6 15.5 %collective-permute-start.1 = (bf16[512,384]{1,0:T(8,128)(2,1)S(1)}, bf16[512,384]{1,0:T(8,128)(2,1)S(1)}, u32[]{:S(2)}, u32[]{:S(2)}) collective-permute-start(bf16[512,384]{1,0:T(8,128)(2,1)S(1)} %collective-permute-done.a), channel_id=1, source_target_pairs={{0,1},{1,2},{2,3},{3,0},{4,5},{5,6},{6,7},{7,4},{8,9},{9,10},{10,1... | collective-permute-start | bytes 1179656 | tf_op jit(solution)/shard_map/ppermute | solution.py:513
  14.9 15.4 %collective-permute-start.3 = (bf16[512,384]{1,0:T(8,128)(2,1)S(1)}, bf16[512,384]{1,0:T(8,128)(2,1)S(1)}, u32[]{:S(2)}, u32[]{:S(2)}) collective-permute-start(bf16[512,384]{1,0:T(8,128)(2,1)S(1)} %collective-permute-done.2.b), channel_id=1, source_target_pairs={{0,3},{1,0},{2,1},{3,2},{4,7},{5,4},{6,5},{7,6},{8,11},{9,8},{10,9... | collective-permute-start | bytes 1179656 | tf_op jit(solution)/shard_map/ppermute | solution.py:513
  34.0 8.7 %collective-permute-start.6 = (bf16[272,128]{1,0:T(8,128)(2,1)S(1)}, bf16[272,128]{1,0:T(8,128)(2,1)S(1)}, u32[]{:S(2)}, u32[]{:S(2)}) collective-permute-start(bf16[272,128]{1,0:T(8,128)(2,1)S(1)} %get-tuple-element.56), channel_id=1, source_target_pairs={{0,4},{4,8},{8,12},{12,0},{16,20},{20,24},{24,28},{28,16},{32,36},... | collective-permute-start | bytes 208904 | tf_op jit(solution)/shard_map/ppermute | solution.py:516
  35.6 7.1 %collective-permute-start.7 = (bf16[272,128]{1,0:T(8,128)(2,1)S(1)}, bf16[272,128]{1,0:T(8,128)(2,1)S(1)}, u32[]{:S(2)}, u32[]{:S(2)}) collective-permute-start(bf16[272,128]{1,0:T(8,128)(2,1)S(1)} %get-tuple-element.57), channel_id=1, source_target_pairs={{0,8},{4,12},{8,0},{12,4},{16,24},{20,28},{24,16},{28,20},{32,40},... | collective-permute-start | bytes 208904 | tf_op jit(solution)/shard_map/ppermute | solution.py:516
  38.5 4.3 %collective-permute-start.8 = (bf16[272,128]{1,0:T(8,128)(2,1)S(1)}, bf16[272,128]{1,0:T(8,128)(2,1)S(1)}, u32[]{:S(2)}, u32[]{:S(2)}) collective-permute-start(bf16[272,128]{1,0:T(8,128)(2,1)S(1)} %get-tuple-element.58), channel_id=1, source_target_pairs={{0,12},{4,0},{8,4},{12,8},{16,28},{20,16},{24,20},{28,24},{32,44},... | collective-permute-start | bytes 208904 | tf_op jit(solution)/shard_map/ppermute | solution.py:516
  43.0 8.9 %collective-permute-start.10 = (bf16[272,128]{1,0:T(8,128)(2,1)S(1)}, bf16[272,128]{1,0:T(8,128)(2,1)S(1)}, u32[]{:S(2)}, u32[]{:S(2)}) collective-permute-start(bf16[272,128]{1,0:T(8,128)(2,1)S(1)} %get-tuple-element.63), channel_id=1, source_target_pairs={{0,32},{4,36},{8,40},{12,44},{16,48},{20,52},{24,56},{28,60},{32,0... | collective-permute-start | bytes 208904 | tf_op jit(solution)/shard_map/ppermute | solution.py:521
  47.0 4.9 %collective-permute-start.11 = (bf16[272,128]{1,0:T(8,128)(2,1)S(1)}, bf16[272,128]{1,0:T(8,128)(2,1)S(1)}, u32[]{:S(2)}, u32[]{:S(2)}) collective-permute-start(bf16[272,128]{1,0:T(8,128)(2,1)S(1)} %get-tuple-element.63), channel_id=1, source_target_pairs={{0,48},{4,52},{8,56},{12,60},{16,0},{20,4},{24,8},{28,12},{32,16},... | collective-permute-start | bytes 208904 | tf_op jit(solution)/shard_map/ppermute | solution.py:521
  47.7 5.5 %collective-permute-start.9 = (bf16[272,128]{1,0:T(8,128)(2,1)S(1)}, bf16[272,128]{1,0:T(8,128)(2,1)S(1)}, u32[]{:S(2)}, u32[]{:S(2)}) collective-permute-start(bf16[272,128]{1,0:T(8,128)(2,1)S(1)} %get-tuple-element.63), channel_id=1, source_target_pairs={{0,16},{4,20},{8,24},{12,28},{16,32},{20,36},{24,40},{28,44},{32,4... | collective-permute-start | bytes 208904 | tf_op jit(solution)/shard_map/ppermute | solution.py:521
  53.7 5.5 %collective-permute-start.12 = (bf16[256,128]{1,0:T(8,128)(2,1)S(1)}, bf16[256,128]{1,0:T(8,128)(2,1)S(1)}, u32[]{:S(2)}, u32[]{:S(2)}) collective-permute-start(bf16[256,128]{1,0:T(8,128)(2,1)S(1)} %get-tuple-element.66), channel_id=1, source_target_pairs={{0,4},{4,8},{8,12},{12,0},{16,20},{20,24},{24,28},{28,16},{32,36},... | collective-permute-start | bytes 196616 | tf_op jit(solution)/shard_map/ppermute | solution.py:516
  54.3 6.4 %collective-permute-start.13 = (bf16[256,128]{1,0:T(8,128)(2,1)S(1)}, bf16[256,128]{1,0:T(8,128)(2,1)S(1)}, u32[]{:S(2)}, u32[]{:S(2)}) collective-permute-start(bf16[256,128]{1,0:T(8,128)(2,1)S(1)} %get-tuple-element.67), channel_id=1, source_target_pairs={{0,8},{4,12},{8,0},{12,4},{16,24},{20,28},{24,16},{28,20},{32,40},... | collective-permute-start | bytes 196616 | tf_op jit(solution)/shard_map/ppermute | solution.py:516
  57.7 4.3 %collective-permute-start.14 = (bf16[256,128]{1,0:T(8,128)(2,1)S(1)}, bf16[256,128]{1,0:T(8,128)(2,1)S(1)}, u32[]{:S(2)}, u32[]{:S(2)}) collective-permute-start(bf16[256,128]{1,0:T(8,128)(2,1)S(1)} %get-tuple-element.68), channel_id=1, source_target_pairs={{0,12},{4,0},{8,4},{12,8},{16,28},{20,16},{24,20},{28,24},{32,44},... | collective-permute-start | bytes 196616 | tf_op jit(solution)/shard_map/ppermute | solution.py:516
  63.7 12.5 %collective-permute-start.19 = (bf16[256,768]{1,0:T(8,128)(2,1)S(1)}, bf16[256,768]{1,0:T(8,128)(2,1)S(1)}, u32[]{:S(2)}, u32[]{:S(2)}) collective-permute-start(bf16[256,768]{1,0:T(8,128)(2,1)S(1)} %get-tuple-element.76), channel_id=1, source_target_pairs={{0,3},{1,0},{2,1},{3,2},{4,7},{5,4},{6,5},{7,6},{8,11},{9,8},{10,9... | collective-permute-start | bytes 1179656 | tf_op jit(solution)/shard_map/ppermute | solution.py:513
  66.7 13.4 %collective-permute-start.15 = (bf16[256,768]{1,0:T(8,128)(2,1)S(1)}, bf16[256,768]{1,0:T(8,128)(2,1)S(1)}, u32[]{:S(2)}, u32[]{:S(2)}) collective-permute-start(bf16[256,768]{1,0:T(8,128)(2,1)S(1)} %get-tuple-element.72), channel_id=1, source_target_pairs={{0,1},{1,2},{2,3},{3,0},{4,5},{5,6},{6,7},{7,4},{8,9},{9,10},{10,1... | collective-permute-start | bytes 1179656 | tf_op jit(solution)/shard_map/ppermute | solution.py:513
  69.3 16.5 %collective-permute-start.17 = (bf16[256,768]{1,0:T(8,128)(2,1)S(1)}, bf16[256,768]{1,0:T(8,128)(2,1)S(1)}, u32[]{:S(2)}, u32[]{:S(2)}) collective-permute-start(bf16[256,768]{1,0:T(8,128)(2,1)S(1)} %get-tuple-element.73), channel_id=1, source_target_pairs={{0,1},{1,2},{2,3},{3,0},{4,5},{5,6},{6,7},{7,4},{8,9},{9,10},{10,1... | collective-permute-start | bytes 1179656 | tf_op jit(solution)/shard_map/ppermute | solution.py:513
  69.9 15.9 %collective-permute-start.18 = (bf16[256,768]{1,0:T(8,128)(2,1)S(1)}, bf16[256,768]{1,0:T(8,128)(2,1)S(1)}, u32[]{:S(2)}, u32[]{:S(2)}) collective-permute-start(bf16[256,768]{1,0:T(8,128)(2,1)S(1)} %get-tuple-element.74), channel_id=1, source_target_pairs={{0,3},{1,0},{2,1},{3,2},{4,7},{5,4},{6,5},{7,6},{8,11},{9,8},{10,9... | collective-permute-start | bytes 1179656 | tf_op jit(solution)/shard_map/ppermute | solution.py:513
  76.3 11.6 %collective-permute-start.20 = (bf16[256,768]{1,0:T(8,128)(2,1)S(1)}, bf16[256,768]{1,0:T(8,128)(2,1)S(1)}, u32[]{:S(2)}, u32[]{:S(2)}) collective-permute-start(bf16[256,768]{1,0:T(8,128)(2,1)S(1)} %add.7), channel_id=1, source_target_pairs={{0,3},{1,0},{2,1},{3,2},{4,7},{5,4},{6,5},{7,6},{8,11},{9,8},{10,9... | collective-permute-start | bytes 1179656 | tf_op jit(solution)/shard_map/ppermute | solution.py:513
  80.1 9.9 %collective-permute-start.16 = (bf16[256,768]{1,0:T(8,128)(2,1)S(1)}, bf16[256,768]{1,0:T(8,128)(2,1)S(1)}, u32[]{:S(2)}, u32[]{:S(2)}) collective-permute-start(bf16[256,768]{1,0:T(8,128)(2,1)S(1)} %add.6), channel_id=1, source_target_pairs={{0,1},{1,2},{2,3},{3,0},{4,5},{5,6},{6,7},{7,4},{8,9},{9,10},{10,1... | collective-permute-start | bytes 1179656 | tf_op jit(solution)/shard_map/ppermute | solution.py:513

commit v4 on v3

--- a/solution.py
+++ b/solution.py
@@ -180,6 +180,103 @@
     )
 
 
+def split_kernel(tokens, w, t0, t1, early, x, wv, tv, sems):
+    depth = t0.shape[1]
+    parts = w.shape[0]
+    copies = Copies(sems)
+    reads = [copies.start(tokens.at[:, pl.ds(m * depth, depth)], t) for m, t in enumerate((t0, t1))]
+    first = lax.axis_index("dp") == 0
+    later = Copies(sems.at[pl.ds(2, parts + parts * tv.shape[1])])
+
+    @pl.when(first)
+    def _():
+        row = pl.multiple_of(tensor_at(0) * 2 * depth, HD)
+        fetches = [later.start(w.at[p, pl.ds(row, 2 * depth), :], wv.at[p]) for p in range(parts)]
+        for r in reads:
+            r.wait()
+        x[:, :depth] = t0[...]
+        x[:, depth:] = t1[...]
+        writes = []
+        for p in range(parts):
+            fetches[p].wait()
+            for j in range(tv.shape[1]):
+                tv[p, j] = dot(x[...], wv[p, :, pl.ds(j * TILE, TILE)])
+                writes.append(later.start(tv.at[p, j], early.at[p, j]))
+        for r in writes:
+            r.wait()
+
+    @pl.when(jnp.logical_not(first))
+    def _():
+        for r in reads:
+            r.wait()
+
+
+def split(tokens, w):
+    rows, width = tokens.shape
+    parts, _, columns = w.shape
+    block = (parts, columns // TILE, rows, TILE)
+    return call(
+        split_kernel,
+        "split",
+        (tokens, w),
+        [like(BF16, rows, width // 2)] * 2 + [like(F32, *block)],
+        16,
+        2 * rows * width * parts * columns,
+        2 * width * parts * columns,
+        scratch=[
+            pltpu.VMEM((rows, width), BF16),
+            pltpu.VMEM((parts, width, columns), BF16),
+            pltpu.VMEM(block, F32),
+            pltpu.SemaphoreType.DMA((2 + parts + parts * block[1],)),
+        ],
+        big=range(2),
+        big_outs=(2,),
+    )
+
+
+def own_kernel(t0, t1, w, early, total, x, wv, sems):
+    depth = t0.shape[1]
+    parts = w.shape[0]
+    copies = Copies(sems)
+    first = lax.axis_index("dp") == 0
+
+    @pl.when(first)
+    def _():
+        copy = copies.start(early, total)
+        copy.wait()
+
+    @pl.when(jnp.logical_not(first))
+    def _():
+        row = pl.multiple_of(tensor_at(0) * 2 * depth, HD)
+        fetches = [copies.start(w.at[p, pl.ds(row, 2 * depth), :], wv.at[p]) for p in range(parts)]
+        x[:, :depth] = t0[...]
+        x[:, depth:] = t1[...]
+        for p in range(parts):
+            fetches[p].wait()
+            for j in range(total.shape[1]):
+                total[p, j] = dot(x[...], wv[p, :, pl.ds(j * TILE, TILE)])
+
+
+def own_products(t0, t1, w, early):
+    rows, depth = t0.shape
+    parts, _, columns = w.shape
+    return call(
+        own_kernel,
+        "own",
+        (t0, t1, w, early),
+        [like(F32, *early.shape)],
+        16,
+        4 * rows * depth * parts * columns,
+        4 * depth * parts * columns,
+        scratch=[
+            pltpu.VMEM((rows, 2 * depth), BF16),
+            pltpu.VMEM((parts, 2 * depth, columns), BF16),
+            pltpu.SemaphoreType.DMA((parts + 1,)),
+        ],
+        big=(2, 3),
+    )[0]
+
+
 def log_rows(log):
     high = log.astype(BF16).astype(F32)
     middle = (log - high).astype(BF16).astype(F32)
@@ -194,11 +291,15 @@
     return jnp.minimum(tail[0:1] + tail[1:2] + tail[2:3], 0.0)
 
 
+def send_order(n):
+    return range(n - 1, 0, -1)
+
+
 def place_along_y(n_y, shift=0):
     return lax.rem(lax.axis_index("seq") + (shift + n_y), n_y)
 
 
-def key_value_kernel(n_y, f0, f1, w, total, ek, ends, shard, k_out, v_out, s1_out, *refs):
+def key_value_kernel(n_y, f0, f1, w, total, ek, ends, shard, mark, k_out, v_out, s1_out, *refs):
     messages, (x, scaled, sv) = refs[:n_y], refs[n_y:]
     n_tiles, rows, _ = k_out.shape
     depth = f0.shape[1]
@@ -237,7 +338,7 @@
         messages[d][...] = sv[place_along_y(n_y, d)]
 
 
-def key_value(n_y, far, w, total, ek, ends, shard):
+def key_value(n_y, far, w, total, ek, ends, shard, after):
     _, n_tiles, rows, _ = total.shape
     width = w.shape[2]
     depth = far[0].shape[1]
@@ -246,7 +347,7 @@
     return call(
         functools.partial(key_value_kernel, n_y),
         "key_value",
-        (*far, w, total, ek, ends, shard),
+        (*far, w, total, ek, ends, shard, after),
         [tiles, tiles, like(F32, width, HD)] + [like(BF16, *size)] * n_y,
         16,
         4 * rows * 2 * depth * width,
@@ -327,7 +428,7 @@
 def row_kernel(n_y, *refs):
     messages, (mark, out, done) = refs[:n_y], refs[n_y:]
     done[...] = mark[...]
-    at = [place_along_y(n_y, -d) for d in range(n_y)]
+    at = [place_along_y(n_y, -d) for d in (0, *send_order(n_y))]
     logs = [log_of(m) for m in messages]
     weights = [jnp.exp(sum_logs(lambda e: at[e] > at[d], logs)) for d in range(n_y)]
     for h in range(out.shape[0] // HD):
@@ -357,10 +458,11 @@
 def state_kernel(n_y, n_z, *refs):
     messages, earlier, outs = refs[:n_y], refs[n_y : n_y + n_z - 1], refs[n_y + n_z :]
     my_z = lax.axis_index("seq") // n_y
-    at = [place_along_y(n_y, -d) for d in range(n_y)]
+    at = [place_along_y(n_y, -d) for d in (0, *send_order(n_y))]
     logs = [log_of(m) for m in messages]
     gap = jnp.zeros_like(logs[0])
     from_rows = []
+    earlier = earlier[::-1]
     for e in range(1, n_z):
         from_rows.append(jnp.where(e <= my_z, jnp.exp(gap), 0.0))
         gap = gap + log_of(earlier[e - 1])
@@ -395,14 +497,14 @@
     )
 
 
-def fetch_kernel(shifts, w, mark, out, done, sems):
+def fetch_kernel(shifts, w, after, out, done, sems):
     copies = Copies(sems)
     slice_width = out.shape[2]
     reads = []
     for i, shift in enumerate(shifts):
         start = pl.multiple_of(tensor_at(shift) * slice_width, HD)
         reads.append(copies.start(w.at[:, pl.ds(start, slice_width)], out.at[i]))
-    done[...] = mark[...]
+    done[...] = jnp.zeros_like(done)
     for r in reads:
         r.wait()
 
@@ -419,6 +521,7 @@
         2 * w_out.size,
         scratch=[pltpu.SemaphoreType.DMA((n,))],
         big=(0,),
+        loose=(1,),
     )
 
 
@@ -427,9 +530,9 @@
     half, slice_width = top.shape
     n_tiles = qs.shape[0]
     size = received[0].shape[0]
-    for d in range(n_y):
+    for d, block in zip((0, *send_order(n_y)), received):
         row = pl.multiple_of(place_along_y(n_y, -d) * size, HD)
-        state[pl.ds(row, size), :] = received[d][...]
+        state[pl.ds(row, size), :] = block[...]
     for j in range(n_tiles):
         for b in range(2):
             h = 2 * j + b
@@ -523,8 +626,7 @@
         )
 
     w = w_qkv.transpose(1, 0, 2)
-    part = slice_width // 2
-    t0, t1 = tokens[:, :part], tokens[:, part:]
+    t0, t1, early = split(tokens, w)
 
     l0 = along_x(t0, 1)
     r1 = along_x(t1, -1)
@@ -536,20 +638,20 @@
     arow, acol, ek, ea, ends, shard = decays(log_decay)
     far_places = ((2, 0), (2, 1))
     side_places = ((-1, 1), (1, 0))
-    total = near(((0, 0), (0, 1)), (t0, t1), w)[0]
+    total = own_products(t0, t1, w, early)
     total, w_side = near(((-1, 0), (1, 1)), (l0, r1), w, total, ahead=side_places)
     total, w_far = near(side_places, (l1, r0), w, total, w_side, ahead=far_places)
     far = (f0, f1)
-    k, v, s1, *kvs = key_value(n_y, far, w_far, total, ek, ends, shard)
-
-    sums = [kvs[0]] + [along_y(kvs[d], d) for d in range(1, n_y)]
+    w_slices, mark = fetch_out((2, 1, -1, 0), w_out, slice_width, total)
+    k, v, s1, *kvs = key_value(n_y, far, w_far, total, ek, ends, shard, mark)
+
+    sums = [kvs[0]] + [along_y(kvs[d], d) for d in send_order(n_y)]
     q = query(far, w_far, total)
     qs, o, mark = inner(q, k, v, acol, arow, ea)
     row, mark = row_sum(sums, mark)
-    earlier = [along_z(row, e) for e in range(1, n_z)]
-    w_slices, mark = fetch_out((2, 1, -1, 0), w_out, slice_width, mark)
+    earlier = [along_z(row, e) for e in send_order(n_z)]
     starts = states(sums, earlier, mark)
-    received = [starts[0]] + [along_y(starts[d], d) for d in range(1, n_y)]
+    received = [starts[0]] + [along_y(starts[d], d) for d in send_order(n_y)]
 
     attn, far_top, far_bot = attend(n_y, qs, o, w_slices, s1, ends, received, slice_width)
     relay_top = along_x(far_top, 1)

time: 91.5 us -> 89 us (0.973)
  Pallas kernels: 28.4 us -> 32.7 us
  local copies, waits for them, and re-layouts: 2.75 us -> 0.12 us
  starting transfers between devices: 36.2 us -> 34.1 us
  waiting for transfers between devices: 23.6 us -> 21.6 us
    ppermute x12, waiting for transfers between devices: 18 us -> 12.5 us  [along_x(): lax.ppermute(x, 'tensor', [(i, (i + shift) % n_t) for i in range(n_t)])]
    pallas_call x13 -> x14, Pallas kernels: 28.4 us -> 32.7 us  [call(): pl.pallas_call(kernel, grid=(1,), in_specs=[HBM if i in big else ANY if i...]
    ppermute x6, waiting for transfers between devices: 4.27 us -> 6.76 us  [along_y(): lax.ppermute(x, 'seq', [(z * n_y + y, z * n_y + (y + shift) % n_y) for z...]
    ppermute x6, starting transfers between devices: 10.1 us -> 7.85 us  [along_y(): lax.ppermute(x, 'seq', [(z * n_y + y, z * n_y + (y + shift) % n_y) for z...]
    unnamed x3, local copies, waits for them, and re-layouts: 1.55 us -> 0.12 us
    ppermute x3, starting transfers between devices: 5.98 us -> 7.2 us  [along_z(): lax.ppermute(x, 'seq', [(z * n_y + y, (z + shift) % n_z * n_y + y) for z...]
    slice x1 -> x0, local copies, waits for them, and re-layouts: 1.19 us -> none  [body(): t0, t1 = (tokens[:, :part], tokens[:, part:])]
    ppermute x12, starting transfers between devices: 20.1 us -> 19 us  [along_x(): lax.ppermute(x, 'tensor', [(i, (i + shift) % n_t) for i in range(n_t)])]
  transfers between devices with their start and end apart: 21 -> 21, of which waited for: 13 -> 11; matrix products, arithmetic and copies ran while one was open for 1% -> 0% of each run, Pallas kernels for 23% -> 22%
where the time goes in v4:
time: 89 us; the launch traced here: 88.9 us
  starting transfers between devices  34.1 us (38%)
  Pallas kernels  32.7 us (37%)
  waiting for transfers between devices  21.6 us (24%)
    pallas_call x14, Pallas kernels, call(): pl.pallas_call(kernel, grid=(1,), in_specs=[HBM if i in big else ANY if i...  32.7 us
    ppermute x12, starting transfers between devices, along_x(): lax.ppermute(x, 'tensor', [(i, (i + shift) % n_t) for i in range(n_t)])  19 us
    ppermute x12, waiting for transfers between devices, along_x(): lax.ppermute(x, 'tensor', [(i, (i + shift) % n_t) for i in range(n_t)])  12.5 us
    ppermute x6, starting transfers between devices, along_y(): lax.ppermute(x, 'seq', [(z * n_y + y, z * n_y + (y + shift) % n_y) for z...  7.85 us
    ppermute x3, starting transfers between devices, along_z(): lax.ppermute(x, 'seq', [(z * n_y + y, (z + shift) % n_z * n_y + y) for z...  7.2 us
    ppermute x6, waiting for transfers between devices, along_y(): lax.ppermute(x, 'seq', [(z * n_y + y, z * n_y + (y + shift) % n_y) for z...  6.76 us
    ppermute x3, waiting for transfers between devices, along_z(): lax.ppermute(x, 'seq', [(z * n_y + y, (z + shift) % n_z * n_y + y) for z...  2.28 us
  transfers between devices with their start and end apart: 21, of which 11 were waited for; matrix products, arithmetic and copies ran while one was open for 0% of the time, Pallas kernels for 22%

profile of v4, /device:TPU:0, one launch (start us, length us, event | category | flops | bytes accessed | tf_op | source)
XLA Modules:
  0.0 88.9 jit_solution(6903327681268987822)
XLA Ops:
  0.0 6.0 %split.1 = (bf16[512,384]{1,0:T(8,128)(2,1)S(1)}, bf16[512,384]{1,0:T(8,128)(2,1)S(1)}, f32[3,4,512,256]{3,2,1,0:T(8,128)}) custom-call(bf16[512,768]{1,0:T(8,128)(2,1)} %tokens.1, bf16[3,3072,1024]{2,1,0:T(8,128)(2,1)} %bitcast.3), custom_call_target="tpu_custom_call" | custom-call | flops 2415919104 | bytes 4718592 | tf_op jit(solution)/shard_map/split/pallas_call | solution.py:45
  6.0 1.6 %collective-permute-start = (bf16[512,384]{1,0:T(8,128)(2,1)S(1)}, bf16[512,384]{1,0:T(8,128)(2,1)S(1)}, u32[]{:S(2)}, u32[]{:S(2)}) collective-permute-start(bf16[512,384]{1,0:T(8,128)(2,1)S(1)} %get-tuple-element.44.t0), channel_id=1, source_target_pairs={{0,1},{1,2},{2,3},{3,0},{4,5},{5,6},{6,7},{7,4},{8,9},{9,10},{10,1... | collective-permute-start | bytes 1179656 | tf_op jit(solution)/shard_map/ppermute | solution.py:616
  7.6 1.7 %collective-permute-start.2 = (bf16[512,384]{1,0:T(8,128)(2,1)S(1)}, bf16[512,384]{1,0:T(8,128)(2,1)S(1)}, u32[]{:S(2)}, u32[]{:S(2)}) collective-permute-start(bf16[512,384]{1,0:T(8,128)(2,1)S(1)} %get-tuple-element.45.t1), channel_id=1, source_target_pairs={{0,3},{1,0},{2,1},{3,2},{4,7},{5,4},{6,5},{7,6},{8,11},{9,8},{10,9... | collective-permute-start | bytes 1179656 | tf_op jit(solution)/shard_map/ppermute | solution.py:616
  9.6 2.9 %collective-permute-start.5 = (bf16[512,384]{1,0:T(8,128)(2,1)S(1)}, bf16[512,384]{1,0:T(8,128)(2,1)S(1)}, u32[]{:S(2)}, u32[]{:S(2)}) collective-permute-start(bf16[512,384]{1,0:T(8,128)(2,1)S(1)} %get-tuple-element.44.t0), channel_id=1, source_target_pairs={{0,3},{1,0},{2,1},{3,2},{4,7},{5,4},{6,5},{7,6},{8,11},{9,8},{10,9... | collective-permute-start | bytes 1179656 | tf_op jit(solution)/shard_map/ppermute | solution.py:616
  13.5 2.8 %own.1.refs_0_ = f32[3,4,512,256]{3,2,1,0:T(8,128)S(1)} custom-call(bf16[512,384]{1,0:T(8,128)(2,1)S(1)} %get-tuple-element.44.t0, bf16[512,384]{1,0:T(8,128)(2,1)S(1)} %get-tuple-element.45.t1, bf16[3,3072,1024]{2,1,0:T(8,128)(2,1)} %bitcast.4, f32[3,4,512,256]{3,2,1,0:T(8,128)} %get-tuple-element.46.early), custom_call_target="tpu_custom_call" | custom-call | flops 2415919104 | bytes 4718592 | tf_op jit(solution)/shard_map/own/pallas_call | solution.py:45
  16.3 2.9 %collective-permute-done.a = bf16[512,384]{1,0:T(8,128)(2,1)S(1)} collective-permute-done((bf16[512,384]{1,0:T(8,128)(2,1)S(1)}, bf16[512,384]{1,0:T(8,128)(2,1)S(1)}, u32[]{:S(2)}, u32[]{:S(2)}) %collective-permute-start) | collective-permute-done | bytes 393248 | tf_op jit(solution)/shard_map/ppermute | solution.py:616
  19.7 2.8 %collective-permute-start.3 = (bf16[512,384]{1,0:T(8,128)(2,1)S(1)}, bf16[512,384]{1,0:T(8,128)(2,1)S(1)}, u32[]{:S(2)}, u32[]{:S(2)}) collective-permute-start(bf16[512,384]{1,0:T(8,128)(2,1)S(1)} %collective-permute-done.2.b), channel_id=1, source_target_pairs={{0,3},{1,0},{2,1},{3,2},{4,7},{5,4},{6,5},{7,6},{8,11},{9,8},{10,9... | collective-permute-start | bytes 1179656 | tf_op jit(solution)/shard_map/ppermute | solution.py:616
  22.4 5.0 %near.2 = (f32[3,4,512,256]{3,2,1,0:T(8,128)S(1)}, bf16[3,768,1024]{2,1,0:T(8,128)(2,1)S(1)}) custom-call(bf16[512,384]{1,0:T(8,128)(2,1)S(1)} %collective-permute-done.a, bf16[512,384]{1,0:T(8,128)(2,1)S(1)} %collective-permute-done.2.b, bf16[3,3072,1024]{2,1,0:T(8,128)(2,1)} %bitcast.5, f32[3,4,512,256]{3,2,1,0:T(8,128)S(1)} %own.1.refs_0_), custom_call_target="tpu_custom_call" | custom-call | flops 2415919104 | bytes 11010048 | tf_op jit(solution)/shard_map/near/pallas_call | solution.py:45
  27.4 2.7 %near.3 = (f32[3,4,512,256]{3,2,1,0:T(8,128)S(1)}, bf16[3,768,1024]{2,1,0:T(8,128)(2,1)S(1)}) custom-call(bf16[512,384]{1,0:T(8,128)(2,1)S(1)} %collective-permute-done.4.a, bf16[512,384]{1,0:T(8,128)(2,1)S(1)} %collective-permute-done.5.b, bf16[3,3072,1024]{2,1,0:T(8,128)(2,1)} %bitcast.6, f32[3,4,512,256]{3,2,1,0:T(8,128)S(1)} %get-tuple-element.47.refs_0_, ...), custom_call_target="tpu_custom_call" | custom-call | flops 2415919104 | bytes 11010048 | tf_op jit(solution)/shard_map/near/pallas_call | solution.py:45
  30.2 2.9 %fetch_out.1 = (bf16[4,1024,768]{2,1,0:T(8,128)(2,1)S(1)}, f32[8,128]{1,0:T(8,128)S(1)}) custom-call(bf16[1024,3072]{1,0:T(8,128)(2,1)} %w.1, f32[3,4,512,256]{3,2,1,0:T(8,128)S(1)} %get-tuple-element.50.total.after), custom_call_target="tpu_custom_call" | custom-call | bytes 6291456 | tf_op jit(solution)/shard_map/fetch_out/pallas_call | solution.py:45
  33.1 3.7 %key_value.1 = (bf16[4,512,256]{2,1,0:T(8,128)(2,1)S(1)}, bf16[4,512,256]{2,1,0:T(8,128)(2,1)S(1)}, f32[1024,128]{1,0:T(8,128)S(1)}, bf16[272,128]{1,0:T(8,128)(...) custom-call(bf16[512,384]{1,0:T(8,128)(2,1)S(1)} %collective-permute-done.1.f0, ...), custom_call_target="tpu_custom_call" | custom-call | flops 1610612736 | bytes 7340032 | tf_op jit(solution)/shard_map/key_value/pallas_call | solution.py:45
  36.8 3.3 %collective-permute-start.6 = (bf16[272,128]{1,0:T(8,128)(2,1)S(1)}, bf16[272,128]{1,0:T(8,128)(2,1)S(1)}, u32[]{:S(2)}, u32[]{:S(2)}) collective-permute-start(bf16[272,128]{1,0:T(8,128)(2,1)S(1)} %get-tuple-element.65), channel_id=1, source_target_pairs={{0,12},{4,0},{8,4},{12,8},{16,28},{20,16},{24,20},{28,24},{32,44},... | collective-permute-start | bytes 208904 | tf_op jit(solution)/shard_map/ppermute | solution.py:619
  46.8 4.0 %collective-permute-start.10 = (bf16[272,128]{1,0:T(8,128)(2,1)S(1)}, bf16[272,128]{1,0:T(8,128)(2,1)S(1)}, u32[]{:S(2)}, u32[]{:S(2)}) collective-permute-start(bf16[272,128]{1,0:T(8,128)(2,1)S(1)} %get-tuple-element.69), channel_id=1, source_target_pairs={{0,32},{4,36},{8,40},{12,44},{16,48},{20,52},{24,56},{28,60},{32,0... | collective-permute-start | bytes 208904 | tf_op jit(solution)/shard_map/ppermute | solution.py:624
  51.8 2.2 %collective-permute-start.9 = (bf16[272,128]{1,0:T(8,128)(2,1)S(1)}, bf16[272,128]{1,0:T(8,128)(2,1)S(1)}, u32[]{:S(2)}, u32[]{:S(2)}) collective-permute-start(bf16[272,128]{1,0:T(8,128)(2,1)S(1)} %get-tuple-element.69), channel_id=1, source_target_pairs={{0,48},{4,52},{8,56},{12,60},{16,0},{20,4},{24,8},{28,12},{32,16},... | collective-permute-start | bytes 208904 | tf_op jit(solution)/shard_map/ppermute | solution.py:624
  54.0 2.3 %collective-permute-done.11.refs_6_ = bf16[272,128]{1,0:T(8,128)(2,1)S(1)} collective-permute-done((bf16[272,128]{1,0:T(8,128)(2,1)S(1)}, bf16[272,128]{1,0:T(8,128)(2,1)S(1)}, u32[]{:S(2)}, u32[]{:S(2)}) %collective-permute-start.11) | collective-permute-done | bytes 69664 | tf_op jit(solution)/shard_map/ppermute | solution.py:624
  59.7 1.6 %collective-permute-done.12.refs_1_ = bf16[256,128]{1,0:T(8,128)(2,1)S(1)} collective-permute-done((bf16[256,128]{1,0:T(8,128)(2,1)S(1)}, bf16[256,128]{1,0:T(8,128)(2,1)S(1)}, u32[]{:S(2)}, u32[]{:S(2)}) %collective-permute-start.12) | collective-permute-done | bytes 65568 | tf_op jit(solution)/shard_map/ppermute | solution.py:619
  61.3 2.1 %collective-permute-done.13.refs_2_ = bf16[256,128]{1,0:T(8,128)(2,1)S(1)} collective-permute-done((bf16[256,128]{1,0:T(8,128)(2,1)S(1)}, bf16[256,128]{1,0:T(8,128)(2,1)S(1)}, u32[]{:S(2)}, u32[]{:S(2)}) %collective-permute-start.13) | collective-permute-done | bytes 65568 | tf_op jit(solution)/shard_map/ppermute | solution.py:619
  64.3 1.7 %attend.1 = (bf16[512,1024]{1,0:T(8,128)(2,1)S(1)}, bf16[256,768]{1,0:T(8,128)(2,1)S(1)}, bf16[256,768]{1,0:T(8,128)(2,1)S(1)}) custom-call(bf16[4,512,256]{2,1,0:T(8,128)(2,1)S(1)} %get-tuple-element.60.qs, f32[4,512,256]{2,1,0:T(8,128)S(1)} %get-tuple-element.61.o, bf16[4,1024,768]{2,1,0:T(8,128)(2,1)S(1)} %get-tuple-element.62.w, ...), custom_call_target="tpu_custom_call" | custom-call | flops 939524096 | bytes 5767168 | tf_op jit(solution)/shard_map/attend/pallas_call | solution.py:45
  68.1 2.6 %output.1 = (bf16[256,768]{1,0:T(8,128)(2,1)S(1)}, bf16[256,768]{1,0:T(8,128)(2,1)S(1)}, bf16[256,768]{1,0:T(8,128)(2,1)S(1)}, bf16[256,768]{1,0:T(8,128)(2,1)S(1)}, bf16[512,768]{1,0:T(8,128)(2,1)S(1)}) custom-call(bf16[512,1024]{1,0:T(8,128)(2,1)S(1)} %get-tuple-element.75.attn, bf16[4,1024,768]{2,1,0:T(8,128)(2,1)S(1)} %get-tuple-element.62.w), custom_call_target="tpu_custom_call" | custom-call | flops 2415919104 | bytes 7864320 | tf_op jit(solution)/shard_map/output/pallas_call | solution.py:45
  70.8 3.2 %collective-permute-start.18 = (bf16[256,768]{1,0:T(8,128)(2,1)S(1)}, bf16[256,768]{1,0:T(8,128)(2,1)S(1)}, u32[]{:S(2)}, u32[]{:S(2)}) collective-permute-start(bf16[256,768]{1,0:T(8,128)(2,1)S(1)} %get-tuple-element.80), channel_id=1, source_target_pairs={{0,3},{1,0},{2,1},{3,2},{4,7},{5,4},{6,5},{7,6},{8,11},{9,8},{10,9... | collective-permute-start | bytes 1179656 | tf_op jit(solution)/shard_map/ppermute | solution.py:616
  74.7 3.8 %collective-permute-start.20 = (bf16[256,768]{1,0:T(8,128)(2,1)S(1)}, bf16[256,768]{1,0:T(8,128)(2,1)S(1)}, u32[]{:S(2)}, u32[]{:S(2)}) collective-permute-start(bf16[256,768]{1,0:T(8,128)(2,1)S(1)} %add.7), channel_id=1, source_target_pairs={{0,3},{1,0},{2,1},{3,2},{4,7},{5,4},{6,5},{7,6},{8,11},{9,8},{10,9... | collective-permute-start | bytes 1179656 | tf_op jit(solution)/shard_map/ppermute | solution.py:616
  78.7 2.4 %collective-permute-done.17.lb = bf16[256,768]{1,0:T(8,128)(2,1)S(1)} collective-permute-done((bf16[256,768]{1,0:T(8,128)(2,1)S(1)}, bf16[256,768]{1,0:T(8,128)(2,1)S(1)}, u32[]{:S(2)}, u32[]{:S(2)}) %collective-permute-start.17) | collective-permute-done | bytes 393248 | tf_op jit(solution)/shard_map/ppermute | solution.py:616
  81.1 2.7 %collective-permute-done.20.rb = bf16[256,768]{1,0:T(8,128)(2,1)S(1)} collective-permute-done((bf16[256,768]{1,0:T(8,128)(2,1)S(1)}, bf16[256,768]{1,0:T(8,128)(2,1)S(1)}, u32[]{:S(2)}, u32[]{:S(2)}) %collective-permute-start.20) | collective-permute-done | bytes 393248 | tf_op jit(solution)/shard_map/ppermute | solution.py:616
  83.8 3.9 %collective-permute-done.16.lt = bf16[256,768]{1,0:T(8,128)(2,1)S(1)} collective-permute-done((bf16[256,768]{1,0:T(8,128)(2,1)S(1)}, bf16[256,768]{1,0:T(8,128)(2,1)S(1)}, u32[]{:S(2)}, u32[]{:S(2)}) %collective-permute-start.16) | collective-permute-done | bytes 393248 | tf_op jit(solution)/shard_map/ppermute | solution.py:616
  (37 shorter events, 18.1 us)
Async XLA Ops:
  0.0 12.5 %copy-start = (f32[8,512]{1,0:T(8,128)S(1)}, f32[8,512]{1,0:T(8,128)}, u32[]{:S(2)}) copy-start(f32[8,512]{1,0:T(8,128)} %ld.1) | copy-start | bytes 49156
  6.0 13.2 %collective-permute-start = (bf16[512,384]{1,0:T(8,128)(2,1)S(1)}, bf16[512,384]{1,0:T(8,128)(2,1)S(1)}, u32[]{:S(2)}, u32[]{:S(2)}) collective-permute-start(bf16[512,384]{1,0:T(8,128)(2,1)S(1)} %get-tuple-element.44.t0), channel_id=1, source_target_pairs={{0,1},{1,2},{2,3},{3,0},{4,5},{5,6},{6,7},{7,4},{8,9},{9,10},{10,1... | collective-permute-start | bytes 1179656 | tf_op jit(solution)/shard_map/ppermute | solution.py:616
  7.6 12.1 %collective-permute-start.2 = (bf16[512,384]{1,0:T(8,128)(2,1)S(1)}, bf16[512,384]{1,0:T(8,128)(2,1)S(1)}, u32[]{:S(2)}, u32[]{:S(2)}) collective-permute-start(bf16[512,384]{1,0:T(8,128)(2,1)S(1)} %get-tuple-element.45.t1), channel_id=1, source_target_pairs={{0,3},{1,0},{2,1},{3,2},{4,7},{5,4},{6,5},{7,6},{8,11},{9,8},{10,9... | collective-permute-start | bytes 1179656 | tf_op jit(solution)/shard_map/ppermute | solution.py:616
  9.3 18.1 %collective-permute-start.4 = (bf16[512,384]{1,0:T(8,128)(2,1)S(1)}, bf16[512,384]{1,0:T(8,128)(2,1)S(1)}, u32[]{:S(2)}, u32[]{:S(2)}) collective-permute-start(bf16[512,384]{1,0:T(8,128)(2,1)S(1)} %get-tuple-element.45.t1), channel_id=1, source_target_pairs={{0,1},{1,2},{2,3},{3,0},{4,5},{5,6},{6,7},{7,4},{8,9},{9,10},{10,1... | collective-permute-start | bytes 1179656 | tf_op jit(solution)/shard_map/ppermute | solution.py:616
  9.6 17.8 %collective-permute-start.5 = (bf16[512,384]{1,0:T(8,128)(2,1)S(1)}, bf16[512,384]{1,0:T(8,128)(2,1)S(1)}, u32[]{:S(2)}, u32[]{:S(2)}) collective-permute-start(bf16[512,384]{1,0:T(8,128)(2,1)S(1)} %get-tuple-element.44.t0), channel_id=1, source_target_pairs={{0,3},{1,0},{2,1},{3,2},{4,7},{5,4},{6,5},{7,6},{8,11},{9,8},{10,9... | collective-permute-start | bytes 1179656 | tf_op jit(solution)/shard_map/ppermute | solution.py:616
  19.2 13.9 %collective-permute-start.1 = (bf16[512,384]{1,0:T(8,128)(2,1)S(1)}, bf16[512,384]{1,0:T(8,128)(2,1)S(1)}, u32[]{:S(2)}, u32[]{:S(2)}) collective-permute-start(bf16[512,384]{1,0:T(8,128)(2,1)S(1)} %collective-permute-done.a), channel_id=1, source_target_pairs={{0,1},{1,2},{2,3},{3,0},{4,5},{5,6},{6,7},{7,4},{8,9},{9,10},{10,1... | collective-permute-start | bytes 1179656 | tf_op jit(solution)/shard_map/ppermute | solution.py:616
  19.7 13.4 %collective-permute-start.3 = (bf16[512,384]{1,0:T(8,128)(2,1)S(1)}, bf16[512,384]{1,0:T(8,128)(2,1)S(1)}, u32[]{:S(2)}, u32[]{:S(2)}) collective-permute-start(bf16[512,384]{1,0:T(8,128)(2,1)S(1)} %collective-permute-done.2.b), channel_id=1, source_target_pairs={{0,3},{1,0},{2,1},{3,2},{4,7},{5,4},{6,5},{7,6},{8,11},{9,8},{10,9... | collective-permute-start | bytes 1179656 | tf_op jit(solution)/shard_map/ppermute | solution.py:616
  36.8 7.6 %collective-permute-start.6 = (bf16[272,128]{1,0:T(8,128)(2,1)S(1)}, bf16[272,128]{1,0:T(8,128)(2,1)S(1)}, u32[]{:S(2)}, u32[]{:S(2)}) collective-permute-start(bf16[272,128]{1,0:T(8,128)(2,1)S(1)} %get-tuple-element.65), channel_id=1, source_target_pairs={{0,12},{4,0},{8,4},{12,8},{16,28},{20,16},{24,20},{28,24},{32,44},... | collective-permute-start | bytes 208904 | tf_op jit(solution)/shard_map/ppermute | solution.py:619
  40.1 5.9 %collective-permute-start.7 = (bf16[272,128]{1,0:T(8,128)(2,1)S(1)}, bf16[272,128]{1,0:T(8,128)(2,1)S(1)}, u32[]{:S(2)}, u32[]{:S(2)}) collective-permute-start(bf16[272,128]{1,0:T(8,128)(2,1)S(1)} %get-tuple-element.66), channel_id=1, source_target_pairs={{0,8},{4,12},{8,0},{12,4},{16,24},{20,28},{24,16},{28,20},{32,40},... | collective-permute-start | bytes 208904 | tf_op jit(solution)/shard_map/ppermute | solution.py:619
  40.7 5.9 %collective-permute-start.8 = (bf16[272,128]{1,0:T(8,128)(2,1)S(1)}, bf16[272,128]{1,0:T(8,128)(2,1)S(1)}, u32[]{:S(2)}, u32[]{:S(2)}) collective-permute-start(bf16[272,128]{1,0:T(8,128)(2,1)S(1)} %get-tuple-element.67), channel_id=1, source_target_pairs={{0,4},{4,8},{8,12},{12,0},{16,20},{20,24},{24,28},{28,16},{32,36},... | collective-permute-start | bytes 208904 | tf_op jit(solution)/shard_map/ppermute | solution.py:619
  46.8 7.2 %collective-permute-start.10 = (bf16[272,128]{1,0:T(8,128)(2,1)S(1)}, bf16[272,128]{1,0:T(8,128)(2,1)S(1)}, u32[]{:S(2)}, u32[]{:S(2)}) collective-permute-start(bf16[272,128]{1,0:T(8,128)(2,1)S(1)} %get-tuple-element.69), channel_id=1, source_target_pairs={{0,32},{4,36},{8,40},{12,44},{16,48},{20,52},{24,56},{28,60},{32,0... | collective-permute-start | bytes 208904 | tf_op jit(solution)/shard_map/ppermute | solution.py:624
  50.8 5.5 %collective-permute-start.11 = (bf16[272,128]{1,0:T(8,128)(2,1)S(1)}, bf16[272,128]{1,0:T(8,128)(2,1)S(1)}, u32[]{:S(2)}, u32[]{:S(2)}) collective-permute-start(bf16[272,128]{1,0:T(8,128)(2,1)S(1)} %get-tuple-element.69), channel_id=1, source_target_pairs={{0,16},{4,20},{8,24},{12,28},{16,32},{20,36},{24,40},{28,44},{32,4... | collective-permute-start | bytes 208904 | tf_op jit(solution)/shard_map/ppermute | solution.py:624
  51.8 4.5 %collective-permute-start.9 = (bf16[272,128]{1,0:T(8,128)(2,1)S(1)}, bf16[272,128]{1,0:T(8,128)(2,1)S(1)}, u32[]{:S(2)}, u32[]{:S(2)}) collective-permute-start(bf16[272,128]{1,0:T(8,128)(2,1)S(1)} %get-tuple-element.69), channel_id=1, source_target_pairs={{0,48},{4,52},{8,56},{12,60},{16,0},{20,4},{24,8},{28,12},{32,16},... | collective-permute-start | bytes 208904 | tf_op jit(solution)/shard_map/ppermute | solution.py:624
  56.8 4.6 %collective-permute-start.12 = (bf16[256,128]{1,0:T(8,128)(2,1)S(1)}, bf16[256,128]{1,0:T(8,128)(2,1)S(1)}, u32[]{:S(2)}, u32[]{:S(2)}) collective-permute-start(bf16[256,128]{1,0:T(8,128)(2,1)S(1)} %get-tuple-element.72), channel_id=1, source_target_pairs={{0,12},{4,0},{8,4},{12,8},{16,28},{20,16},{24,20},{28,24},{32,44},... | collective-permute-start | bytes 196616 | tf_op jit(solution)/shard_map/ppermute | solution.py:619
  57.6 5.8 %collective-permute-start.13 = (bf16[256,128]{1,0:T(8,128)(2,1)S(1)}, bf16[256,128]{1,0:T(8,128)(2,1)S(1)}, u32[]{:S(2)}, u32[]{:S(2)}) collective-permute-start(bf16[256,128]{1,0:T(8,128)(2,1)S(1)} %get-tuple-element.73), channel_id=1, source_target_pairs={{0,8},{4,12},{8,0},{12,4},{16,24},{20,28},{24,16},{28,20},{32,40},... | collective-permute-start | bytes 196616 | tf_op jit(solution)/shard_map/ppermute | solution.py:619
  58.8 5.5 %collective-permute-start.14 = (bf16[256,128]{1,0:T(8,128)(2,1)S(1)}, bf16[256,128]{1,0:T(8,128)(2,1)S(1)}, u32[]{:S(2)}, u32[]{:S(2)}) collective-permute-start(bf16[256,128]{1,0:T(8,128)(2,1)S(1)} %get-tuple-element.74), channel_id=1, source_target_pairs={{0,4},{4,8},{8,12},{12,0},{16,20},{20,24},{24,28},{28,16},{32,36},... | collective-permute-start | bytes 196616 | tf_op jit(solution)/shard_map/ppermute | solution.py:619
  66.0 8.7 %collective-permute-start.19 = (bf16[256,768]{1,0:T(8,128)(2,1)S(1)}, bf16[256,768]{1,0:T(8,128)(2,1)S(1)}, u32[]{:S(2)}, u32[]{:S(2)}) collective-permute-start(bf16[256,768]{1,0:T(8,128)(2,1)S(1)} %get-tuple-element.82), channel_id=1, source_target_pairs={{0,3},{1,0},{2,1},{3,2},{4,7},{5,4},{6,5},{7,6},{8,11},{9,8},{10,9... | collective-permute-start | bytes 1179656 | tf_op jit(solution)/shard_map/ppermute | solution.py:616
  67.5 11.0 %collective-permute-start.15 = (bf16[256,768]{1,0:T(8,128)(2,1)S(1)}, bf16[256,768]{1,0:T(8,128)(2,1)S(1)}, u32[]{:S(2)}, u32[]{:S(2)}) collective-permute-start(bf16[256,768]{1,0:T(8,128)(2,1)S(1)} %get-tuple-element.78), channel_id=1, source_target_pairs={{0,1},{1,2},{2,3},{3,0},{4,5},{5,6},{6,7},{7,4},{8,9},{9,10},{10,1... | collective-permute-start | bytes 1179656 | tf_op jit(solution)/shard_map/ppermute | solution.py:616
  70.7 10.4 %collective-permute-start.17 = (bf16[256,768]{1,0:T(8,128)(2,1)S(1)}, bf16[256,768]{1,0:T(8,128)(2,1)S(1)}, u32[]{:S(2)}, u32[]{:S(2)}) collective-permute-start(bf16[256,768]{1,0:T(8,128)(2,1)S(1)} %get-tuple-element.79), channel_id=1, source_target_pairs={{0,1},{1,2},{2,3},{3,0},{4,5},{5,6},{6,7},{7,4},{8,9},{9,10},{10,1... | collective-permute-start | bytes 1179656 | tf_op jit(solution)/shard_map/ppermute | solution.py:616
  70.8 10.3 %collective-permute-start.18 = (bf16[256,768]{1,0:T(8,128)(2,1)S(1)}, bf16[256,768]{1,0:T(8,128)(2,1)S(1)}, u32[]{:S(2)}, u32[]{:S(2)}) collective-permute-start(bf16[256,768]{1,0:T(8,128)(2,1)S(1)} %get-tuple-element.80), channel_id=1, source_target_pairs={{0,3},{1,0},{2,1},{3,2},{4,7},{5,4},{6,5},{7,6},{8,11},{9,8},{10,9... | collective-permute-start | bytes 1179656 | tf_op jit(solution)/shard_map/ppermute | solution.py:616
  74.7 9.1 %collective-permute-start.20 = (bf16[256,768]{1,0:T(8,128)(2,1)S(1)}, bf16[256,768]{1,0:T(8,128)(2,1)S(1)}, u32[]{:S(2)}, u32[]{:S(2)}) collective-permute-start(bf16[256,768]{1,0:T(8,128)(2,1)S(1)} %add.7), channel_id=1, source_target_pairs={{0,3},{1,0},{2,1},{3,2},{4,7},{5,4},{6,5},{7,6},{8,11},{9,8},{10,9... | collective-permute-start | bytes 1179656 | tf_op jit(solution)/shard_map/ppermute | solution.py:616
  78.6 9.1 %collective-permute-start.16 = (bf16[256,768]{1,0:T(8,128)(2,1)S(1)}, bf16[256,768]{1,0:T(8,128)(2,1)S(1)}, u32[]{:S(2)}, u32[]{:S(2)}) collective-permute-start(bf16[256,768]{1,0:T(8,128)(2,1)S(1)} %add.6), channel_id=1, source_target_pairs={{0,1},{1,2},{2,3},{3,0},{4,5},{5,6},{6,7},{7,4},{8,9},{9,10},{10,1... | collective-permute-start | bytes 1179656 | tf_op jit(solution)/shard_map/ppermute | solution.py:616

commit v5 on v4

--- a/solution.py
+++ b/solution.py
@@ -92,7 +92,7 @@
     return lax.rem(lax.axis_index("tensor") + (shift + n), n)
 
 
-def decay_kernel(ld, ldt, arow, acol, ek, ea, ends, shard):
+def decay_kernel(ld, ldt, after, arow, acol, ek, ea, ends, shard):
     heads, rows = ld.shape
     r = lax.broadcasted_iota(jnp.int32, (CHUNK, CHUNK), 0)
     c = lax.broadcasted_iota(jnp.int32, (CHUNK, CHUNK), 1)
@@ -113,11 +113,11 @@
     shard[0:1, 0:heads] = jnp.minimum(total, 0.0)
 
 
-def decays(log_decay):
+def decays(log_decay, after):
     heads, rows = log_decay.shape
     outs = [like(F32, heads, rows)] + [like(F32, rows, heads)] * 3
     outs += [like(F32, rows // CHUNK, heads), like(F32, 1, HD)]
-    return call(decay_kernel, "decays", (log_decay, log_decay.T), outs, 4, 0, 1e5)
+    return call(decay_kernel, "decays", (log_decay, log_decay.T, after), outs, 4, 0, 1e5, loose=(2,))
 
 
 def piece_rows(w, part, place, depth):
@@ -170,7 +170,7 @@
         "near",
         [*two, w] + [m for m in (before, held) if m is not None],
         outs,
-        16,
+        12 if held is None else 4,
         4 * rows * depth * parts * width,
         4 * depth * parts * width + rows * parts * width * 4,
         scratch=[pltpu.VMEM((rows, 2 * depth), BF16)]
@@ -234,47 +234,64 @@
     )
 
 
-def own_kernel(t0, t1, w, early, total, x, wv, sems):
+def own_kernel(shifts, t0, t1, w, early, w_out, total, slices, x, wv, sems):
     depth = t0.shape[1]
     parts = w.shape[0]
+    columns = slices.shape[2]
     copies = Copies(sems)
     first = lax.axis_index("dp") == 0
+
+    def fetch_slices():
+        reads = []
+        for i, shift in enumerate(shifts):
+            start = pl.multiple_of(tensor_at(shift) * columns, HD)
+            reads.append(copies.start(w_out.at[:, pl.ds(start, columns)], slices.at[i]))
+        return reads
 
     @pl.when(first)
     def _():
         copy = copies.start(early, total)
+        reads = fetch_slices()
         copy.wait()
+        for r in reads:
+            r.wait()
 
     @pl.when(jnp.logical_not(first))
     def _():
+        copies.used = 0
         row = pl.multiple_of(tensor_at(0) * 2 * depth, HD)
         fetches = [copies.start(w.at[p, pl.ds(row, 2 * depth), :], wv.at[p]) for p in range(parts)]
         x[:, :depth] = t0[...]
         x[:, depth:] = t1[...]
         for p in range(parts):
             fetches[p].wait()
+            if p == 0:
+                reads = fetch_slices()
             for j in range(total.shape[1]):
                 total[p, j] = dot(x[...], wv[p, :, pl.ds(j * TILE, TILE)])
-
-
-def own_products(t0, t1, w, early):
+        for r in reads:
+            r.wait()
+
+
+def own_products(t0, t1, w, early, w_out):
     rows, depth = t0.shape
     parts, _, columns = w.shape
-    return call(
-        own_kernel,
+    shifts = (2, 1, -1, 0)
+    return call(
+        functools.partial(own_kernel, shifts),
         "own",
-        (t0, t1, w, early),
-        [like(F32, *early.shape)],
-        16,
+        (t0, t1, w, early, w_out),
+        [like(F32, *early.shape), like(BF16, len(shifts), w_out.shape[0], 2 * depth)],
+        12,
         4 * rows * depth * parts * columns,
-        4 * depth * parts * columns,
+        4 * depth * parts * columns + 2 * w_out.size,
         scratch=[
             pltpu.VMEM((rows, 2 * depth), BF16),
             pltpu.VMEM((parts, 2 * depth, columns), BF16),
-            pltpu.SemaphoreType.DMA((parts + 1,)),
+            pltpu.SemaphoreType.DMA((parts + 1 + len(shifts),)),
         ],
-        big=(2, 3),
-    )[0]
+        big=(2, 3, 4),
+    )
 
 
 def log_rows(log):
@@ -299,7 +316,7 @@
     return lax.rem(lax.axis_index("seq") + (shift + n_y), n_y)
 
 
-def key_value_kernel(n_y, f0, f1, w, total, ek, ends, shard, mark, k_out, v_out, s1_out, *refs):
+def key_value_kernel(n_y, f0, f1, w, total, ek, ends, shard, k_out, v_out, s1_out, *refs):
     messages, (x, scaled, sv) = refs[:n_y], refs[n_y:]
     n_tiles, rows, _ = k_out.shape
     depth = f0.shape[1]
@@ -338,7 +355,7 @@
         messages[d][...] = sv[place_along_y(n_y, d)]
 
 
-def key_value(n_y, far, w, total, ek, ends, shard, after):
+def key_value(n_y, far, w, total, ek, ends, shard):
     _, n_tiles, rows, _ = total.shape
     width = w.shape[2]
     depth = far[0].shape[1]
@@ -347,7 +364,7 @@
     return call(
         functools.partial(key_value_kernel, n_y),
         "key_value",
-        (*far, w, total, ek, ends, shard, after),
+        (*far, w, total, ek, ends, shard),
         [tiles, tiles, like(F32, width, HD)] + [like(BF16, *size)] * n_y,
         16,
         4 * rows * 2 * depth * width,
@@ -497,34 +514,6 @@
     )
 
 
-def fetch_kernel(shifts, w, after, out, done, sems):
-    copies = Copies(sems)
-    slice_width = out.shape[2]
-    reads = []
-    for i, shift in enumerate(shifts):
-        start = pl.multiple_of(tensor_at(shift) * slice_width, HD)
-        reads.append(copies.start(w.at[:, pl.ds(start, slice_width)], out.at[i]))
-    done[...] = jnp.zeros_like(done)
-    for r in reads:
-        r.wait()
-
-
-def fetch_out(shifts, w_out, slice_width, after):
-    n = len(shifts)
-    return call(
-        functools.partial(fetch_kernel, shifts),
-        "fetch_out",
-        (w_out, after),
-        [like(BF16, n, w_out.shape[0], slice_width), MARK],
-        4,
-        0,
-        2 * w_out.size,
-        scratch=[pltpu.SemaphoreType.DMA((n,))],
-        big=(0,),
-        loose=(1,),
-    )
-
-
 def attend_kernel(n_y, qs, o, w, s1, ends, *refs):
     received, (attn, top, bot, state) = refs[:n_y], refs[n_y:]
     half, slice_width = top.shape
@@ -595,16 +584,30 @@
     )
 
 
-def finish_kernel(own, lt, lb, rt, rb, out):
-    half = lt.shape[0]
-    for i, (a, b) in enumerate(((lt, rt), (lb, rb))):
-        sl = pl.ds(i * half, half)
-        out[sl, :] = (own[sl, :].astype(F32) + a[...].astype(F32) + b[...].astype(F32)).astype(BF16)
-
-
-def finish(*parts):
-    own = parts[0]
-    return call(finish_kernel, "finish", parts, [like(BF16, *own.shape)], 8, own.size * 2, own.size * 8)[0]
+def finish_kernel(half, *refs):
+    own, a, b, out, held, sem = (*refs[:3], *refs[-3:])
+    rows = a.shape[0]
+    sl = pl.ds(half * rows, rows)
+    held[...] = (own[sl, :].astype(F32) + a[...].astype(F32) + b[...].astype(F32)).astype(BF16)
+    copy = pltpu.make_async_copy(held, out.at[sl, :], sem)
+    copy.start()
+    copy.wait()
+
+
+def finish(half, own, a, b, out=None):
+    return call(
+        functools.partial(finish_kernel, half),
+        "finish",
+        (own, a, b) if out is None else (own, a, b, out),
+        [like(BF16, *own.shape)],
+        8,
+        own.size,
+        own.size * 4,
+        scratch=[pltpu.VMEM(a.shape, BF16), pltpu.SemaphoreType.DMA],
+        big=(3,),
+        big_outs=(0,),
+        aliases=None if out is None else {3: 0},
+    )[0]
 
 
 def body(n_y, tokens, w_qkv, log_decay, w_out):
@@ -635,15 +638,14 @@
     f0 = along_x(l0, 1)
     f1 = along_x(r1, -1)
 
-    arow, acol, ek, ea, ends, shard = decays(log_decay)
     far_places = ((2, 0), (2, 1))
     side_places = ((-1, 1), (1, 0))
-    total = own_products(t0, t1, w, early)
+    total, w_slices = own_products(t0, t1, w, early, w_out)
     total, w_side = near(((-1, 0), (1, 1)), (l0, r1), w, total, ahead=side_places)
     total, w_far = near(side_places, (l1, r0), w, total, w_side, ahead=far_places)
+    arow, acol, ek, ea, ends, shard = decays(log_decay, total)
     far = (f0, f1)
-    w_slices, mark = fetch_out((2, 1, -1, 0), w_out, slice_width, total)
-    k, v, s1, *kvs = key_value(n_y, far, w_far, total, ek, ends, shard, mark)
+    k, v, s1, *kvs = key_value(n_y, far, w_far, total, ek, ends, shard)
 
     sums = [kvs[0]] + [along_y(kvs[d], d) for d in send_order(n_y)]
     q = query(far, w_far, total)
@@ -661,7 +663,8 @@
     right_top = along_x(m_top, -1)
     left_top = along_x(p_top + relay_top, 1)
     right_bot = along_x(m_bot + relay_bot, -1)
-    return finish(own, left_top, left_bot, right_top, right_bot)
+    out = finish(1, own, left_bot, right_bot)
+    return finish(0, own, left_top, right_top, out)
 
 
 def solution(mesh):

time: 89 us -> 88.4 us (level)
  no operation moved by 1% of the time
where the time goes in v5:
time: 88.4 us; the launch traced here: 88.3 us
  starting transfers between devices  33.9 us (38%)
  Pallas kernels  32.4 us (37%)
  waiting for transfers between devices  21.2 us (24%)
    pallas_call x14, Pallas kernels, call(): pl.pallas_call(kernel, grid=(1,), in_specs=[HBM if i in big else ANY if i...  32.4 us
    ppermute x12, starting transfers between devices, along_x(): lax.ppermute(x, 'tensor', [(i, (i + shift) % n_t) for i in range(n_t)])  19.2 us
    ppermute x12, waiting for transfers between devices, along_x(): lax.ppermute(x, 'tensor', [(i, (i + shift) % n_t) for i in range(n_t)])  12.2 us
    ppermute x6, starting transfers between devices, along_y(): lax.ppermute(x, 'seq', [(z * n_y + y, z * n_y + (y + shift) % n_y) for z...  7.53 us
    ppermute x3, starting transfers between devices, along_z(): lax.ppermute(x, 'seq', [(z * n_y + y, (z + shift) % n_z * n_y + y) for z...  7.2 us
    ppermute x6, waiting for transfers between devices, along_y(): lax.ppermute(x, 'seq', [(z * n_y + y, z * n_y + (y + shift) % n_y) for z...  6.75 us
    ppermute x3, waiting for transfers between devices, along_z(): lax.ppermute(x, 'seq', [(z * n_y + y, (z + shift) % n_z * n_y + y) for z...  2.28 us
  transfers between devices with their start and end apart: 21, of which 11 were waited for; matrix products, arithmetic and copies ran while one was open for 0% of the time, Pallas kernels for 22%

profile of v5, /device:TPU:0, one launch (start us, length us, event | category | flops | bytes accessed | tf_op | source)
XLA Modules:
  0.0 88.3 jit_solution(13329876909429348137)
XLA Ops:
  0.0 6.0 %split.1 = (bf16[512,384]{1,0:T(8,128)(2,1)S(1)}, bf16[512,384]{1,0:T(8,128)(2,1)S(1)}, f32[3,4,512,256]{3,2,1,0:T(8,128)}) custom-call(bf16[512,768]{1,0:T(8,128)(2,1)} %tokens.1, bf16[3,3072,1024]{2,1,0:T(8,128)(2,1)} %bitcast.3), custom_call_target="tpu_custom_call" | custom-call | flops 2415919104 | bytes 4718592 | tf_op jit(solution)/shard_map/split/pallas_call | solution.py:45
  6.0 1.6 %collective-permute-start = (bf16[512,384]{1,0:T(8,128)(2,1)S(1)}, bf16[512,384]{1,0:T(8,128)(2,1)S(1)}, u32[]{:S(2)}, u32[]{:S(2)}) collective-permute-start(bf16[512,384]{1,0:T(8,128)(2,1)S(1)} %get-tuple-element.44.t0), channel_id=1, source_target_pairs={{0,1},{1,2},{2,3},{3,0},{4,5},{5,6},{6,7},{7,4},{8,9},{9,10},{10,1... | collective-permute-start | bytes 1179656 | tf_op jit(solution)/shard_map/ppermute | solution.py:619
  7.6 1.7 %collective-permute-start.2 = (bf16[512,384]{1,0:T(8,128)(2,1)S(1)}, bf16[512,384]{1,0:T(8,128)(2,1)S(1)}, u32[]{:S(2)}, u32[]{:S(2)}) collective-permute-start(bf16[512,384]{1,0:T(8,128)(2,1)S(1)} %get-tuple-element.45.t1), channel_id=1, source_target_pairs={{0,3},{1,0},{2,1},{3,2},{4,7},{5,4},{6,5},{7,6},{8,11},{9,8},{10,9... | collective-permute-start | bytes 1179656 | tf_op jit(solution)/shard_map/ppermute | solution.py:619
  9.6 2.9 %collective-permute-start.5 = (bf16[512,384]{1,0:T(8,128)(2,1)S(1)}, bf16[512,384]{1,0:T(8,128)(2,1)S(1)}, u32[]{:S(2)}, u32[]{:S(2)}) collective-permute-start(bf16[512,384]{1,0:T(8,128)(2,1)S(1)} %get-tuple-element.44.t0), channel_id=1, source_target_pairs={{0,3},{1,0},{2,1},{3,2},{4,7},{5,4},{6,5},{7,6},{8,11},{9,8},{10,9... | collective-permute-start | bytes 1179656 | tf_op jit(solution)/shard_map/ppermute | solution.py:619
  12.6 4.7 %own.1 = (f32[3,4,512,256]{3,2,1,0:T(8,128)S(1)}, bf16[4,1024,768]{2,1,0:T(8,128)(2,1)S(1)}) custom-call(bf16[512,384]{1,0:T(8,128)(2,1)S(1)} %get-tuple-element.44.t0, bf16[512,384]{1,0:T(8,128)(2,1)S(1)} %get-tuple-element.45.t1, bf16[3,3072,1024]{2,1,0:T(8,128)(2,1)} %bitcast.4, f32[3,4,512,256]{3,2,1,0:T(8,128)} %get-tuple-element.46.early, ...), custom_call_target="tpu_custom_call" | custom-call | flops 2415919104 | bytes 11010048 | tf_op jit(solution)/shard_map/own/pallas_call | solution.py:45
  17.3 2.0 %collective-permute-done.a = bf16[512,384]{1,0:T(8,128)(2,1)S(1)} collective-permute-done((bf16[512,384]{1,0:T(8,128)(2,1)S(1)}, bf16[512,384]{1,0:T(8,128)(2,1)S(1)}, u32[]{:S(2)}, u32[]{:S(2)}) %collective-permute-start) | collective-permute-done | bytes 393248 | tf_op jit(solution)/shard_map/ppermute | solution.py:619
  19.7 2.9 %collective-permute-start.3 = (bf16[512,384]{1,0:T(8,128)(2,1)S(1)}, bf16[512,384]{1,0:T(8,128)(2,1)S(1)}, u32[]{:S(2)}, u32[]{:S(2)}) collective-permute-start(bf16[512,384]{1,0:T(8,128)(2,1)S(1)} %collective-permute-done.2.b), channel_id=1, source_target_pairs={{0,3},{1,0},{2,1},{3,2},{4,7},{5,4},{6,5},{7,6},{8,11},{9,8},{10,9... | collective-permute-start | bytes 1179656 | tf_op jit(solution)/shard_map/ppermute | solution.py:619
  22.5 5.0 %near.2 = (f32[3,4,512,256]{3,2,1,0:T(8,128)S(1)}, bf16[3,768,1024]{2,1,0:T(8,128)(2,1)S(1)}) custom-call(bf16[512,384]{1,0:T(8,128)(2,1)S(1)} %collective-permute-done.a, bf16[512,384]{1,0:T(8,128)(2,1)S(1)} %collective-permute-done.2.b, bf16[3,3072,1024]{2,1,0:T(8,128)(2,1)} %bitcast.5, f32[3,4,512,256]{3,2,1,0:T(8,128)S(1)} %get-tuple-element.47.refs_0_), custom_call_target="tpu_custom_call" | custom-call | flops 2415919104 | bytes 11010048 | tf_op jit(solution)/shard_map/near/pallas_call | solution.py:45
  27.5 2.7 %near.3 = (f32[3,4,512,256]{3,2,1,0:T(8,128)S(1)}, bf16[3,768,1024]{2,1,0:T(8,128)(2,1)S(1)}) custom-call(bf16[512,384]{1,0:T(8,128)(2,1)S(1)} %collective-permute-done.4.a, bf16[512,384]{1,0:T(8,128)(2,1)S(1)} %collective-permute-done.5.b, bf16[3,3072,1024]{2,1,0:T(8,128)(2,1)} %bitcast.6, f32[3,4,512,256]{3,2,1,0:T(8,128)S(1)} %get-tuple-element.48.refs_0_, ...), custom_call_target="tpu_custom_call" | custom-call | flops 2415919104 | bytes 11010048 | tf_op jit(solution)/shard_map/near/pallas_call | solution.py:45
  31.1 3.8 %key_value.1 = (bf16[4,512,256]{2,1,0:T(8,128)(2,1)S(1)}, bf16[4,512,256]{2,1,0:T(8,128)(2,1)S(1)}, f32[1024,128]{1,0:T(8,128)S(1)}, bf16[272,128]{1,0:T(8,128)(...) custom-call(bf16[512,384]{1,0:T(8,128)(2,1)S(1)} %collective-permute-done.1.f0, ...), custom_call_target="tpu_custom_call" | custom-call | flops 1610612736 | bytes 7340032 | tf_op jit(solution)/shard_map/key_value/pallas_call | solution.py:45
  34.9 3.2 %collective-permute-start.6 = (bf16[272,128]{1,0:T(8,128)(2,1)S(1)}, bf16[272,128]{1,0:T(8,128)(2,1)S(1)}, u32[]{:S(2)}, u32[]{:S(2)}) collective-permute-start(bf16[272,128]{1,0:T(8,128)(2,1)S(1)} %get-tuple-element.65), channel_id=1, source_target_pairs={{0,12},{4,0},{8,4},{12,8},{16,28},{20,16},{24,20},{28,24},{32,44},... | collective-permute-start | bytes 208904 | tf_op jit(solution)/shard_map/ppermute | solution.py:622
  44.8 4.0 %collective-permute-start.10 = (bf16[272,128]{1,0:T(8,128)(2,1)S(1)}, bf16[272,128]{1,0:T(8,128)(2,1)S(1)}, u32[]{:S(2)}, u32[]{:S(2)}) collective-permute-start(bf16[272,128]{1,0:T(8,128)(2,1)S(1)} %get-tuple-element.69), channel_id=1, source_target_pairs={{0,32},{4,36},{8,40},{12,44},{16,48},{20,52},{24,56},{28,60},{32,0... | collective-permute-start | bytes 208904 | tf_op jit(solution)/shard_map/ppermute | solution.py:627
  49.7 2.2 %collective-permute-start.9 = (bf16[272,128]{1,0:T(8,128)(2,1)S(1)}, bf16[272,128]{1,0:T(8,128)(2,1)S(1)}, u32[]{:S(2)}, u32[]{:S(2)}) collective-permute-start(bf16[272,128]{1,0:T(8,128)(2,1)S(1)} %get-tuple-element.69), channel_id=1, source_target_pairs={{0,48},{4,52},{8,56},{12,60},{16,0},{20,4},{24,8},{28,12},{32,16},... | collective-permute-start | bytes 208904 | tf_op jit(solution)/shard_map/ppermute | solution.py:627
  52.0 2.3 %collective-permute-done.11.refs_6_ = bf16[272,128]{1,0:T(8,128)(2,1)S(1)} collective-permute-done((bf16[272,128]{1,0:T(8,128)(2,1)S(1)}, bf16[272,128]{1,0:T(8,128)(2,1)S(1)}, u32[]{:S(2)}, u32[]{:S(2)}) %collective-permute-start.11) | collective-permute-done | bytes 69664 | tf_op jit(solution)/shard_map/ppermute | solution.py:627
  59.1 2.1 %collective-permute-done.13.refs_2_ = bf16[256,128]{1,0:T(8,128)(2,1)S(1)} collective-permute-done((bf16[256,128]{1,0:T(8,128)(2,1)S(1)}, bf16[256,128]{1,0:T(8,128)(2,1)S(1)}, u32[]{:S(2)}, u32[]{:S(2)}) %collective-permute-start.13) | collective-permute-done | bytes 65568 | tf_op jit(solution)/shard_map/ppermute | solution.py:622
  62.1 1.7 %attend.1 = (bf16[512,1024]{1,0:T(8,128)(2,1)S(1)}, bf16[256,768]{1,0:T(8,128)(2,1)S(1)}, bf16[256,768]{1,0:T(8,128)(2,1)S(1)}) custom-call(bf16[4,512,256]{2,1,0:T(8,128)(2,1)S(1)} %get-tuple-element.60.qs, f32[4,512,256]{2,1,0:T(8,128)S(1)} %get-tuple-element.61.o, bf16[4,1024,768]{2,1,0:T(8,128)(2,1)S(1)} %get-tuple-element.62.w, ...), custom_call_target="tpu_custom_call" | custom-call | flops 939524096 | bytes 5767168 | tf_op jit(solution)/shard_map/attend/pallas_call | solution.py:45
  63.8 2.2 %collective-permute-start.19 = (bf16[256,768]{1,0:T(8,128)(2,1)S(1)}, bf16[256,768]{1,0:T(8,128)(2,1)S(1)}, u32[]{:S(2)}, u32[]{:S(2)}) collective-permute-start(bf16[256,768]{1,0:T(8,128)(2,1)S(1)} %get-tuple-element.82), channel_id=1, source_target_pairs={{0,3},{1,0},{2,1},{3,2},{4,7},{5,4},{6,5},{7,6},{8,11},{9,8},{10,9... | collective-permute-start | bytes 1179656 | tf_op jit(solution)/shard_map/ppermute | solution.py:619
  66.0 2.6 %output.1 = (bf16[256,768]{1,0:T(8,128)(2,1)S(1)}, bf16[256,768]{1,0:T(8,128)(2,1)S(1)}, bf16[256,768]{1,0:T(8,128)(2,1)S(1)}, bf16[256,768]{1,0:T(8,128)(2,1)S(1)}, bf16[512,768]{1,0:T(8,128)(2,1)S(1)}) custom-call(bf16[512,1024]{1,0:T(8,128)(2,1)S(1)} %get-tuple-element.75.attn, bf16[4,1024,768]{2,1,0:T(8,128)(2,1)S(1)} %get-tuple-element.62.w), custom_call_target="tpu_custom_call" | custom-call | flops 2415919104 | bytes 7864320 | tf_op jit(solution)/shard_map/output/pallas_call | solution.py:45
  69.2 2.8 %collective-permute-start.17 = (bf16[256,768]{1,0:T(8,128)(2,1)S(1)}, bf16[256,768]{1,0:T(8,128)(2,1)S(1)}, u32[]{:S(2)}, u32[]{:S(2)}) collective-permute-start(bf16[256,768]{1,0:T(8,128)(2,1)S(1)} %get-tuple-element.79), channel_id=1, source_target_pairs={{0,3},{1,0},{2,1},{3,2},{4,7},{5,4},{6,5},{7,6},{8,11},{9,8},{10,9... | collective-permute-start | bytes 1179656 | tf_op jit(solution)/shard_map/ppermute | solution.py:619
  72.0 2.2 %collective-permute-done.19 = bf16[256,768]{1,0:T(8,128)(2,1)S(1)} collective-permute-done((bf16[256,768]{1,0:T(8,128)(2,1)S(1)}, bf16[256,768]{1,0:T(8,128)(2,1)S(1)}, u32[]{:S(2)}, u32[]{:S(2)}) %collective-permute-start.19) | collective-permute-done | bytes 393248 | tf_op jit(solution)/shard_map/ppermute | solution.py:619
  74.3 3.8 %collective-permute-start.20 = (bf16[256,768]{1,0:T(8,128)(2,1)S(1)}, bf16[256,768]{1,0:T(8,128)(2,1)S(1)}, u32[]{:S(2)}, u32[]{:S(2)}) collective-permute-start(bf16[256,768]{1,0:T(8,128)(2,1)S(1)} %add.7), channel_id=1, source_target_pairs={{0,3},{1,0},{2,1},{3,2},{4,7},{5,4},{6,5},{7,6},{8,11},{9,8},{10,9... | collective-permute-start | bytes 1179656 | tf_op jit(solution)/shard_map/ppermute | solution.py:619
  78.2 2.4 %collective-permute-done.18.refs_1_ = bf16[256,768]{1,0:T(8,128)(2,1)S(1)} collective-permute-done((bf16[256,768]{1,0:T(8,128)(2,1)S(1)}, bf16[256,768]{1,0:T(8,128)(2,1)S(1)}, u32[]{:S(2)}, u32[]{:S(2)}) %collective-permute-start.18) | collective-permute-done | bytes 393248 | tf_op jit(solution)/shard_map/ppermute | solution.py:619
  80.6 2.7 %collective-permute-done.20.refs_2_ = bf16[256,768]{1,0:T(8,128)(2,1)S(1)} collective-permute-done((bf16[256,768]{1,0:T(8,128)(2,1)S(1)}, bf16[256,768]{1,0:T(8,128)(2,1)S(1)}, u32[]{:S(2)}, u32[]{:S(2)}) %collective-permute-start.20) | collective-permute-done | bytes 393248 | tf_op jit(solution)/shard_map/ppermute | solution.py:619
  84.2 2.9 %collective-permute-done.16.refs_1_ = bf16[256,768]{1,0:T(8,128)(2,1)S(1)} collective-permute-done((bf16[256,768]{1,0:T(8,128)(2,1)S(1)}, bf16[256,768]{1,0:T(8,128)(2,1)S(1)}, u32[]{:S(2)}, u32[]{:S(2)}) %collective-permute-start.16) | collective-permute-done | bytes 393248 | tf_op jit(solution)/shard_map/ppermute | solution.py:619
  (37 shorter events, 17.9 us)
Async XLA Ops:
  0.0 12.5 %copy-start = (f32[8,512]{1,0:T(8,128)S(1)}, f32[8,512]{1,0:T(8,128)}, u32[]{:S(2)}) copy-start(f32[8,512]{1,0:T(8,128)} %ld.1) | copy-start | bytes 49156
  6.0 13.3 %collective-permute-start = (bf16[512,384]{1,0:T(8,128)(2,1)S(1)}, bf16[512,384]{1,0:T(8,128)(2,1)S(1)}, u32[]{:S(2)}, u32[]{:S(2)}) collective-permute-start(bf16[512,384]{1,0:T(8,128)(2,1)S(1)} %get-tuple-element.44.t0), channel_id=1, source_target_pairs={{0,1},{1,2},{2,3},{3,0},{4,5},{5,6},{6,7},{7,4},{8,9},{9,10},{10,1... | collective-permute-start | bytes 1179656 | tf_op jit(solution)/shard_map/ppermute | solution.py:619
  7.6 12.1 %collective-permute-start.2 = (bf16[512,384]{1,0:T(8,128)(2,1)S(1)}, bf16[512,384]{1,0:T(8,128)(2,1)S(1)}, u32[]{:S(2)}, u32[]{:S(2)}) collective-permute-start(bf16[512,384]{1,0:T(8,128)(2,1)S(1)} %get-tuple-element.45.t1), channel_id=1, source_target_pairs={{0,3},{1,0},{2,1},{3,2},{4,7},{5,4},{6,5},{7,6},{8,11},{9,8},{10,9... | collective-permute-start | bytes 1179656 | tf_op jit(solution)/shard_map/ppermute | solution.py:619
  9.3 18.2 %collective-permute-start.4 = (bf16[512,384]{1,0:T(8,128)(2,1)S(1)}, bf16[512,384]{1,0:T(8,128)(2,1)S(1)}, u32[]{:S(2)}, u32[]{:S(2)}) collective-permute-start(bf16[512,384]{1,0:T(8,128)(2,1)S(1)} %get-tuple-element.45.t1), channel_id=1, source_target_pairs={{0,1},{1,2},{2,3},{3,0},{4,5},{5,6},{6,7},{7,4},{8,9},{9,10},{10,1... | collective-permute-start | bytes 1179656 | tf_op jit(solution)/shard_map/ppermute | solution.py:619
  9.6 17.9 %collective-permute-start.5 = (bf16[512,384]{1,0:T(8,128)(2,1)S(1)}, bf16[512,384]{1,0:T(8,128)(2,1)S(1)}, u32[]{:S(2)}, u32[]{:S(2)}) collective-permute-start(bf16[512,384]{1,0:T(8,128)(2,1)S(1)} %get-tuple-element.44.t0), channel_id=1, source_target_pairs={{0,3},{1,0},{2,1},{3,2},{4,7},{5,4},{6,5},{7,6},{8,11},{9,8},{10,9... | collective-permute-start | bytes 1179656 | tf_op jit(solution)/shard_map/ppermute | solution.py:619
  19.3 11.8 %collective-permute-start.1 = (bf16[512,384]{1,0:T(8,128)(2,1)S(1)}, bf16[512,384]{1,0:T(8,128)(2,1)S(1)}, u32[]{:S(2)}, u32[]{:S(2)}) collective-permute-start(bf16[512,384]{1,0:T(8,128)(2,1)S(1)} %collective-permute-done.a), channel_id=1, source_target_pairs={{0,1},{1,2},{2,3},{3,0},{4,5},{5,6},{6,7},{7,4},{8,9},{9,10},{10,1... | collective-permute-start | bytes 1179656 | tf_op jit(solution)/shard_map/ppermute | solution.py:619
  19.7 11.4 %collective-permute-start.3 = (bf16[512,384]{1,0:T(8,128)(2,1)S(1)}, bf16[512,384]{1,0:T(8,128)(2,1)S(1)}, u32[]{:S(2)}, u32[]{:S(2)}) collective-permute-start(bf16[512,384]{1,0:T(8,128)(2,1)S(1)} %collective-permute-done.2.b), channel_id=1, source_target_pairs={{0,3},{1,0},{2,1},{3,2},{4,7},{5,4},{6,5},{7,6},{8,11},{9,8},{10,9... | collective-permute-start | bytes 1179656 | tf_op jit(solution)/shard_map/ppermute | solution.py:619
  34.9 7.6 %collective-permute-start.6 = (bf16[272,128]{1,0:T(8,128)(2,1)S(1)}, bf16[272,128]{1,0:T(8,128)(2,1)S(1)}, u32[]{:S(2)}, u32[]{:S(2)}) collective-permute-start(bf16[272,128]{1,0:T(8,128)(2,1)S(1)} %get-tuple-element.65), channel_id=1, source_target_pairs={{0,12},{4,0},{8,4},{12,8},{16,28},{20,16},{24,20},{28,24},{32,44},... | collective-permute-start | bytes 208904 | tf_op jit(solution)/shard_map/ppermute | solution.py:622
  38.0 5.9 %collective-permute-start.7 = (bf16[272,128]{1,0:T(8,128)(2,1)S(1)}, bf16[272,128]{1,0:T(8,128)(2,1)S(1)}, u32[]{:S(2)}, u32[]{:S(2)}) collective-permute-start(bf16[272,128]{1,0:T(8,128)(2,1)S(1)} %get-tuple-element.66), channel_id=1, source_target_pairs={{0,8},{4,12},{8,0},{12,4},{16,24},{20,28},{24,16},{28,20},{32,40},... | collective-permute-start | bytes 208904 | tf_op jit(solution)/shard_map/ppermute | solution.py:622
  38.7 5.9 %collective-permute-start.8 = (bf16[272,128]{1,0:T(8,128)(2,1)S(1)}, bf16[272,128]{1,0:T(8,128)(2,1)S(1)}, u32[]{:S(2)}, u32[]{:S(2)}) collective-permute-start(bf16[272,128]{1,0:T(8,128)(2,1)S(1)} %get-tuple-element.67), channel_id=1, source_target_pairs={{0,4},{4,8},{8,12},{12,0},{16,20},{20,24},{24,28},{28,16},{32,36},... | collective-permute-start | bytes 208904 | tf_op jit(solution)/shard_map/ppermute | solution.py:622
  44.8 7.2 %collective-permute-start.10 = (bf16[272,128]{1,0:T(8,128)(2,1)S(1)}, bf16[272,128]{1,0:T(8,128)(2,1)S(1)}, u32[]{:S(2)}, u32[]{:S(2)}) collective-permute-start(bf16[272,128]{1,0:T(8,128)(2,1)S(1)} %get-tuple-element.69), channel_id=1, source_target_pairs={{0,32},{4,36},{8,40},{12,44},{16,48},{20,52},{24,56},{28,60},{32,0... | collective-permute-start | bytes 208904 | tf_op jit(solution)/shard_map/ppermute | solution.py:627
  48.7 5.5 %collective-permute-start.11 = (bf16[272,128]{1,0:T(8,128)(2,1)S(1)}, bf16[272,128]{1,0:T(8,128)(2,1)S(1)}, u32[]{:S(2)}, u32[]{:S(2)}) collective-permute-start(bf16[272,128]{1,0:T(8,128)(2,1)S(1)} %get-tuple-element.69), channel_id=1, source_target_pairs={{0,16},{4,20},{8,24},{12,28},{16,32},{20,36},{24,40},{28,44},{32,4... | collective-permute-start | bytes 208904 | tf_op jit(solution)/shard_map/ppermute | solution.py:627
  49.7 4.5 %collective-permute-start.9 = (bf16[272,128]{1,0:T(8,128)(2,1)S(1)}, bf16[272,128]{1,0:T(8,128)(2,1)S(1)}, u32[]{:S(2)}, u32[]{:S(2)}) collective-permute-start(bf16[272,128]{1,0:T(8,128)(2,1)S(1)} %get-tuple-element.69), channel_id=1, source_target_pairs={{0,48},{4,52},{8,56},{12,60},{16,0},{20,4},{24,8},{28,12},{32,16},... | collective-permute-start | bytes 208904 | tf_op jit(solution)/shard_map/ppermute | solution.py:627
  54.7 4.3 %collective-permute-start.12 = (bf16[256,128]{1,0:T(8,128)(2,1)S(1)}, bf16[256,128]{1,0:T(8,128)(2,1)S(1)}, u32[]{:S(2)}, u32[]{:S(2)}) collective-permute-start(bf16[256,128]{1,0:T(8,128)(2,1)S(1)} %get-tuple-element.72), channel_id=1, source_target_pairs={{0,12},{4,0},{8,4},{12,8},{16,28},{20,16},{24,20},{28,24},{32,44},... | collective-permute-start | bytes 196616 | tf_op jit(solution)/shard_map/ppermute | solution.py:622
  55.4 5.8 %collective-permute-start.13 = (bf16[256,128]{1,0:T(8,128)(2,1)S(1)}, bf16[256,128]{1,0:T(8,128)(2,1)S(1)}, u32[]{:S(2)}, u32[]{:S(2)}) collective-permute-start(bf16[256,128]{1,0:T(8,128)(2,1)S(1)} %get-tuple-element.73), channel_id=1, source_target_pairs={{0,8},{4,12},{8,0},{12,4},{16,24},{20,28},{24,16},{28,20},{32,40},... | collective-permute-start | bytes 196616 | tf_op jit(solution)/shard_map/ppermute | solution.py:622
  56.6 5.5 %collective-permute-start.14 = (bf16[256,128]{1,0:T(8,128)(2,1)S(1)}, bf16[256,128]{1,0:T(8,128)(2,1)S(1)}, u32[]{:S(2)}, u32[]{:S(2)}) collective-permute-start(bf16[256,128]{1,0:T(8,128)(2,1)S(1)} %get-tuple-element.74), channel_id=1, source_target_pairs={{0,4},{4,8},{8,12},{12,0},{16,20},{20,24},{24,28},{28,16},{32,36},... | collective-permute-start | bytes 196616 | tf_op jit(solution)/shard_map/ppermute | solution.py:622
  63.8 10.3 %collective-permute-start.19 = (bf16[256,768]{1,0:T(8,128)(2,1)S(1)}, bf16[256,768]{1,0:T(8,128)(2,1)S(1)}, u32[]{:S(2)}, u32[]{:S(2)}) collective-permute-start(bf16[256,768]{1,0:T(8,128)(2,1)S(1)} %get-tuple-element.82), channel_id=1, source_target_pairs={{0,3},{1,0},{2,1},{3,2},{4,7},{5,4},{6,5},{7,6},{8,11},{9,8},{10,9... | collective-permute-start | bytes 1179656 | tf_op jit(solution)/shard_map/ppermute | solution.py:619
  66.0 12.0 %collective-permute-start.15 = (bf16[256,768]{1,0:T(8,128)(2,1)S(1)}, bf16[256,768]{1,0:T(8,128)(2,1)S(1)}, u32[]{:S(2)}, u32[]{:S(2)}) collective-permute-start(bf16[256,768]{1,0:T(8,128)(2,1)S(1)} %get-tuple-element.78), channel_id=1, source_target_pairs={{0,1},{1,2},{2,3},{3,0},{4,5},{5,6},{6,7},{7,4},{8,9},{9,10},{10,1... | collective-permute-start | bytes 1179656 | tf_op jit(solution)/shard_map/ppermute | solution.py:619
  68.6 12.0 %collective-permute-start.18 = (bf16[256,768]{1,0:T(8,128)(2,1)S(1)}, bf16[256,768]{1,0:T(8,128)(2,1)S(1)}, u32[]{:S(2)}, u32[]{:S(2)}) collective-permute-start(bf16[256,768]{1,0:T(8,128)(2,1)S(1)} %get-tuple-element.80), channel_id=1, source_target_pairs={{0,1},{1,2},{2,3},{3,0},{4,5},{5,6},{6,7},{7,4},{8,9},{9,10},{10,1... | collective-permute-start | bytes 1179656 | tf_op jit(solution)/shard_map/ppermute | solution.py:619
  69.2 15.0 %collective-permute-start.17 = (bf16[256,768]{1,0:T(8,128)(2,1)S(1)}, bf16[256,768]{1,0:T(8,128)(2,1)S(1)}, u32[]{:S(2)}, u32[]{:S(2)}) collective-permute-start(bf16[256,768]{1,0:T(8,128)(2,1)S(1)} %get-tuple-element.79), channel_id=1, source_target_pairs={{0,3},{1,0},{2,1},{3,2},{4,7},{5,4},{6,5},{7,6},{8,11},{9,8},{10,9... | collective-permute-start | bytes 1179656 | tf_op jit(solution)/shard_map/ppermute | solution.py:619
  74.3 9.1 %collective-permute-start.20 = (bf16[256,768]{1,0:T(8,128)(2,1)S(1)}, bf16[256,768]{1,0:T(8,128)(2,1)S(1)}, u32[]{:S(2)}, u32[]{:S(2)}) collective-permute-start(bf16[256,768]{1,0:T(8,128)(2,1)S(1)} %add.7), channel_id=1, source_target_pairs={{0,3},{1,0},{2,1},{3,2},{4,7},{5,4},{6,5},{7,6},{8,11},{9,8},{10,9... | collective-permute-start | bytes 1179656 | tf_op jit(solution)/shard_map/ppermute | solution.py:619
  78.1 9.1 %collective-permute-start.16 = (bf16[256,768]{1,0:T(8,128)(2,1)S(1)}, bf16[256,768]{1,0:T(8,128)(2,1)S(1)}, u32[]{:S(2)}, u32[]{:S(2)}) collective-permute-start(bf16[256,768]{1,0:T(8,128)(2,1)S(1)} %add.6), channel_id=1, source_target_pairs={{0,1},{1,2},{2,3},{3,0},{4,5},{5,6},{6,7},{7,4},{8,9},{9,10},{10,1... | collective-permute-start | bytes 1179656 | tf_op jit(solution)/shard_map/ppermute | solution.py:619

commit v6 on v5

--- a/solution.py
+++ b/solution.py
@@ -557,30 +557,24 @@
     )
 
 
-def output_kernel(attn, w, p_top, p_bot, m_top, m_bot, own):
-    half, slice_width = p_top.shape
-    for i, outs in enumerate(((p_top, p_bot), (m_top, m_bot), (own,))):
-        for j in range(slice_width // TILE):
+def columns_kernel(takes, attn, w, *refs):
+    for (m, start, rows), out in zip(takes, refs):
+        for j in range(out.shape[1] // TILE):
             cols = pl.ds(j * TILE, TILE)
-            out = dot(attn[...], w[i + 1, :, cols]).astype(BF16)
-            if len(outs) == 1:
-                own[:, cols] = out
-            else:
-                outs[0][:, cols] = out[:half]
-                outs[1][:, cols] = out[half:]
-
-
-def output(attn, w_out, slice_width):
-    rows, width = attn.shape
-    half = rows // 2
-    return call(
-        output_kernel,
-        "output",
-        (attn, w_out),
-        [like(BF16, half, slice_width)] * 4 + [like(BF16, rows, slice_width)],
+            out[:, cols] = dot(attn[pl.ds(start, rows), :], w[m, :, cols]).astype(BF16)
+
+
+def columns(takes, attn, w):
+    slice_width = w.shape[2]
+    rows = sum(r for _, _, r in takes)
+    return call(
+        functools.partial(columns_kernel, takes),
+        "columns",
+        (attn, w),
+        [like(BF16, r, slice_width) for _, _, r in takes],
         16,
-        6 * rows * width * slice_width,
-        6 * width * slice_width + 8 * rows * slice_width,
+        2 * rows * attn.shape[1] * slice_width,
+        6 * attn.shape[1] * slice_width + 2 * rows * slice_width,
     )
 
 
@@ -658,9 +652,11 @@
     attn, far_top, far_bot = attend(n_y, qs, o, w_slices, s1, ends, received, slice_width)
     relay_top = along_x(far_top, 1)
     relay_bot = along_x(far_bot, -1)
-    p_top, p_bot, m_top, m_bot, own = output(attn, w_slices, slice_width)
+    rows, half = attn.shape[0], attn.shape[0] // 2
+    p_bot, m_top = columns([(1, half, half), (2, 0, half)], attn, w_slices)
     left_bot = along_x(p_bot, 1)
     right_top = along_x(m_top, -1)
+    p_top, m_bot, own = columns([(1, 0, half), (2, half, half), (3, 0, rows)], attn, w_slices)
     left_top = along_x(p_top + relay_top, 1)
     right_bot = along_x(m_bot + relay_bot, -1)
     out = finish(1, own, left_bot, right_bot)

time: 88.4 us -> 87.1 us (0.985)
  waiting for transfers between devices: 21.2 us -> 19.8 us
    ppermute x12, waiting for transfers between devices: 12.2 us -> 10.7 us  [along_x(): lax.ppermute(x, 'tensor', [(i, (i + shift) % n_t) for i in range(n_t)])]
    pallas_call x14 -> x15, Pallas kernels: 32.4 us -> 32.7 us  [call(): pl.pallas_call(kernel, grid=(1,), in_specs=[HBM if i in big else ANY if i...]
  transfers between devices with their start and end apart: 21 -> 21, of which waited for: 11 -> 11; matrix products, arithmetic and copies ran while one was open for 0% -> 0% of each run, Pallas kernels for 22% -> 23%
where the time goes in v6:
time: 87.1 us; the launch traced here: 87 us
  starting transfers between devices  33.9 us (39%)
  Pallas kernels  32.7 us (38%)
  waiting for transfers between devices  19.8 us (23%)
    pallas_call x15, Pallas kernels, call(): pl.pallas_call(kernel, grid=(1,), in_specs=[HBM if i in big else ANY if i...  32.7 us
    ppermute x12, starting transfers between devices, along_x(): lax.ppermute(x, 'tensor', [(i, (i + shift) % n_t) for i in range(n_t)])  19.1 us
    ppermute x12, waiting for transfers between devices, along_x(): lax.ppermute(x, 'tensor', [(i, (i + shift) % n_t) for i in range(n_t)])  10.7 us
    ppermute x6, starting transfers between devices, along_y(): lax.ppermute(x, 'seq', [(z * n_y + y, z * n_y + (y + shift) % n_y) for z...  7.54 us
    ppermute x3, starting transfers between devices, along_z(): lax.ppermute(x, 'seq', [(z * n_y + y, (z + shift) % n_z * n_y + y) for z...  7.2 us
    ppermute x6, waiting for transfers between devices, along_y(): lax.ppermute(x, 'seq', [(z * n_y + y, z * n_y + (y + shift) % n_y) for z...  6.75 us
    ppermute x3, waiting for transfers between devices, along_z(): lax.ppermute(x, 'seq', [(z * n_y + y, (z + shift) % n_z * n_y + y) for z...  2.28 us
  transfers between devices with their start and end apart: 21, of which 11 were waited for; matrix products, arithmetic and copies ran while one was open for 0% of the time, Pallas kernels for 23%

profile of v6, /device:TPU:0, one launch (start us, length us, event | category | flops | bytes accessed | tf_op | source)
XLA Modules:
  0.0 87.0 jit_solution(11772156459691053023)
XLA Ops:
  0.0 6.0 %split.1 = (bf16[512,384]{1,0:T(8,128)(2,1)S(1)}, bf16[512,384]{1,0:T(8,128)(2,1)S(1)}, f32[3,4,512,256]{3,2,1,0:T(8,128)}) custom-call(bf16[512,768]{1,0:T(8,128)(2,1)} %tokens.1, bf16[3,3072,1024]{2,1,0:T(8,128)(2,1)} %bitcast.3), custom_call_target="tpu_custom_call" | custom-call | flops 2415919104 | bytes 4718592 | tf_op jit(solution)/shard_map/split/pallas_call | solution.py:45
  6.0 1.6 %collective-permute-start = (bf16[512,384]{1,0:T(8,128)(2,1)S(1)}, bf16[512,384]{1,0:T(8,128)(2,1)S(1)}, u32[]{:S(2)}, u32[]{:S(2)}) collective-permute-start(bf16[512,384]{1,0:T(8,128)(2,1)S(1)} %get-tuple-element.44.t0), channel_id=1, source_target_pairs={{0,1},{1,2},{2,3},{3,0},{4,5},{5,6},{6,7},{7,4},{8,9},{9,10},{10,1... | collective-permute-start | bytes 1179656 | tf_op jit(solution)/shard_map/ppermute | solution.py:613
  7.6 1.7 %collective-permute-start.2 = (bf16[512,384]{1,0:T(8,128)(2,1)S(1)}, bf16[512,384]{1,0:T(8,128)(2,1)S(1)}, u32[]{:S(2)}, u32[]{:S(2)}) collective-permute-start(bf16[512,384]{1,0:T(8,128)(2,1)S(1)} %get-tuple-element.45.t1), channel_id=1, source_target_pairs={{0,3},{1,0},{2,1},{3,2},{4,7},{5,4},{6,5},{7,6},{8,11},{9,8},{10,9... | collective-permute-start | bytes 1179656 | tf_op jit(solution)/shard_map/ppermute | solution.py:613
  9.7 2.9 %collective-permute-start.5 = (bf16[512,384]{1,0:T(8,128)(2,1)S(1)}, bf16[512,384]{1,0:T(8,128)(2,1)S(1)}, u32[]{:S(2)}, u32[]{:S(2)}) collective-permute-start(bf16[512,384]{1,0:T(8,128)(2,1)S(1)} %get-tuple-element.44.t0), channel_id=1, source_target_pairs={{0,3},{1,0},{2,1},{3,2},{4,7},{5,4},{6,5},{7,6},{8,11},{9,8},{10,9... | collective-permute-start | bytes 1179656 | tf_op jit(solution)/shard_map/ppermute | solution.py:613
  12.7 4.7 %own.1 = (f32[3,4,512,256]{3,2,1,0:T(8,128)S(1)}, bf16[4,1024,768]{2,1,0:T(8,128)(2,1)S(1)}) custom-call(bf16[512,384]{1,0:T(8,128)(2,1)S(1)} %get-tuple-element.44.t0, bf16[512,384]{1,0:T(8,128)(2,1)S(1)} %get-tuple-element.45.t1, bf16[3,3072,1024]{2,1,0:T(8,128)(2,1)} %bitcast.4, f32[3,4,512,256]{3,2,1,0:T(8,128)} %get-tuple-element.46.early, ...), custom_call_target="tpu_custom_call" | custom-call | flops 2415919104 | bytes 11010048 | tf_op jit(solution)/shard_map/own/pallas_call | solution.py:45
  17.3 2.0 %collective-permute-done.a = bf16[512,384]{1,0:T(8,128)(2,1)S(1)} collective-permute-done((bf16[512,384]{1,0:T(8,128)(2,1)S(1)}, bf16[512,384]{1,0:T(8,128)(2,1)S(1)}, u32[]{:S(2)}, u32[]{:S(2)}) %collective-permute-start) | collective-permute-done | bytes 393248 | tf_op jit(solution)/shard_map/ppermute | solution.py:613
  19.7 2.9 %collective-permute-start.3 = (bf16[512,384]{1,0:T(8,128)(2,1)S(1)}, bf16[512,384]{1,0:T(8,128)(2,1)S(1)}, u32[]{:S(2)}, u32[]{:S(2)}) collective-permute-start(bf16[512,384]{1,0:T(8,128)(2,1)S(1)} %collective-permute-done.2.b), channel_id=1, source_target_pairs={{0,3},{1,0},{2,1},{3,2},{4,7},{5,4},{6,5},{7,6},{8,11},{9,8},{10,9... | collective-permute-start | bytes 1179656 | tf_op jit(solution)/shard_map/ppermute | solution.py:613
  22.6 5.0 %near.2 = (f32[3,4,512,256]{3,2,1,0:T(8,128)S(1)}, bf16[3,768,1024]{2,1,0:T(8,128)(2,1)S(1)}) custom-call(bf16[512,384]{1,0:T(8,128)(2,1)S(1)} %collective-permute-done.a, bf16[512,384]{1,0:T(8,128)(2,1)S(1)} %collective-permute-done.2.b, bf16[3,3072,1024]{2,1,0:T(8,128)(2,1)} %bitcast.5, f32[3,4,512,256]{3,2,1,0:T(8,128)S(1)} %get-tuple-element.47.refs_0_), custom_call_target="tpu_custom_call" | custom-call | flops 2415919104 | bytes 11010048 | tf_op jit(solution)/shard_map/near/pallas_call | solution.py:45
  27.6 2.7 %near.3 = (f32[3,4,512,256]{3,2,1,0:T(8,128)S(1)}, bf16[3,768,1024]{2,1,0:T(8,128)(2,1)S(1)}) custom-call(bf16[512,384]{1,0:T(8,128)(2,1)S(1)} %collective-permute-done.4.a, bf16[512,384]{1,0:T(8,128)(2,1)S(1)} %collective-permute-done.5.b, bf16[3,3072,1024]{2,1,0:T(8,128)(2,1)} %bitcast.6, f32[3,4,512,256]{3,2,1,0:T(8,128)S(1)} %get-tuple-element.48.refs_0_, ...), custom_call_target="tpu_custom_call" | custom-call | flops 2415919104 | bytes 11010048 | tf_op jit(solution)/shard_map/near/pallas_call | solution.py:45
  31.2 3.8 %key_value.1 = (bf16[4,512,256]{2,1,0:T(8,128)(2,1)S(1)}, bf16[4,512,256]{2,1,0:T(8,128)(2,1)S(1)}, f32[1024,128]{1,0:T(8,128)S(1)}, bf16[272,128]{1,0:T(8,128)(...) custom-call(bf16[512,384]{1,0:T(8,128)(2,1)S(1)} %collective-permute-done.1.f0, ...), custom_call_target="tpu_custom_call" | custom-call | flops 1610612736 | bytes 7340032 | tf_op jit(solution)/shard_map/key_value/pallas_call | solution.py:45
  34.9 3.2 %collective-permute-start.6 = (bf16[272,128]{1,0:T(8,128)(2,1)S(1)}, bf16[272,128]{1,0:T(8,128)(2,1)S(1)}, u32[]{:S(2)}, u32[]{:S(2)}) collective-permute-start(bf16[272,128]{1,0:T(8,128)(2,1)S(1)} %get-tuple-element.65), channel_id=1, source_target_pairs={{0,12},{4,0},{8,4},{12,8},{16,28},{20,16},{24,20},{28,24},{32,44},... | collective-permute-start | bytes 208904 | tf_op jit(solution)/shard_map/ppermute | solution.py:616
  40.9 1.6 %inner.1 = (bf16[4,512,256]{2,1,0:T(8,128)(2,1)S(1)}, f32[4,512,256]{2,1,0:T(8,128)S(1)}, f32[8,128]{1,0:T(8,128)S(1)}) custom-call(bf16[4,512,256]{2,1,0:T(8,128)(2,1)S(1)} %query.1.q, bf16[4,512,256]{2,1,0:T(8,128)(2,1)S(1)} %get-tuple-element.55.k, bf16[4,512,256]{2,1,0:T(8,128)(2,1)S(1)} %get-tuple-element.56.v, f32[512,8]{1,0:T(8,128)S(1)} %get-tuple-element.57.acol, ...), custom_call_target="tpu_custom_call" | custom-call | flops 536870912 | bytes 7340032 | tf_op jit(solution)/shard_map/inner/pallas_call | solution.py:45
  44.8 4.0 %collective-permute-start.10 = (bf16[272,128]{1,0:T(8,128)(2,1)S(1)}, bf16[272,128]{1,0:T(8,128)(2,1)S(1)}, u32[]{:S(2)}, u32[]{:S(2)}) collective-permute-start(bf16[272,128]{1,0:T(8,128)(2,1)S(1)} %get-tuple-element.69), channel_id=1, source_target_pairs={{0,32},{4,36},{8,40},{12,44},{16,48},{20,52},{24,56},{28,60},{32,0... | collective-permute-start | bytes 208904 | tf_op jit(solution)/shard_map/ppermute | solution.py:621
  49.8 2.2 %collective-permute-start.9 = (bf16[272,128]{1,0:T(8,128)(2,1)S(1)}, bf16[272,128]{1,0:T(8,128)(2,1)S(1)}, u32[]{:S(2)}, u32[]{:S(2)}) collective-permute-start(bf16[272,128]{1,0:T(8,128)(2,1)S(1)} %get-tuple-element.69), channel_id=1, source_target_pairs={{0,48},{4,52},{8,56},{12,60},{16,0},{20,4},{24,8},{28,12},{32,16},... | collective-permute-start | bytes 208904 | tf_op jit(solution)/shard_map/ppermute | solution.py:621
  52.0 2.3 %collective-permute-done.11.refs_6_ = bf16[272,128]{1,0:T(8,128)(2,1)S(1)} collective-permute-done((bf16[272,128]{1,0:T(8,128)(2,1)S(1)}, bf16[272,128]{1,0:T(8,128)(2,1)S(1)}, u32[]{:S(2)}, u32[]{:S(2)}) %collective-permute-start.11) | collective-permute-done | bytes 69664 | tf_op jit(solution)/shard_map/ppermute | solution.py:621
  57.5 1.6 %collective-permute-done.12.refs_1_ = bf16[256,128]{1,0:T(8,128)(2,1)S(1)} collective-permute-done((bf16[256,128]{1,0:T(8,128)(2,1)S(1)}, bf16[256,128]{1,0:T(8,128)(2,1)S(1)}, u32[]{:S(2)}, u32[]{:S(2)}) %collective-permute-start.12) | collective-permute-done | bytes 65568 | tf_op jit(solution)/shard_map/ppermute | solution.py:616
  59.1 2.1 %collective-permute-done.13.refs_2_ = bf16[256,128]{1,0:T(8,128)(2,1)S(1)} collective-permute-done((bf16[256,128]{1,0:T(8,128)(2,1)S(1)}, bf16[256,128]{1,0:T(8,128)(2,1)S(1)}, u32[]{:S(2)}, u32[]{:S(2)}) %collective-permute-start.13) | collective-permute-done | bytes 65568 | tf_op jit(solution)/shard_map/ppermute | solution.py:616
  62.2 1.7 %attend.1 = (bf16[512,1024]{1,0:T(8,128)(2,1)S(1)}, bf16[256,768]{1,0:T(8,128)(2,1)S(1)}, bf16[256,768]{1,0:T(8,128)(2,1)S(1)}) custom-call(bf16[4,512,256]{2,1,0:T(8,128)(2,1)S(1)} %get-tuple-element.60.qs, f32[4,512,256]{2,1,0:T(8,128)S(1)} %get-tuple-element.61.o, bf16[4,1024,768]{2,1,0:T(8,128)(2,1)S(1)} %get-tuple-element.62.w, ...), custom_call_target="tpu_custom_call" | custom-call | flops 939524096 | bytes 5767168 | tf_op jit(solution)/shard_map/attend/pallas_call | solution.py:45
  63.9 2.1 %collective-permute-start.19 = (bf16[256,768]{1,0:T(8,128)(2,1)S(1)}, bf16[256,768]{1,0:T(8,128)(2,1)S(1)}, u32[]{:S(2)}, u32[]{:S(2)}) collective-permute-start(bf16[256,768]{1,0:T(8,128)(2,1)S(1)} %get-tuple-element.82), channel_id=1, source_target_pairs={{0,3},{1,0},{2,1},{3,2},{4,7},{5,4},{6,5},{7,6},{8,11},{9,8},{10,9... | collective-permute-start | bytes 1179656 | tf_op jit(solution)/shard_map/ppermute | solution.py:613
  67.7 2.8 %collective-permute-start.17 = (bf16[256,768]{1,0:T(8,128)(2,1)S(1)}, bf16[256,768]{1,0:T(8,128)(2,1)S(1)}, u32[]{:S(2)}, u32[]{:S(2)}) collective-permute-start(bf16[256,768]{1,0:T(8,128)(2,1)S(1)} %get-tuple-element.79), channel_id=1, source_target_pairs={{0,3},{1,0},{2,1},{3,2},{4,7},{5,4},{6,5},{7,6},{8,11},{9,8},{10,9... | collective-permute-start | bytes 1179656 | tf_op jit(solution)/shard_map/ppermute | solution.py:613
  70.4 1.8 %columns.2 = (bf16[256,768]{1,0:T(8,128)(2,1)S(1)}, bf16[256,768]{1,0:T(8,128)(2,1)S(1)}, bf16[512,768]{1,0:T(8,128)(2,1)S(1)}) custom-call(bf16[512,1024]{1,0:T(8,128)(2,1)S(1)} %get-tuple-element.75.attn, bf16[4,1024,768]{2,1,0:T(8,128)(2,1)S(1)} %get-tuple-element.62.w), custom_call_target="tpu_custom_call" | custom-call | flops 1610612736 | bytes 6291456 | tf_op jit(solution)/shard_map/columns/pallas_call | solution.py:45
  73.0 3.8 %collective-permute-start.20 = (bf16[256,768]{1,0:T(8,128)(2,1)S(1)}, bf16[256,768]{1,0:T(8,128)(2,1)S(1)}, u32[]{:S(2)}, u32[]{:S(2)}) collective-permute-start(bf16[256,768]{1,0:T(8,128)(2,1)S(1)} %add.7), channel_id=1, source_target_pairs={{0,3},{1,0},{2,1},{3,2},{4,7},{5,4},{6,5},{7,6},{8,11},{9,8},{10,9... | collective-permute-start | bytes 1179656 | tf_op jit(solution)/shard_map/ppermute | solution.py:613
  77.0 3.6 %collective-permute-done.18.refs_1_ = bf16[256,768]{1,0:T(8,128)(2,1)S(1)} collective-permute-done((bf16[256,768]{1,0:T(8,128)(2,1)S(1)}, bf16[256,768]{1,0:T(8,128)(2,1)S(1)}, u32[]{:S(2)}, u32[]{:S(2)}) %collective-permute-start.18) | collective-permute-done | bytes 393248 | tf_op jit(solution)/shard_map/ppermute | solution.py:613
  83.0 2.9 %collective-permute-done.16.refs_1_ = bf16[256,768]{1,0:T(8,128)(2,1)S(1)} collective-permute-done((bf16[256,768]{1,0:T(8,128)(2,1)S(1)}, bf16[256,768]{1,0:T(8,128)(2,1)S(1)}, u32[]{:S(2)}, u32[]{:S(2)}) %collective-permute-start.16) | collective-permute-done | bytes 393248 | tf_op jit(solution)/shard_map/ppermute | solution.py:613
  (38 shorter events, 17.9 us)
Async XLA Ops:
  0.0 12.5 %copy-start = (f32[8,512]{1,0:T(8,128)S(1)}, f32[8,512]{1,0:T(8,128)}, u32[]{:S(2)}) copy-start(f32[8,512]{1,0:T(8,128)} %ld.1) | copy-start | bytes 49156
  6.0 13.3 %collective-permute-start = (bf16[512,384]{1,0:T(8,128)(2,1)S(1)}, bf16[512,384]{1,0:T(8,128)(2,1)S(1)}, u32[]{:S(2)}, u32[]{:S(2)}) collective-permute-start(bf16[512,384]{1,0:T(8,128)(2,1)S(1)} %get-tuple-element.44.t0), channel_id=1, source_target_pairs={{0,1},{1,2},{2,3},{3,0},{4,5},{5,6},{6,7},{7,4},{8,9},{9,10},{10,1... | collective-permute-start | bytes 1179656 | tf_op jit(solution)/shard_map/ppermute | solution.py:613
  7.6 12.1 %collective-permute-start.2 = (bf16[512,384]{1,0:T(8,128)(2,1)S(1)}, bf16[512,384]{1,0:T(8,128)(2,1)S(1)}, u32[]{:S(2)}, u32[]{:S(2)}) collective-permute-start(bf16[512,384]{1,0:T(8,128)(2,1)S(1)} %get-tuple-element.45.t1), channel_id=1, source_target_pairs={{0,3},{1,0},{2,1},{3,2},{4,7},{5,4},{6,5},{7,6},{8,11},{9,8},{10,9... | collective-permute-start | bytes 1179656 | tf_op jit(solution)/shard_map/ppermute | solution.py:613
  9.3 18.3 %collective-permute-start.4 = (bf16[512,384]{1,0:T(8,128)(2,1)S(1)}, bf16[512,384]{1,0:T(8,128)(2,1)S(1)}, u32[]{:S(2)}, u32[]{:S(2)}) collective-permute-start(bf16[512,384]{1,0:T(8,128)(2,1)S(1)} %get-tuple-element.45.t1), channel_id=1, source_target_pairs={{0,1},{1,2},{2,3},{3,0},{4,5},{5,6},{6,7},{7,4},{8,9},{9,10},{10,1... | collective-permute-start | bytes 1179656 | tf_op jit(solution)/shard_map/ppermute | solution.py:613
  9.7 17.9 %collective-permute-start.5 = (bf16[512,384]{1,0:T(8,128)(2,1)S(1)}, bf16[512,384]{1,0:T(8,128)(2,1)S(1)}, u32[]{:S(2)}, u32[]{:S(2)}) collective-permute-start(bf16[512,384]{1,0:T(8,128)(2,1)S(1)} %get-tuple-element.44.t0), channel_id=1, source_target_pairs={{0,3},{1,0},{2,1},{3,2},{4,7},{5,4},{6,5},{7,6},{8,11},{9,8},{10,9... | collective-permute-start | bytes 1179656 | tf_op jit(solution)/shard_map/ppermute | solution.py:613
  19.3 11.8 %collective-permute-start.1 = (bf16[512,384]{1,0:T(8,128)(2,1)S(1)}, bf16[512,384]{1,0:T(8,128)(2,1)S(1)}, u32[]{:S(2)}, u32[]{:S(2)}) collective-permute-start(bf16[512,384]{1,0:T(8,128)(2,1)S(1)} %collective-permute-done.a), channel_id=1, source_target_pairs={{0,1},{1,2},{2,3},{3,0},{4,5},{5,6},{6,7},{7,4},{8,9},{9,10},{10,1... | collective-permute-start | bytes 1179656 | tf_op jit(solution)/shard_map/ppermute | solution.py:613
  19.7 11.5 %collective-permute-start.3 = (bf16[512,384]{1,0:T(8,128)(2,1)S(1)}, bf16[512,384]{1,0:T(8,128)(2,1)S(1)}, u32[]{:S(2)}, u32[]{:S(2)}) collective-permute-start(bf16[512,384]{1,0:T(8,128)(2,1)S(1)} %collective-permute-done.2.b), channel_id=1, source_target_pairs={{0,3},{1,0},{2,1},{3,2},{4,7},{5,4},{6,5},{7,6},{8,11},{9,8},{10,9... | collective-permute-start | bytes 1179656 | tf_op jit(solution)/shard_map/ppermute | solution.py:613
  34.9 7.6 %collective-permute-start.6 = (bf16[272,128]{1,0:T(8,128)(2,1)S(1)}, bf16[272,128]{1,0:T(8,128)(2,1)S(1)}, u32[]{:S(2)}, u32[]{:S(2)}) collective-permute-start(bf16[272,128]{1,0:T(8,128)(2,1)S(1)} %get-tuple-element.65), channel_id=1, source_target_pairs={{0,12},{4,0},{8,4},{12,8},{16,28},{20,16},{24,20},{28,24},{32,44},... | collective-permute-start | bytes 208904 | tf_op jit(solution)/shard_map/ppermute | solution.py:616
  38.1 5.9 %collective-permute-start.7 = (bf16[272,128]{1,0:T(8,128)(2,1)S(1)}, bf16[272,128]{1,0:T(8,128)(2,1)S(1)}, u32[]{:S(2)}, u32[]{:S(2)}) collective-permute-start(bf16[272,128]{1,0:T(8,128)(2,1)S(1)} %get-tuple-element.66), channel_id=1, source_target_pairs={{0,8},{4,12},{8,0},{12,4},{16,24},{20,28},{24,16},{28,20},{32,40},... | collective-permute-start | bytes 208904 | tf_op jit(solution)/shard_map/ppermute | solution.py:616
  38.7 5.9 %collective-permute-start.8 = (bf16[272,128]{1,0:T(8,128)(2,1)S(1)}, bf16[272,128]{1,0:T(8,128)(2,1)S(1)}, u32[]{:S(2)}, u32[]{:S(2)}) collective-permute-start(bf16[272,128]{1,0:T(8,128)(2,1)S(1)} %get-tuple-element.67), channel_id=1, source_target_pairs={{0,4},{4,8},{8,12},{12,0},{16,20},{20,24},{24,28},{28,16},{32,36},... | collective-permute-start | bytes 208904 | tf_op jit(solution)/shard_map/ppermute | solution.py:616
  44.8 7.2 %collective-permute-start.10 = (bf16[272,128]{1,0:T(8,128)(2,1)S(1)}, bf16[272,128]{1,0:T(8,128)(2,1)S(1)}, u32[]{:S(2)}, u32[]{:S(2)}) collective-permute-start(bf16[272,128]{1,0:T(8,128)(2,1)S(1)} %get-tuple-element.69), channel_id=1, source_target_pairs={{0,32},{4,36},{8,40},{12,44},{16,48},{20,52},{24,56},{28,60},{32,0... | collective-permute-start | bytes 208904 | tf_op jit(solution)/shard_map/ppermute | solution.py:621
  48.8 5.5 %collective-permute-start.11 = (bf16[272,128]{1,0:T(8,128)(2,1)S(1)}, bf16[272,128]{1,0:T(8,128)(2,1)S(1)}, u32[]{:S(2)}, u32[]{:S(2)}) collective-permute-start(bf16[272,128]{1,0:T(8,128)(2,1)S(1)} %get-tuple-element.69), channel_id=1, source_target_pairs={{0,16},{4,20},{8,24},{12,28},{16,32},{20,36},{24,40},{28,44},{32,4... | collective-permute-start | bytes 208904 | tf_op jit(solution)/shard_map/ppermute | solution.py:621
  49.8 4.5 %collective-permute-start.9 = (bf16[272,128]{1,0:T(8,128)(2,1)S(1)}, bf16[272,128]{1,0:T(8,128)(2,1)S(1)}, u32[]{:S(2)}, u32[]{:S(2)}) collective-permute-start(bf16[272,128]{1,0:T(8,128)(2,1)S(1)} %get-tuple-element.69), channel_id=1, source_target_pairs={{0,48},{4,52},{8,56},{12,60},{16,0},{20,4},{24,8},{28,12},{32,16},... | collective-permute-start | bytes 208904 | tf_op jit(solution)/shard_map/ppermute | solution.py:621
  54.8 4.3 %collective-permute-start.12 = (bf16[256,128]{1,0:T(8,128)(2,1)S(1)}, bf16[256,128]{1,0:T(8,128)(2,1)S(1)}, u32[]{:S(2)}, u32[]{:S(2)}) collective-permute-start(bf16[256,128]{1,0:T(8,128)(2,1)S(1)} %get-tuple-element.72), channel_id=1, source_target_pairs={{0,12},{4,0},{8,4},{12,8},{16,28},{20,16},{24,20},{28,24},{32,44},... | collective-permute-start | bytes 196616 | tf_op jit(solution)/shard_map/ppermute | solution.py:616
  55.4 5.8 %collective-permute-start.13 = (bf16[256,128]{1,0:T(8,128)(2,1)S(1)}, bf16[256,128]{1,0:T(8,128)(2,1)S(1)}, u32[]{:S(2)}, u32[]{:S(2)}) collective-permute-start(bf16[256,128]{1,0:T(8,128)(2,1)S(1)} %get-tuple-element.73), channel_id=1, source_target_pairs={{0,8},{4,12},{8,0},{12,4},{16,24},{20,28},{24,16},{28,20},{32,40},... | collective-permute-start | bytes 196616 | tf_op jit(solution)/shard_map/ppermute | solution.py:616
  56.7 5.5 %collective-permute-start.14 = (bf16[256,128]{1,0:T(8,128)(2,1)S(1)}, bf16[256,128]{1,0:T(8,128)(2,1)S(1)}, u32[]{:S(2)}, u32[]{:S(2)}) collective-permute-start(bf16[256,128]{1,0:T(8,128)(2,1)S(1)} %get-tuple-element.74), channel_id=1, source_target_pairs={{0,4},{4,8},{8,12},{12,0},{16,20},{20,24},{24,28},{28,16},{32,36},... | collective-permute-start | bytes 196616 | tf_op jit(solution)/shard_map/ppermute | solution.py:616
  63.9 9.0 %collective-permute-start.19 = (bf16[256,768]{1,0:T(8,128)(2,1)S(1)}, bf16[256,768]{1,0:T(8,128)(2,1)S(1)}, u32[]{:S(2)}, u32[]{:S(2)}) collective-permute-start(bf16[256,768]{1,0:T(8,128)(2,1)S(1)} %get-tuple-element.82), channel_id=1, source_target_pairs={{0,3},{1,0},{2,1},{3,2},{4,7},{5,4},{6,5},{7,6},{8,11},{9,8},{10,9... | collective-permute-start | bytes 1179656 | tf_op jit(solution)/shard_map/ppermute | solution.py:613
  66.0 10.8 %collective-permute-start.15 = (bf16[256,768]{1,0:T(8,128)(2,1)S(1)}, bf16[256,768]{1,0:T(8,128)(2,1)S(1)}, u32[]{:S(2)}, u32[]{:S(2)}) collective-permute-start(bf16[256,768]{1,0:T(8,128)(2,1)S(1)} %get-tuple-element.78), channel_id=1, source_target_pairs={{0,1},{1,2},{2,3},{3,0},{4,5},{5,6},{6,7},{7,4},{8,9},{9,10},{10,1... | collective-permute-start | bytes 1179656 | tf_op jit(solution)/shard_map/ppermute | solution.py:613
  67.0 13.6 %collective-permute-start.18 = (bf16[256,768]{1,0:T(8,128)(2,1)S(1)}, bf16[256,768]{1,0:T(8,128)(2,1)S(1)}, u32[]{:S(2)}, u32[]{:S(2)}) collective-permute-start(bf16[256,768]{1,0:T(8,128)(2,1)S(1)} %get-tuple-element.80), channel_id=1, source_target_pairs={{0,1},{1,2},{2,3},{3,0},{4,5},{5,6},{6,7},{7,4},{8,9},{9,10},{10,1... | collective-permute-start | bytes 1179656 | tf_op jit(solution)/shard_map/ppermute | solution.py:613
  67.7 15.4 %collective-permute-start.17 = (bf16[256,768]{1,0:T(8,128)(2,1)S(1)}, bf16[256,768]{1,0:T(8,128)(2,1)S(1)}, u32[]{:S(2)}, u32[]{:S(2)}) collective-permute-start(bf16[256,768]{1,0:T(8,128)(2,1)S(1)} %get-tuple-element.79), channel_id=1, source_target_pairs={{0,3},{1,0},{2,1},{3,2},{4,7},{5,4},{6,5},{7,6},{8,11},{9,8},{10,9... | collective-permute-start | bytes 1179656 | tf_op jit(solution)/shard_map/ppermute | solution.py:613
  73.0 9.1 %collective-permute-start.20 = (bf16[256,768]{1,0:T(8,128)(2,1)S(1)}, bf16[256,768]{1,0:T(8,128)(2,1)S(1)}, u32[]{:S(2)}, u32[]{:S(2)}) collective-permute-start(bf16[256,768]{1,0:T(8,128)(2,1)S(1)} %add.7), channel_id=1, source_target_pairs={{0,3},{1,0},{2,1},{3,2},{4,7},{5,4},{6,5},{7,6},{8,11},{9,8},{10,9... | collective-permute-start | bytes 1179656 | tf_op jit(solution)/shard_map/ppermute | solution.py:613
  76.9 9.1 %collective-permute-start.16 = (bf16[256,768]{1,0:T(8,128)(2,1)S(1)}, bf16[256,768]{1,0:T(8,128)(2,1)S(1)}, u32[]{:S(2)}, u32[]{:S(2)}) collective-permute-start(bf16[256,768]{1,0:T(8,128)(2,1)S(1)} %add.6), channel_id=1, source_target_pairs={{0,1},{1,2},{2,3},{3,0},{4,5},{5,6},{6,7},{7,4},{8,9},{9,10},{10,1... | collective-permute-start | bytes 1179656 | tf_op jit(solution)/shard_map/ppermute | solution.py:613
